TPU v7x, 256 devices: a whole 4x4x8 slice. The times are simulated.
256 devices in a mesh: dp: 32 (over z, x), tensor: 8 (over y, core).
Axes of the slice: x: 4, y: 4, z: 8, core: 2. Of those that a mesh axis runs over, the one named last changes fastest.
Arguments:
- query: bfloat16 [256, 5120], P('dp', 'tensor'), may hold values from -256 to 256
- cache: bfloat16 [256, 2, 1024, 1024], P('dp', None, None, 'tensor'), may hold values from -6.5 to 6.5
- new_kv: bfloat16 [256, 2, 1024], P('dp', None, 'tensor'), may hold values from -12 to 12
- lengths: int32 [256], replicated, may hold values from 128 to 1024, as said below
- hidden_in: bfloat16 [256, 5120], P(None, 'dp'), may hold values from -24 to 24
- out_proj: bfloat16 [5120, 5120], P('tensor', 'dp'), may hold values from -0.078125 to 0.078125
- final_gain: float32 [5120], P('dp'), may hold values from 0.1 to 1.9
- lm_head: bfloat16 [152064, 5120], P(('dp', 'tensor')), may hold values from -32 to 32
- tokens: int32 [256], replicated, may hold values from 0 to 152063
- mu: float32 [256], replicated, may hold values from 6 to 10
Outputs:
- logprobs: float32 [256, 152064], P(None, ('dp', 'tensor'))
- surprise: float32 [256], replicated
- mu_next: float32 [256], replicated
Inputs may be any that keep to these rules, and one draw needn't show every extreme that they name: Request r's cache holds live keys and values at positions 0 to lengths[r] - 1; the new token comes after them.
All inputs are finite; a program needn't handle non-finite values.
Results may differ from a plain program's by a relative error of at most 0.01.
Values may be sent and summed in bfloat16 or wider, within the bound.
No kernel may reach another device: no remote copies, remote signals or barrier semaphores. Data moves between devices by JAX's collectives and lax.ppermute only.
A program may use at most 64 MiB of HBM per device.

v0:
```python
import math

import jax
import jax.numpy as jnp
from jax import lax
from jax.sharding import PartitionSpec as P

D = 5120
HEADS = 40
KV_HEADS = 8
HEAD_DIM = 128


masked_score = -1e30
epsilon = 1e-06
learn_rate = 0.1
target_bits = 5.0


def attend(state, per_head_rows, slab, positions, live_lengths):
    running_top, running_mass, running_sum = state
    request_count = slab.shape[0]
    key_block = slab.shape[2]
    kv_local = slab.shape[3] // HEAD_DIM
    cached_key_rows = slab[:, 0].reshape(request_count, key_block, kv_local, HEAD_DIM)
    cached_value_rows = slab[:, 1].reshape(request_count, key_block, kv_local, HEAD_DIM)
    attention_scores = jnp.einsum(
        "rkgd,rbkd->rkgb", per_head_rows, cached_key_rows, preferred_element_type=jnp.float32
    ) * HEAD_DIM ** (-0.5)
    live = positions[None, :] < live_lengths[:, None]
    attention_scores = jnp.where(live[:, None, None, :], attention_scores, masked_score)
    new_top = jnp.maximum(running_top, jnp.max(attention_scores, axis=-1))
    rescale = jnp.exp(running_top - new_top)
    attention_weights = jnp.exp(attention_scores - new_top[..., None])
    new_mass = running_mass * rescale + jnp.sum(attention_weights, axis=-1)
    new_sum = running_sum * rescale[..., None] + jnp.einsum(
        "rkgb,rbkd->rkgd",
        attention_weights,
        cached_value_rows.astype(jnp.float32),
        precision=lax.Precision.HIGHEST,
    )
    return (new_top, new_mass, new_sum)


def sweep(state, source, per_head_rows, live_lengths, offset, count, key_block):

    def advance(index, current):
        slab = lax.dynamic_slice_in_dim(source, index * key_block, key_block, 2)
        positions = offset + index * key_block + jnp.arange(key_block, dtype=jnp.int32)
        return attend(current, per_head_rows, slab, positions, live_lengths)

    return lax.fori_loop(0, count, advance, state)


def normalize(resid, final_gain):
    resid_wide = resid.astype(jnp.float32)
    sum_squares = lax.psum(jnp.sum(resid_wide * resid_wide, axis=1), "dp")
    factor = lax.rsqrt(sum_squares / D + epsilon)
    return (resid_wide * factor[:, None] * final_gain[None, :]).astype(jnp.bfloat16)


def contract_rows(left_rows, table):
    return lax.dot_general(
        left_rows, table, (((1,), (1,)), ((), ())), preferred_element_type=jnp.float32
    )


def shards(query, cache, new_kv, lengths, hidden_in, out_proj, final_gain, lm_head, tokens, mu):
    request_count = query.shape[0]
    kv_local = cache.shape[3] // HEAD_DIM
    group_size = HEADS // KV_HEADS
    slot_count = cache.shape[2]
    key_block = slot_count // 4
    dp_rank = lax.axis_index("dp")
    own_lengths = lax.dynamic_slice_in_dim(lengths, dp_rank * request_count, request_count)
    per_head_rows = query.reshape(request_count, kv_local, group_size, HEAD_DIM)
    new_keys = new_kv[:, 0].reshape(request_count, kv_local, HEAD_DIM)
    new_values = new_kv[:, 1].reshape(request_count, kv_local, HEAD_DIM).astype(jnp.float32)
    own_score = jnp.einsum(
        "rkgd,rkd->rkg", per_head_rows, new_keys, preferred_element_type=jnp.float32
    ) * HEAD_DIM ** (-0.5)
    start_state = (
        own_score,
        jnp.ones_like(own_score),
        jnp.broadcast_to(
            new_values[:, :, None, :], (request_count, kv_local, group_size, HEAD_DIM)
        ),
    )
    block_count = (jnp.max(own_lengths) + key_block - 1) // key_block
    state = sweep(start_state, cache, per_head_rows, own_lengths, 0, block_count, key_block)
    attended = (state[2] / state[1][..., None]).reshape(request_count, -1).astype(jnp.bfloat16)
    all_heads = lax.all_gather(attended, "dp", axis=0, tiled=True)
    vocab_rows = lm_head.shape[0]
    weighted_value_sum = lax.psum(
        jnp.dot(all_heads, out_proj, preferred_element_type=jnp.float32), "tensor"
    )
    resid = (hidden_in.astype(jnp.float32) + weighted_value_sum).astype(jnp.bfloat16)
    normed = normalize(resid, final_gain)
    logits = contract_rows(lax.all_gather(normed, "dp", axis=1, tiled=True), lm_head)
    offset = (
        lax.axis_index("dp") * lax.axis_size("tensor") + lax.axis_index("tensor")
    ) * vocab_rows
    local_ids = tokens - offset
    hits = jnp.arange(vocab_rows, dtype=jnp.int32)[None, :] == local_ids[:, None]
    picked = jnp.sum(jnp.where(hits, logits, 0.0), axis=1)
    local_top = jnp.max(logits, axis=1)
    top_logit = lax.pmax(local_top, ("dp", "tensor"))
    local_mass = jnp.sum(jnp.exp(logits - top_logit[:, None]), axis=1)
    total_mass, chosen = lax.psum((local_mass, picked), ("dp", "tensor"))
    log_mass = top_logit + jnp.log(total_mass)
    logprobs = logits - log_mass[:, None]
    surprise = (log_mass - chosen) / math.log(2.0)
    mu_next = mu - learn_rate * (surprise - target_bits)
    return (logprobs, surprise, mu_next)


def solution(mesh):
    placed = (
        P("dp", "tensor"),
        P("dp", None, None, "tensor"),
        P("dp", None, "tensor"),
        P(),
        P(None, "dp"),
        P("tensor", "dp"),
        P("dp"),
        P(("dp", "tensor"), None),
        P(),
        P(),
    )
    return jax.shard_map(
        shards,
        mesh=mesh,
        in_specs=placed,
        out_specs=(P(None, ("dp", "tensor")), P(), P()),
        check_vma=False,
    )
```

profile of v0, /device:TPU:1, one launch (start us, length us, event | category | flops | bytes accessed | tf_op | source)
XLA Modules:
  0.0 450.3 jit_solution(13380550378907427488)
XLA Ops:
  7.2 0.0 copy-start
  7.2 0.0 all-reduce.3.cloned.1.call-start
  7.2 1.4 fusion.17
  9.3 0.8 slice_convert_fusion
  10.1 0.8 fusion.13
  10.9 0.7 copy.16
  11.7 0.0 copy-start.1
  11.7 0.0 copy-start.2
  11.7 0.0 copy-start.4
  11.7 9.4 %while.14 = (s32[]{:T(128)}, f32[8,1,5]{2,0,1:T(8,128)S(1)}, f32[8,1,5]{2,0,1:T(8,128)S(1)}, f32[8,1,5,128]{3,2,0,1:T(8,128)S(1)}, s32[]{:T(128)}, /*index=5*/s3...) while((s32[]{:T(128)}, f32[8,1,5]{2,0,1:T(8,128)S(1)}, ...), condition=%wide.region_4.5_spmd, body=%wide.region_1.4_spmd.sunk | while | flops 18424192 | bytes 1231591 | solution.py:52
  11.7 0.1 broadcast_compare_fusion.2
  11.8 1.4 fusion.29
  13.2 0.2 fusion.31
  13.3 1.4 fusion.32
  14.8 0.1 broadcast_compare_fusion.2
  14.9 1.4 fusion.29
  16.3 0.2 fusion.31
  16.5 1.4 fusion.32
  18.0 0.1 broadcast_compare_fusion.2
  18.0 1.4 fusion.29
  19.4 0.2 fusion.31
  19.6 1.4 fusion.32
  21.0 0.1 copy.17
  21.1 0.1 fusion.15
  21.2 42.9 %all_gather.6 = bf16[256,640]{1,0:T(8,128)(2,1)S(1)} all-gather(bf16[8,640]{1,0:T(8,128)(2,1)S(1)} %fusion.15), channel_id=1, replica_groups=mesh['dp'=32,'tensor'=8] {'dp'}, dimensions={0}, use_global_device_ids=true | all-gather | bytes 337920 | tf_op jit(solution)/shard_map/all_gather | solution.py:92
  64.1 0.0 copy-done
  64.1 0.9 fusion.20
  65.0 0.0 all-reduce.3.cloned.1.call-update
  65.0 0.0 all-gather.2.cloned.1.call-start
  65.1 73.8 %all-reduce.3.cloned.1.call-done = f32[256,160]{0,1:T(8,128)} async-done(((f32[256,160]{0,1:T(8,128)}), f32[256,160]{0,1:T(8,128)}) %all-reduce.3.cloned.1.call-update) | async-done | bytes 163856 | tf_op jit(solution)/shard_map/psum | solution.py:94
  138.9 0.0 copy-done.1
  138.9 1.0 fusion.9
  139.8 61.2 %psum.29 = f32[256]{0:T(256)S(1)} all-reduce(f32[256]{0:T(256)S(1)} %fusion.9), channel_id=1, replica_groups=mesh['dp'=32,'tensor'=8] {'dp'}, use_global_device_ids=true, to_apply=%region_7.8 | all-reduce | flops 256 | bytes 2048 | tf_op jit(solution)/shard_map/psum | solution.py:57
  201.0 0.0 copy-done.2
  201.0 1.6 fusion.11
  202.6 0.0 all-gather.2.cloned.1.call-update
  202.7 0.0 copy-done.4
  202.7 0.0 copy-start.3
  202.7 83.3 %all-gather.2.cloned.1.call-done = bf16[256,5120]{0,1:T(8,128)(2,1)} async-done(((bf16[256,160]{0,1:T(8,128)(2,1)}), bf16[256,5120]{0,1:T(8,128)(2,1)}) %all-gather.2.cloned.1.call-update) | async-done | bytes 2621456 | tf_op jit(solution)/shard_map/all_gather | solution.py:99
  286.1 5.3 %fusion.19 = (f32[256]{0:T(256)S(1)}, f32[256,594]{0,1:T(8,128)S(1)}) fusion(bf16[256,5120]{0,1:T(8,128)(2,1)} %all-gather.2.cloned.1.call-done, bf16[594,5120]{1,0:T(8,128)(2,1)} %param.19), kind=kOutput, calls=%fused_computation.45 | convolution fusion | flops 1557287168 | bytes 9313280 | tf_op jit(solution)/shard_map/dot_general | solution.py:63
  291.4 77.7 %pmax.7 = f32[256]{0:T(256)S(1)} all-reduce(f32[256]{0:T(256)S(1)} %get-tuple-element.96), channel_id=1, replica_groups=mesh['dp'=32,'tensor'=8] {'dp','tensor'}, use_global_device_ids=true, to_apply=%region_9.10 | all-reduce | flops 256 | bytes 2048 | tf_op jit(solution)/shard_map/pmax | solution.py:107
  369.1 0.2 select_reduce_fusion
  369.2 72.8 %all-reduce = (f32[256]{0:T(256)S(1)}, f32[256]{0:T(256)S(1)}) all-reduce(f32[256]{0:T(256)S(1)} %get-tuple-element.66, f32[256]{0:T(256)S(1)} %get-tuple-element.65), channel_id=1, replica_groups=mesh['dp'=32,'tensor'=8] {'dp','tensor'}, use_global_device_ids=true, to_apply=%region_11.12 | all-reduce | flops 512 | bytes 4096 | tf_op jit(solution)/shard_map/psum | solution.py:109
  442.1 0.0 copy-done.3
  442.1 0.6 multiply_subtract_fusion
  442.6 0.9 broadcast_subtract_fusion
  (18 shorter events, 0.1 us)
Async XLA Ops:
  7.2 56.9 %copy-start = (bf16[640,160]{0,1:T(8,128)(2,1)S(1)}, bf16[640,160]{0,1:T(8,128)(2,1)}, u32[]{:S(2)}) copy-start(bf16[640,160]{0,1:T(8,128)(2,1)} %param.17) | copy-start | bytes 614404
  7.2 131.7 %all-reduce.3.cloned.1.call-start = ((), (), s32[]{:S(2)}) async-start(), calls=%async_computation | async-start | bytes 327680 | tf_op jit(solution)/shard_map/psum | solution.py:94
  11.7 127.2 %copy-start.1 = (bf16[256,160]{0,1:T(8,128)(2,1)S(1)}, bf16[256,160]{0,1:T(8,128)(2,1)}, u32[]{:S(2)}) copy-start(bf16[256,160]{0,1:T(8,128)(2,1)} %param.16) | copy-start | bytes 245764
  11.7 189.3 %copy-start.2 = (f32[160]{0:T(256)S(1)}, f32[160]{0:T(256)}, u32[]{:S(2)}) copy-start(f32[160]{0:T(256)} %param.18) | copy-start | bytes 1924
  11.7 191.0 %copy-start.4 = (s32[256]{0:T(256)S(1)}, s32[256]{0:T(256)}, u32[]{:S(2)}) copy-start(s32[256]{0:T(256)} %param.20) | copy-start | bytes 3076
  65.0 221.0 %all-gather.2.cloned.1.call-start = ((), (), s32[]{:S(2)}) async-start(), calls=%async_computation.1 | async-start | bytes 2703360 | tf_op jit(solution)/shard_map/all_gather | solution.py:99
  202.7 239.4 %copy-start.3 = (f32[256]{0:T(256)S(1)}, f32[256]{0:T(256)}, u32[]{:S(2)}) copy-start(f32[256]{0:T(256)} %param.21) | copy-start | bytes 3076
Sparse Core Ops, SparseCore 0:
  65.2 73.6 all-reduce.2
  202.8 83.2 all-gather.1
where the time goes:
time: 451 us; the launch traced here: 450 us
  blocking collectives  255 us (57%)
  waiting for transfers between devices  157 us (35%)
  matrix products  15.4 us (3%)
  between operations  14.8 us (3%)
  other arithmetic  7.36 us (2%)
    all_gather x1, waiting for transfers between devices, shards(): lax.all_gather(normed, 'dp', axis=1, tiled=True)  83.3 us
    pmax x1, blocking collectives, shards(): top_logit = lax.pmax(local_top, ('dp', 'tensor'))  77.7 us
    psum x1, waiting for transfers between devices, shards(): lax.psum(jnp.dot(all_heads, out_proj, preferred_element_type=jnp.float32)...  73.8 us
    psum x1, blocking collectives, shards(): total_mass, chosen = lax.psum((local_mass, picked), ('dp', 'tensor'))  72.8 us
    psum x1, blocking collectives, normalize(): sum_squares = lax.psum(jnp.sum(resid_wide * resid_wide, axis=1), 'dp')  61.2 us
    all_gather x1, blocking collectives, shards(): all_heads = lax.all_gather(attended, 'dp', axis=0, tiled=True)  42.9 us
  transfers between devices with their start and end apart: 2, of which 2 were waited for; matrix products, arithmetic and copies ran while one was open for 0% of the time, Pallas kernels for 0%

commit v1 on v0

v1 whole, which is shorter than its diff:
```python
import math

import jax
import jax.numpy as jnp
import numpy as np
from jax import lax
from jax.sharding import Mesh
from jax.sharding import PartitionSpec as P

D = 5120
HEADS = 40
KV_HEADS = 8
HEAD_DIM = 128

masked_score = -1e30
epsilon = 1e-06
learn_rate = 0.1
target_bits = 5.0

bf16 = jnp.bfloat16
f32 = jnp.float32


def attend_all(query, cache, new_kv, own_lengths):
    request_count = query.shape[0]
    kv_local = cache.shape[3] // HEAD_DIM
    group_size = HEADS // KV_HEADS
    slots = cache.shape[2]
    per_head_rows = query.reshape(request_count, kv_local, group_size, HEAD_DIM)
    new_keys = new_kv[:, 0].reshape(request_count, kv_local, HEAD_DIM)
    new_values = new_kv[:, 1].reshape(request_count, kv_local, HEAD_DIM).astype(f32)
    scale = HEAD_DIM ** (-0.5)
    own_score = jnp.einsum("rkgd,rkd->rkg", per_head_rows, new_keys, preferred_element_type=f32) * scale
    keys = cache[:, 0].reshape(request_count, slots, kv_local, HEAD_DIM)
    values = cache[:, 1].reshape(request_count, slots, kv_local, HEAD_DIM)
    scores = jnp.einsum("rkgd,rbkd->rkgb", per_head_rows, keys, preferred_element_type=f32) * scale
    live = jnp.arange(slots, dtype=jnp.int32)[None, :] < own_lengths[:, None]
    scores = jnp.where(live[:, None, None, :], scores, masked_score)
    top = jnp.maximum(jnp.max(scores, axis=-1), own_score)
    weights = jnp.exp(scores - top[..., None])
    own_weight = jnp.exp(own_score - top)
    mass = jnp.sum(weights, axis=-1) + own_weight
    total = jnp.einsum(
        "rkgb,rbkd->rkgd", weights, values.astype(f32), precision=lax.Precision.HIGHEST
    )
    total = total + own_weight[..., None] * new_values[:, :, None, :]
    return (total / mass[..., None]).reshape(request_count, -1).astype(bf16)


def spread(block, axes, count):
    many = jnp.broadcast_to(block[None], (count,) + block.shape)
    return lax.all_to_all(many, axes, split_axis=0, concat_axis=0, tiled=False)


def three_parts(wide):
    first = wide.astype(bf16)
    rest = wide - first.astype(f32)
    second = rest.astype(bf16)
    third = (rest - second.astype(f32)).astype(bf16)
    return first, second, third


def shards(query, cache, new_kv, lengths, hidden_in, out_proj, final_gain, lm_head, tokens, mu):
    nz, nx, ny, nc = (lax.axis_size(a) for a in ("z", "x", "y", "c"))
    z, x, y, c = (lax.axis_index(a) for a in ("z", "x", "y", "c"))
    request_count = query.shape[0]
    columns = out_proj.shape[1]
    part = c * ny + y

    gain_rows = jnp.stack(three_parts(final_gain))
    packs = []
    for step in range(nx):
        target = lax.rem(x + step, nx)
        rows = lax.dynamic_slice_in_dim(hidden_in, (part * nx + target) * request_count, request_count)
        pack = jnp.concatenate([out_proj, rows, gain_rows], axis=0)
        if step:
            pack = lax.ppermute(pack, "x", [(i, (i + step) % nx) for i in range(nx)])
        packs.append(pack)
    heads = out_proj.shape[0]
    table = jnp.concatenate([p[:heads] for p in packs], axis=1)
    hidden = jnp.concatenate([p[heads : heads + request_count] for p in packs], axis=1)
    gains = jnp.concatenate([p[heads + request_count :] for p in packs], axis=1)

    own_lengths = lax.dynamic_slice_in_dim(lengths, (z * nx + x) * request_count, request_count)
    attended = attend_all(query, cache, new_kv, own_lengths)
    gathered = spread(attended, "z", nz).reshape(nz * request_count, -1)
    partial = jnp.dot(gathered, table, preferred_element_type=f32)
    partial = partial.reshape(nz, request_count, nx * columns)
    partial = lax.all_to_all(partial, ("c", "y"), split_axis=0, concat_axis=0, tiled=False)
    resid = (hidden.astype(f32) + jnp.sum(partial, axis=0)).astype(bf16)

    both = jnp.concatenate([resid, gains], axis=0)
    blocks = [both[:, i * columns : (i + 1) * columns] for i in range(nx)]
    twice = jnp.concatenate(blocks[::-1] + blocks[::-1], axis=1)
    ordered = lax.dynamic_slice_in_dim(twice, (nx - 1 - x) * columns, nx * columns, axis=1)

    rows = spread(ordered, "z", nz)
    gain = jnp.sum(rows[:, request_count:].astype(f32), axis=1)
    resid_wide = rows[:, :request_count].astype(f32)
    sum_squares = jnp.sum(resid_wide * resid_wide, axis=(0, 2))
    factor = lax.rsqrt(sum_squares / D + epsilon)
    normed = (resid_wide * factor[None, :, None] * gain[:, None, :]).astype(bf16)
    normed = jnp.swapaxes(normed, 0, 1).reshape(request_count, -1)

    half = spread(normed, ("y", "x"), ny * nx).reshape(ny * nx * request_count, -1)
    other = lax.ppermute(half, "c", [(i, 1 - i) for i in range(2)])
    first = jnp.where(c == 0, half, other)
    second = jnp.where(c == 0, other, half)
    everyone = jnp.concatenate([first, second], axis=0)
    logits = lax.dot_general(lm_head, everyone, (((1,), (1,)), ((), ())), preferred_element_type=f32)

    vocab_rows = lm_head.shape[0]
    offset = (((z * nx + x) * ny + y) * nc + c) * vocab_rows
    hits = jnp.arange(vocab_rows, dtype=jnp.int32)[:, None] == (tokens - offset)[None, :]
    picked = jnp.sum(jnp.where(hits, logits, 0.0), axis=0)
    top = jnp.max(logits, axis=0)
    log_mass = top + jnp.log(jnp.sum(jnp.exp(logits - top[None, :]), axis=0))
    for axes, count in ((("x", "y", "c"), nx * ny * nc), ("z", nz)):
        stats = spread(jnp.stack([log_mass, picked]), axes, count)
        top = jnp.max(stats[:, 0], axis=0)
        log_mass = top + jnp.log(jnp.sum(jnp.exp(stats[:, 0] - top[None, :]), axis=0))
        picked = jnp.sum(stats[:, 1], axis=0)
    logprobs = (logits - log_mass[None, :]).T
    surprise = (log_mass - picked) / math.log(2.0)
    mu_next = mu - learn_rate * (surprise - target_bits)
    return (logprobs, surprise, mu_next)


def solution(mesh):
    grid = Mesh(np.asarray(mesh.devices).reshape(8, 4, 4, 2), ("z", "x", "y", "c"))
    dp, tensor = ("z", "x"), ("y", "c")
    placed = (
        P(dp, tensor),
        P(dp, None, None, tensor),
        P(dp, None, tensor),
        P(),
        P(None, dp),
        P(tensor, dp),
        P(dp),
        P(dp + tensor, None),
        P(),
        P(),
    )
    return jax.shard_map(
        shards,
        mesh=grid,
        in_specs=placed,
        out_specs=(P(None, dp + tensor), P(), P()),
        check_vma=False,
    )
```

time: 451 us -> 112 us (0.25)
  blocking collectives: 255 us -> 52.2 us
  waiting for transfers between devices: 157 us -> 15.3 us
  starting transfers between devices: 0.08 us -> 24 us
  between operations: 14.8 us -> 0.96 us
    psum x2 -> x0, blocking collectives: 134 us -> none  [the longest x1 72.8 us: shards(): total_mass, chosen = lax.psum((local_mass, picked), ('dp', 'tensor'))]
    all_gather x1 -> x0, waiting for transfers between devices: 83.3 us -> none  [shards(): lax.all_gather(normed, 'dp', axis=1, tiled=True)]
    pmax x1 -> x0, blocking collectives: 77.7 us -> none  [shards(): top_logit = lax.pmax(local_top, ('dp', 'tensor'))]
    psum x1 -> x0, waiting for transfers between devices: 73.8 us -> none  [shards(): lax.psum(jnp.dot(all_heads, out_proj, preferred_element_type=jnp.float32)...]
    all_to_all x0 -> x4, blocking collectives: none -> 52.2 us  [spread(): return lax.all_to_all(many, axes, split_axis=0, concat_axis=0, tiled=False)]
    all_gather x1 -> x0, blocking collectives: 42.9 us -> none  [shards(): all_heads = lax.all_gather(attended, 'dp', axis=0, tiled=True)]
    all_to_all x0 -> x2, starting transfers between devices: none -> 15.5 us  [the longest x1 8.19 us: spread(): return lax.all_to_all(many, axes, split_axis=0, concat_axis=0, tiled=False)]
    all_to_all x0 -> x2, waiting for transfers between devices: none -> 12.7 us  [the longest x1 7.29 us: spread(): return lax.all_to_all(many, axes, split_axis=0, concat_axis=0, tiled=False)]
  transfers between devices with their start and end apart: 2 -> 6, of which waited for: 2 -> 3; matrix products, arithmetic and copies ran while one was open for 0% -> 6% of each run, Pallas kernels for 0% -> 0%
where the time goes in v1:
time: 112 us
  blocking collectives  52.2 us (47%)
  starting transfers between devices  24 us (21%)
  waiting for transfers between devices  15.3 us (14%)
  matrix products  10.9 us (10%)
  local copies, waits for them, and re-layouts  4.87 us (4%)
  other arithmetic  3.51 us (3%)
    all_to_all x4, blocking collectives, spread(): return lax.all_to_all(many, axes, split_axis=0, concat_axis=0, tiled=False)  52.2 us
    all_to_all x1, starting transfers between devices, spread(): return lax.all_to_all(many, axes, split_axis=0, concat_axis=0, tiled=False)  8.19 us
    all_to_all x1, waiting for transfers between devices, spread(): return lax.all_to_all(many, axes, split_axis=0, concat_axis=0, tiled=False)  7.29 us
    all_to_all x1, starting transfers between devices, shards(): lax.all_to_all(partial, ('c', 'y'), split_axis=0, concat_axis=0, tiled=Fa...  7.28 us
    ppermute x3, starting transfers between devices, shards(): pack = lax.ppermute(pack, 'x', [(i, (i + step) % nx) for i in range(nx)])  5.87 us
    all_to_all x1, waiting for transfers between devices, shards(): lax.all_to_all(partial, ('c', 'y'), split_axis=0, concat_axis=0, tiled=Fa...  5.38 us
    dot_general x1, matrix products, shards(): lax.dot_general(lm_head, everyone, (((1,), (1,)), ((), ())), preferred_el...  4.62 us
    ppermute x1, waiting for transfers between devices, shards(): other = lax.ppermute(half, 'c', [(i, 1 - i) for i in range(2)])  2.66 us
  transfers between devices with their start and end apart: 6, of which 3 were waited for; matrix products, arithmetic and copies ran while one was open for 6% of the time, Pallas kernels for 0%

profile of v1, /device:TPU:1, one launch (start us, length us, event | category | flops | bytes accessed | tf_op | source)
XLA Modules:
  0.0 111.8 jit_solution(5096314467161863019)
XLA Ops:
  0.7 0.8 subtract_convert_fusion
  1.5 1.2 %constant_dynamic-slice_fusion.4 = (bf16[8,160]{0,1:T(8,128)(2,1)S(1)}, bf16[8,160]{0,1:T(8,128)(2,1)S(1)}, bf16[8,160]{0,1:T(8,128)(2,1)S(1)}, bf16[8,160]{0,1:T(8,128)(2,1)S(1)}) fusion(bf16[256,160]{0,1:T(8,128)(2,1)} %param.14, s32[]{:T(128)S(6)} %select_n.40, s32[]{:T(128)S(6)} %select_n.42, s32[]{:T(128)S(6)} %select_n.41, s32[]{:T(128)S(6)} %select_n.43), kind=kLoop, calls=%fused_computation.68 | loop fusion | bytes 20496 | tf_op jit(solution)/shard_map/dynamic_slice | solution.py:74
  2.7 0.1 copy.92
  2.7 1.1 %copy.68 = bf16[640,160]{1,0:T(8,128)(2,1)S(1)} copy(bf16[640,160]{0,1:T(8,128)(2,1)} %param.15) | data formatting | bytes 409600 | tf_op args[5]
  3.9 0.3 concatenate.30
  4.2 2.1 %collective-permute-start = (bf16[651,160]{1,0:T(8,128)(2,1)S(1)}, bf16[651,160]{1,0:T(8,128)(2,1)S(1)}, u32[]{:S(2)}, u32[]{:S(2)}) collective-permute-start(bf16[651,160]{1,0:T(8,128)(2,1)S(1)} %concatenate.30), channel_id=1, source_target_pairs={{0,8},{8,16},{16,24},{24,0},{1,9},{9,17},{17,25},{25,1},{2,10},{10... | collective-permute-start | bytes 624968 | tf_op jit(solution)/shard_map/ppermute | solution.py:77
  6.3 0.1 copy.93
  6.4 0.3 concatenate.31
  6.7 2.5 %collective-permute-start.1 = (bf16[651,160]{1,0:T(8,128)(2,1)S(1)}, bf16[651,160]{1,0:T(8,128)(2,1)S(1)}, u32[]{:S(2)}, u32[]{:S(2)}) collective-permute-start(bf16[651,160]{1,0:T(8,128)(2,1)S(1)} %concatenate.31), channel_id=1, source_target_pairs={{0,16},{8,24},{16,0},{24,8},{1,17},{9,25},{17,1},{25,9},{2,18},{10... | collective-permute-start | bytes 624968 | tf_op jit(solution)/shard_map/ppermute | solution.py:77
  9.2 0.1 copy.94
  9.3 0.3 concatenate.32
  9.6 1.2 %collective-permute-start.2 = (bf16[651,160]{1,0:T(8,128)(2,1)S(1)}, bf16[651,160]{1,0:T(8,128)(2,1)S(1)}, u32[]{:S(2)}, u32[]{:S(2)}) collective-permute-start(bf16[651,160]{1,0:T(8,128)(2,1)S(1)} %concatenate.32), channel_id=1, source_target_pairs={{0,24},{8,0},{16,8},{24,16},{1,25},{9,1},{17,9},{25,17},{2,26},{10... | collective-permute-start | bytes 624968 | tf_op jit(solution)/shard_map/ppermute | solution.py:77
  10.9 0.1 dynamic_slice.22
  10.9 0.1 iota_compare_fusion.1
  11.1 0.1 fusion.45
  11.2 2.3 %fusion.56 = (f32[8,5]{1,0:T(8,128)S(1)}, f32[8,5,1024]{2,1,0:T(8,128)S(1)}) fusion(bf16[8,2,1024,128]{3,2,1,0:T(8,128)(2,1)} %param.11, bf16[8,5,128]{2,0,1:T(8,128)(2,1)S(1)} %bitcast.77, pred[8,1024]{1,0:T(8,128)(4,1)S(1)} %iota_compare_fusion.1), kind=kOutput, calls=%fused_computation.85 | convolution fusion | flops 10608600 | bytes 2279584 | tf_op jit(solution)/shard_map/rkgd,rbkd->rkgb/dot_general | solution.py:36
  13.5 0.2 fusion.38
  13.7 2.6 %fusion.25 = bf16[1,8,5,128]{3,2,1,0:T(8,128)(2,1)S(1)} fusion(bf16[8,2,1024,128]{3,2,1,0:T(8,128)(2,1)} %param.11, f32[8,5,1024]{2,1,0:T(8,128)S(1)} %get-tuple-element.32, f32[8,5]{1,0:T(8,128)S(1)} %multiply_maximum_fusion, f32[8,5]{1,0:T(8,128)S(1)} %get-tuple-element.12, f32[8,128]{1,0:T(8,128)S(1)} %bitcast.78, f32[8,5]{1,0:T(8,128)S(1)} %get-tuple-element.13), kind=kOutput, calls=%fused_computation.17 | convolution fusion | flops 62976000 | bytes 2275808 | tf_op jit(solution)/shard_map/rkgb,rbkd->rkgd/dot_general | solution.py:43
  16.3 0.6 broadcast_in_dim.29
  17.0 8.2 %all-to-all-start = ((bf16[8,8,640]{2,1,0:T(8,128)(2,1)}), bf16[8,8,640]{2,1,0:T(8,128)(2,1)S(1)}, u32[]{:S(2)}, u32[]{:S(2)}) async-start(bf16[8,8,640]{2,1,0:T(8,128)(2,1)} %broadcast_in_dim.29), calls=%async_computation | async-start | bytes 163840 | tf_op jit(solution)/shard_map/all_to_all | solution.py:52
  25.2 0.0 collective-permute-done
  25.3 7.3 %all-to-all-done = bf16[8,8,640]{2,1,0:T(8,128)(2,1)S(1)} async-done(((bf16[8,8,640]{2,1,0:T(8,128)(2,1)}), bf16[8,8,640]{2,1,0:T(8,128)(2,1)S(1)}, u32[]{:S(2)}, u32[]{:S(2)}) %all-to-all-start) | async-done | bytes 81952 | tf_op jit(solution)/shard_map/all_to_all | solution.py:52
  32.6 1.3 %fusion.28 = f32[8,8,640]{2,1,0:T(8,128)} fusion(bf16[8,8,640]{2,1,0:T(8,128)(2,1)S(1)} %all-to-all-done, bf16[640,160]{1,0:T(8,128)(2,1)S(1)} %slice.99, bf16[640,160]{1,0:T(8,128)(2,1)S(1)} %slice.98, bf16[640,160]{1,0:T(8,128)(2,1)S(1)} %slice.97, bf16[640,160]{1,0:T(8,128)(2,1)S(1)} %copy.68), kind=kOutput, calls=%fused_computation.19 | convolution fusion | flops 55705600 | bytes 1064960 | tf_op jit(solution)/shard_map/dot_general | solution.py:87
  33.9 7.3 %all-to-all-start.1 = ((f32[8,8,640]{2,1,0:T(8,128)}), f32[8,8,640]{2,1,0:T(8,128)S(1)}, u32[]{:S(2)}, u32[]{:S(2)}) async-start(f32[8,8,640]{2,1,0:T(8,128)} %fusion.28), calls=%async_computation.1 | async-start | bytes 327680 | tf_op jit(solution)/shard_map/all_to_all | solution.py:89
  41.1 0.1 copy.91
  41.3 5.4 %all-to-all-done.1 = f32[8,8,640]{2,1,0:T(8,128)S(1)} async-done(((f32[8,8,640]{2,1,0:T(8,128)}), f32[8,8,640]{2,1,0:T(8,128)S(1)}, u32[]{:S(2)}, u32[]{:S(2)}) %all-to-all-start.1) | async-done | bytes 163872 | tf_op jit(solution)/shard_map/all_to_all | solution.py:89
  46.7 0.1 add_convert_fusion
  46.8 0.1 maximum_maximum_fusion
  46.8 0.1 fusion.55
  46.9 0.1 concatenate.37
  47.0 0.1 constant_dynamic-slice_fusion
  47.1 11.6 %all_to_all.30 = bf16[8,11,640]{2,1,0:T(8,128)(2,1)S(1)} all-to-all(bf16[8,11,640]{2,1,0:T(8,128)(2,1)S(1)} %broadcast_in_dim.30), channel_id=1, replica_groups=mesh['z'=8,'x'=4,'y'=4,'c'=2] {'z'}, dimensions={0} | all-to-all | bytes 225280 | tf_op jit(solution)/shard_map/all_to_all | solution.py:52
  58.7 0.2 fusion.39
  58.9 0.0 copy-start.3
  58.9 0.1 fusion.41
  59.0 0.1 broadcast_in_dim.33
  59.1 20.9 %all_to_all.31 = bf16[16,8,5120]{2,1,0:T(8,128)(2,1)S(1)} all-to-all(bf16[16,8,5120]{2,1,0:T(8,128)(2,1)S(1)} %broadcast_in_dim.33), channel_id=1, replica_groups=mesh['z'=8,'x'=4,'y'=4,'c'=2] {'y','x'}, dimensions={0} | all-to-all | bytes 2621440 | tf_op jit(solution)/shard_map/all_to_all | solution.py:52
  80.1 2.6 %collective-permute-start.3 = (bf16[128,5120]{1,0:T(8,128)(2,1)S(1)}, bf16[128,5120]{1,0:T(8,128)(2,1)S(1)}, u32[]{:S(2)}, u32[]{:S(2)}) collective-permute-start(bf16[128,5120]{1,0:T(8,128)(2,1)S(1)} %bitcast.73), channel_id=1, source_target_pairs={{0,1},{1,0},{2,3},{3,2},{4,5},{5,4},{6,7},{7,6},{8,9},{9,8},{10,11... | collective-permute-start | bytes 3932168 | tf_op jit(solution)/shard_map/ppermute | solution.py:106
  82.7 2.7 %collective-permute-done.3 = bf16[128,5120]{1,0:T(8,128)(2,1)S(1)} collective-permute-done((bf16[128,5120]{1,0:T(8,128)(2,1)S(1)}, bf16[128,5120]{1,0:T(8,128)(2,1)S(1)}, u32[]{:S(2)}, u32[]{:S(2)}) %collective-permute-start.3) | collective-permute-done | bytes 1310752 | tf_op jit(solution)/shard_map/ppermute | solution.py:106
  85.4 0.2 broadcast_select_fusion.1
  85.5 0.0 copy-start.2
  85.5 4.6 %fusion.57 = (f32[256]{0:T(256)S(1)}, f32[256,594]{0,1:T(8,128)S(1)}) fusion(bf16[594,5120]{1,0:T(8,128)(2,1)} %param.17, bf16[128,5120]{1,0:T(8,128)(2,1)S(1)} %get-tuple-element.15, bf16[128,5120]{1,0:T(8,128)(2,1)S(1)} %get-tuple-element.14), kind=kOutput, calls=%fused_computation.86 | convolution fusion | flops 1562530048 | bytes 9313280 | tf_op jit(solution)/shard_map/dot_general | solution.py:110
  90.2 0.2 fusion.36
  90.4 10.7 %all_to_all.32 = f32[32,2,256]{2,1,0:T(2,128)S(1)} all-to-all(f32[32,2,256]{2,1,0:T(2,128)S(1)} %broadcast_in_dim.35), channel_id=1, replica_groups=mesh['z'=8,'x'=4,'y'=4,'c'=2] {'x','y','c'}, dimensions={0} | all-to-all | bytes 131072 | tf_op jit(solution)/shard_map/all_to_all | solution.py:52
  101.1 0.1 slice_reduce_fusion.3
  101.3 9.0 %all_to_all.33 = f32[8,2,256]{2,1,0:T(2,128)S(1)} all-to-all(f32[8,2,256]{2,1,0:T(2,128)S(1)} %broadcast_in_dim.36), channel_id=1, replica_groups=mesh['z'=8,'x'=4,'y'=4,'c'=2] {'z'}, dimensions={0} | all-to-all | bytes 32768 | tf_op jit(solution)/shard_map/all_to_all | solution.py:52
  110.3 0.6 multiply_subtract_fusion
  110.9 0.9 broadcast_subtract_fusion
  (42 shorter events, 0.4 us)
Async XLA Ops:
  0.6 10.2 %copy-start.4 = (s32[256]{0:T(256)S(1)}, s32[256]{0:T(256)}, u32[]{:S(2)}) copy-start(s32[256]{0:T(256)} %param.13) | copy-start | bytes 3076
  0.6 10.4 %copy-start.1 = (bf16[8,2,128]{2,1,0:T(2,128)(2,1)S(1)}, bf16[8,2,128]{2,1,0:T(2,128)(2,1)}, u32[]{:S(2)}) copy-start(bf16[8,2,128]{2,1,0:T(2,128)(2,1)} %param.12) | copy-start | bytes 12292
  0.7 10.4 %copy-start = (bf16[8,640]{1,0:T(8,128)(2,1)S(1)}, bf16[8,640]{1,0:T(8,128)(2,1)}, u32[]{:S(2)}) copy-start(bf16[8,640]{1,0:T(8,128)(2,1)} %param.10) | copy-start | bytes 30724
  4.2 21.0 %collective-permute-start = (bf16[651,160]{1,0:T(8,128)(2,1)S(1)}, bf16[651,160]{1,0:T(8,128)(2,1)S(1)}, u32[]{:S(2)}, u32[]{:S(2)}) collective-permute-start(bf16[651,160]{1,0:T(8,128)(2,1)S(1)} %concatenate.30), channel_id=1, source_target_pairs={{0,8},{8,16},{16,24},{24,0},{1,9},{9,17},{17,25},{25,1},{2,10},{10... | collective-permute-start | bytes 624968 | tf_op jit(solution)/shard_map/ppermute | solution.py:77
  6.7 18.5 %collective-permute-start.1 = (bf16[651,160]{1,0:T(8,128)(2,1)S(1)}, bf16[651,160]{1,0:T(8,128)(2,1)S(1)}, u32[]{:S(2)}, u32[]{:S(2)}) collective-permute-start(bf16[651,160]{1,0:T(8,128)(2,1)S(1)} %concatenate.31), channel_id=1, source_target_pairs={{0,16},{8,24},{16,0},{24,8},{1,17},{9,25},{17,1},{25,9},{2,18},{10... | collective-permute-start | bytes 624968 | tf_op jit(solution)/shard_map/ppermute | solution.py:77
  9.6 15.6 %collective-permute-start.2 = (bf16[651,160]{1,0:T(8,128)(2,1)S(1)}, bf16[651,160]{1,0:T(8,128)(2,1)S(1)}, u32[]{:S(2)}, u32[]{:S(2)}) collective-permute-start(bf16[651,160]{1,0:T(8,128)(2,1)S(1)} %concatenate.32), channel_id=1, source_target_pairs={{0,24},{8,0},{16,8},{24,16},{1,25},{9,1},{17,9},{25,17},{2,26},{10... | collective-permute-start | bytes 624968 | tf_op jit(solution)/shard_map/ppermute | solution.py:77
  17.0 15.6 %all-to-all-start = ((bf16[8,8,640]{2,1,0:T(8,128)(2,1)}), bf16[8,8,640]{2,1,0:T(8,128)(2,1)S(1)}, u32[]{:S(2)}, u32[]{:S(2)}) async-start(bf16[8,8,640]{2,1,0:T(8,128)(2,1)} %broadcast_in_dim.29), calls=%async_computation | async-start | bytes 163840 | tf_op jit(solution)/shard_map/all_to_all | solution.py:52
  33.9 12.8 %all-to-all-start.1 = ((f32[8,8,640]{2,1,0:T(8,128)}), f32[8,8,640]{2,1,0:T(8,128)S(1)}, u32[]{:S(2)}, u32[]{:S(2)}) async-start(f32[8,8,640]{2,1,0:T(8,128)} %fusion.28), calls=%async_computation.1 | async-start | bytes 327680 | tf_op jit(solution)/shard_map/all_to_all | solution.py:89
  58.9 23.8 %copy-start.3 = (s32[256]{0:T(256)S(1)}, s32[256]{0:T(256)}, u32[]{:S(2)}) copy-start(s32[256]{0:T(256)} %param.18) | copy-start | bytes 3076
  80.1 5.3 %collective-permute-start.3 = (bf16[128,5120]{1,0:T(8,128)(2,1)S(1)}, bf16[128,5120]{1,0:T(8,128)(2,1)S(1)}, u32[]{:S(2)}, u32[]{:S(2)}) collective-permute-start(bf16[128,5120]{1,0:T(8,128)(2,1)S(1)} %bitcast.73), channel_id=1, source_target_pairs={{0,1},{1,0},{2,3},{3,2},{4,5},{5,4},{6,7},{7,6},{8,9},{9,8},{10,11... | collective-permute-start | bytes 3932168 | tf_op jit(solution)/shard_map/ppermute | solution.py:106
  85.5 24.8 %copy-start.2 = (f32[256]{0:T(256)S(1)}, f32[256]{0:T(256)}, u32[]{:S(2)}) copy-start(f32[256]{0:T(256)} %param.19) | copy-start | bytes 3076

commit v2 on v1

v2 whole, which is shorter than its diff:
```python
import functools
import math

import jax
import jax.numpy as jnp
import numpy as np
from jax import lax
from jax.experimental import pallas as pl
from jax.experimental.pallas import tpu as pltpu
from jax.sharding import Mesh
from jax.sharding import PartitionSpec as P

D = 5120
HEADS = 40
KV_HEADS = 8
HEAD_DIM = 128

masked_score = -1e30
epsilon = 1e-06
learn_rate = 0.1
target_bits = 5.0

bf16 = jnp.bfloat16
f32 = jnp.float32
LANES = 128

IN_VMEM = pl.BlockSpec(memory_space=pltpu.VMEM)
IN_SMEM = pl.BlockSpec(memory_space=pltpu.SMEM)
IN_PLACE = pl.BlockSpec(memory_space=pl.ANY)
SMALL = pltpu.CompilerParams(vmem_limit_bytes=20 << 20)
WIDE = pltpu.CompilerParams(vmem_limit_bytes=50 << 20)
WHOLE = pltpu.CompilerParams(vmem_limit_bytes=60 << 20)
TAIL = 16
CHUNK = 1280


def three_parts(wide):
    first = wide.astype(bf16).astype(f32)
    rest = wide - first
    second = rest.astype(bf16).astype(f32)
    third = (rest - second).astype(bf16).astype(f32)
    return first, second, third


def pack_kernel(count, place_ref, table_hbm, hidden_hbm, gain_hbm, own_ref, *refs):
    packs, (table_ref, hidden_ref, gain_ref, sems) = refs[:-4], refs[-4:]
    loads = [
        pltpu.make_async_copy(source, target, sems.at[k])
        for k, (source, target) in enumerate(
            ((table_hbm, table_ref), (hidden_hbm, hidden_ref), (gain_hbm, gain_ref))
        )
    ]
    for load in loads:
        load.start()
    columns, heads = table_ref.shape
    requests = hidden_ref.shape[1]
    for load in loads:
        load.wait()
    row = lax.broadcasted_iota(jnp.int32, (count, requests), 0)
    lane = lax.broadcasted_iota(jnp.int32, (count, requests), 1)
    parts = three_parts(gain_ref[...])
    below = jnp.concatenate(parts + (jnp.zeros((TAIL - count - 3, columns), f32),), axis=0)
    for step in range(len(packs) + 1):
        chosen = jnp.where(lane == row + place_ref[step], 1.0, 0.0).astype(bf16)
        hidden = lax.dot_general(
            chosen, hidden_ref[...], (((1,), (1,)), ((), ())), preferred_element_type=f32
        )
        tail = jnp.concatenate([hidden, below], axis=0).astype(bf16)
        if step == 0:
            own_ref[...] = tail
        else:
            packs[step - 1][:columns] = table_ref[...]
            packs[step - 1][columns:] = jnp.zeros((TAIL, heads), bf16)
            packs[step - 1][columns:, :columns] = tail


def attend_kernel(group, base_ref, lengths_ref, query_ref, new_ref, cache_ref, out_ref, slots_ref, rows_ref, sems):
    count, _, slots, head_dim = cache_ref.shape
    copies = out_ref.shape[0]
    scale = head_dim ** (-0.5)
    loads = [pltpu.make_async_copy(cache_ref.at[r], slots_ref.at[r], sems.at[r]) for r in range(count)]
    for load in loads:
        load.start()
    query = query_ref[...].astype(f32)
    fresh = new_ref[...].astype(f32)
    position = lax.broadcasted_iota(jnp.int32, (8, slots), 1)
    for r in range(count):
        pieces = [query[r : r + 1, g * head_dim : (g + 1) * head_dim] for g in range(group)]
        pieces.append(jnp.zeros((8 - group, head_dim), f32))
        heads = jnp.concatenate(pieces, axis=0)
        own_score = jnp.sum(heads * fresh[r, 0:1], axis=1, keepdims=True) * scale
        loads[r].wait()
        scores = lax.dot_general(
            heads.astype(bf16), slots_ref[r, 0], (((1,), (1,)), ((), ())), preferred_element_type=f32
        ) * scale
        scores = jnp.where(position < lengths_ref[base_ref[0] + r], scores, masked_score)
        top = jnp.maximum(jnp.max(scores, axis=1, keepdims=True), own_score)
        weights = jnp.exp(scores - top)
        own_weight = jnp.exp(own_score - top)
        mass = jnp.sum(weights, axis=1, keepdims=True) + own_weight
        stacked = jnp.concatenate(three_parts(weights), axis=0).astype(bf16)
        sums = jnp.dot(stacked, slots_ref[r, 1], preferred_element_type=f32)
        total = sums[:8] + sums[8:16] + sums[16:24] + own_weight * fresh[r, 1:2]
        total = total / mass
        for g in range(group):
            rows_ref[r : r + 1, g * head_dim : (g + 1) * head_dim] = total[g : g + 1]
    done = rows_ref[...].astype(bf16)
    for k in range(copies):
        out_ref[k] = done


def resid_kernel(x_ref, partial_ref, own_ref, *refs):
    packs, out_ref = refs[:-1], refs[-1]
    count, width = partial_ref.shape[1:]
    columns = width // (len(packs) + 1)
    total = partial_ref[0]
    for k in range(1, partial_ref.shape[0]):
        total = total + partial_ref[k]
    squares = jnp.zeros((count, 1), f32)
    blocks = []
    for step in range(len(packs) + 1):
        tail = own_ref[...] if step == 0 else packs[step - 1][columns:, :columns]
        tail = tail.astype(f32)
        gain = tail[count : count + 1] + tail[count + 1 : count + 2] + tail[count + 2 : count + 3]
        resid = total[:, step * columns : (step + 1) * columns] + tail[:count]
        resid = resid.astype(bf16).astype(f32)
        squares = squares + jnp.sum(resid * resid, axis=1, keepdims=True)
        blocks.append(resid * gain)
    ordered = pltpu.roll(jnp.concatenate(blocks[::-1], axis=1), x_ref[0], 1)
    lane = lax.broadcasted_iota(jnp.int32, (count, LANES), 1)
    spare = jnp.zeros((count, LANES), f32)
    for k, part in enumerate(three_parts(squares)):
        spare = jnp.where(lane == k, part, spare)
    done = jnp.concatenate([ordered, spare], axis=1).astype(bf16)
    for k in range(out_ref.shape[0]):
        out_ref[k] = done


def norm_kernel(rows_ref, out_ref):
    blocks, count, padded = rows_ref.shape
    width = padded - LANES
    squares = jnp.zeros((count, LANES), f32)
    for k in range(blocks):
        squares = squares + rows_ref[k, :, width:].astype(f32)
    factor = lax.rsqrt(jnp.sum(squares, axis=1, keepdims=True) / D + epsilon)
    for k in range(blocks):
        done = (rows_ref[k, :, :width].astype(f32) * factor).astype(bf16)
        for copy in range(out_ref.shape[0]):
            out_ref[copy, :, k * width : (k + 1) * width] = done


def logits_kernel(head_hbm, rows_ref, ids_ref, logits_ref, stats_ref, head_ref, sems):
    depth = head_ref.shape[1]
    spans = [slice(k, k + CHUNK) for k in range(0, depth, CHUNK)]
    loads = [
        pltpu.make_async_copy(head_hbm.at[:, span], head_ref.at[:, span], sems.at[k])
        for k, span in enumerate(spans)
    ]
    for load in loads:
        load.start()
    for k, span in enumerate(spans):
        loads[k].wait()
        product = lax.dot_general(
            head_ref[:, span], rows_ref[:, span], (((1,), (1,)), ((), ())), preferred_element_type=f32
        )
        if k == 0:
            logits_ref[...] = product
        else:
            logits_ref[...] += product
    logits = logits_ref[...]
    top = jnp.max(logits, axis=0, keepdims=True)
    log_mass = top + jnp.log(jnp.sum(jnp.exp(logits - top), axis=0, keepdims=True))
    hits = lax.broadcasted_iota(jnp.int32, logits.shape, 0) == ids_ref[...]
    picked = jnp.sum(jnp.where(hits, logits, 0.0), axis=0, keepdims=True)
    stats_ref[...] = jnp.concatenate([log_mass, picked], axis=0)


def final_kernel(logits_ref, stats_ref, mu_ref, logprobs_ref, surprise_ref, mu_next_ref):
    masses = stats_ref[:, 0]
    top = jnp.max(masses, axis=0, keepdims=True)
    log_mass = top + jnp.log(jnp.sum(jnp.exp(masses - top), axis=0, keepdims=True))
    picked = jnp.sum(stats_ref[:, 1], axis=0, keepdims=True)
    logprobs_ref[...] = logits_ref[...] - log_mass
    surprise = (log_mass - picked) / math.log(2.0)
    surprise_ref[...] = surprise
    mu_next_ref[...] = mu_ref[...] - learn_rate * (surprise - target_bits)


def spread(block, axes, count):
    many = jnp.broadcast_to(block[None], (count,) + block.shape)
    return lax.all_to_all(many, axes, split_axis=0, concat_axis=0, tiled=False)


def shards(query, cache, new_kv, lengths, hidden_in, out_proj, final_gain, lm_head, tokens, mu):
    nz, nx, ny, nc = (lax.axis_size(a) for a in ("z", "x", "y", "c"))
    z, x, y, c = (lax.axis_index(a) for a in ("z", "x", "y", "c"))
    count = query.shape[0]
    heads, columns = out_proj.shape
    part = c * ny + y

    targets = lax.rem(x + jnp.arange(nx, dtype=jnp.int32), nx)
    place = (part * nx + targets) * count
    pack_shape = jax.ShapeDtypeStruct((columns + TAIL, heads), bf16)
    own_tail, *packs = pl.pallas_call(
        functools.partial(pack_kernel, count),
        out_shape=[jax.ShapeDtypeStruct((TAIL, columns), bf16)] + [pack_shape] * (nx - 1),
        in_specs=[IN_SMEM] + [IN_PLACE] * 3,
        out_specs=[IN_VMEM] * nx,
        scratch_shapes=[
            pltpu.VMEM((columns, heads), bf16),
            pltpu.VMEM((columns, hidden_in.shape[0]), bf16),
            pltpu.VMEM((1, columns), f32),
            pltpu.SemaphoreType.DMA((3,)),
        ],
        compiler_params=WHOLE,
        name="pack",
    )(place, out_proj.T, hidden_in.T, final_gain[None])
    packs = [
        lax.ppermute(pack, "x", [(i, (i + step) % nx) for i in range(nx)])
        for step, pack in enumerate(packs, 1)
    ]
    table = jnp.concatenate([out_proj.T] + [p[:columns] for p in packs], axis=0)

    many = pl.pallas_call(
        functools.partial(attend_kernel, HEADS // KV_HEADS),
        out_shape=jax.ShapeDtypeStruct((nz,) + query.shape, bf16),
        in_specs=[IN_SMEM] * 2 + [IN_VMEM] * 2 + [IN_PLACE],
        out_specs=IN_VMEM,
        scratch_shapes=[
            pltpu.VMEM(cache.shape, bf16),
            pltpu.VMEM(query.shape, f32),
            pltpu.SemaphoreType.DMA((count,)),
        ],
        compiler_params=WHOLE,
        name="attend",
    )(((z * nx + x) * count)[None], lengths, query, new_kv, cache)
    gathered = lax.all_to_all(many, "z", split_axis=0, concat_axis=0, tiled=False)
    gathered = gathered.reshape(nz * count, -1)
    partial = lax.dot_general(
        gathered, table, (((1,), (1,)), ((), ())), preferred_element_type=f32
    )
    partial = partial.reshape(nz, count, nx * columns)
    partial = lax.all_to_all(partial, ("c", "y"), split_axis=0, concat_axis=0, tiled=False)

    width = nx * columns
    rows = pl.pallas_call(
        resid_kernel,
        out_shape=jax.ShapeDtypeStruct((nz, count, width + LANES), bf16),
        in_specs=[IN_SMEM] + [IN_VMEM] * (nx + 1),
        out_specs=IN_VMEM,
        compiler_params=SMALL,
        name="resid",
    )((lax.rem(x + 1, nx) * columns)[None], partial, own_tail, *packs)
    rows = lax.all_to_all(rows, "z", split_axis=0, concat_axis=0, tiled=False)
    half = pl.pallas_call(
        norm_kernel,
        out_shape=jax.ShapeDtypeStruct((nx * ny, count, nz * width), bf16),
        in_specs=[IN_VMEM],
        out_specs=IN_VMEM,
        compiler_params=SMALL,
        name="norm",
    )(rows)
    half = lax.all_to_all(half, ("x", "y"), split_axis=0, concat_axis=0, tiled=False)
    other = lax.ppermute(half, "c", [(i, 1 - i) for i in range(2)])
    half, other = (
        jnp.swapaxes(h.reshape(nx, ny, count, -1), 0, 1).reshape(nx * ny * count, -1) for h in (half, other)
    )
    first = jnp.where(c == 0, half, other)
    second = jnp.where(c == 0, other, half)
    everyone = jnp.concatenate([first, second], axis=0)

    vocab = lm_head.shape[0]
    requests = everyone.shape[0]
    offset = (((z * nx + x) * ny + y) * nc + c) * vocab
    logits, stats = pl.pallas_call(
        logits_kernel,
        out_shape=[jax.ShapeDtypeStruct((vocab, requests), f32), jax.ShapeDtypeStruct((2, requests), f32)],
        in_specs=[IN_PLACE] + [IN_VMEM] * 2,
        out_specs=[IN_VMEM] * 2,
        scratch_shapes=[
            pltpu.VMEM(lm_head.shape, bf16),
            pltpu.SemaphoreType.DMA((lm_head.shape[1] // CHUNK,)),
        ],
        compiler_params=WIDE,
        name="logits",
    )(lm_head, everyone, (tokens - offset)[None])

    stats = spread(stats, ("x", "y", "c"), nx * ny * nc)
    top = jnp.max(stats[:, 0], axis=0)
    log_mass = top + jnp.log(jnp.sum(jnp.exp(stats[:, 0] - top[None, :]), axis=0))
    picked = jnp.sum(stats[:, 1], axis=0)
    stats = spread(jnp.stack([log_mass, picked]), "z", nz)
    row_shape = jax.ShapeDtypeStruct((1, requests), f32)
    logprobs, surprise, mu_next = pl.pallas_call(
        final_kernel,
        out_shape=[jax.ShapeDtypeStruct((vocab, requests), f32), row_shape, row_shape],
        in_specs=[IN_VMEM] * 3,
        out_specs=[IN_VMEM] * 3,
        compiler_params=SMALL,
        name="final",
    )(logits, stats, mu[None])
    return (logprobs.T, surprise[0], mu_next[0])


def solution(mesh):
    grid = Mesh(np.asarray(mesh.devices).reshape(8, 4, 4, 2), ("z", "x", "y", "c"))
    dp, tensor = ("z", "x"), ("y", "c")
    placed = (
        P(dp, tensor),
        P(dp, None, None, tensor),
        P(dp, None, tensor),
        P(),
        P(None, dp),
        P(tensor, dp),
        P(dp),
        P(dp + tensor, None),
        P(),
        P(),
    )
    return jax.shard_map(
        shards,
        mesh=grid,
        in_specs=placed,
        out_specs=(P(None, dp + tensor), P(), P()),
        check_vma=False,
    )
```

time: 112 us -> 110 us (0.982)
  Pallas kernels: 0 us -> 15.6 us
  matrix products: 10.9 us -> 1.05 us
  local copies, waits for them, and re-layouts: 4.87 us -> 0.28 us
  other arithmetic: 3.51 us -> 1 us
  blocking collectives: 52.2 us -> 50.2 us
    all_to_all x4 -> x2, blocking collectives: 52.2 us -> 20.3 us  [spread(): return lax.all_to_all(many, axes, split_axis=0, concat_axis=0, tiled=False)]
    all_to_all x0 -> x2, blocking collectives: none -> 29.9 us  [the longest x1 19.9 us: shards(): lax.all_to_all(half, ('x', 'y'), split_axis=0, concat_axis=0, tiled=False)]
    pallas_call x0 -> x6, Pallas kernels: none -> 15.6 us  [the longest x1 6.03 us: shards(): pl.pallas_call(functools.partial(attend_kernel, HEADS // KV_HEADS), out_s...]
    dot_general x5 -> x1, matrix products: 10.9 us -> 1.05 us  [shards(): lax.dot_general(gathered, table, (((1,), (1,)), ((), ())), preferred_elem...]
    sub x2 -> x0, other arithmetic: 1.44 us -> none  [the longest x1 0.86 us: shards(): logprobs = (logits - log_mass[None, :]).T]
    unnamed x17 -> x8, local copies, waits for them, and re-layouts: 1.39 us -> 0.02 us
    dynamic_slice x3 -> x0, local copies, waits for them, and re-layouts: 1.34 us -> none  [the longest x1 1.18 us: shards(): lax.dynamic_slice_in_dim(hidden_in, (part * nx + target) * request_count,...]
  transfers between devices with their start and end apart: 6 -> 6, of which waited for: 3 -> 3; matrix products, arithmetic and copies ran while one was open for 6% -> 0% of each run, Pallas kernels for 0% -> 6%
where the time goes in v2:
time: 110 us; the launch traced here: 109 us
  blocking collectives  50.2 us (46%)
  starting transfers between devices  24.6 us (22%)
  Pallas kernels  15.6 us (14%)
  waiting for transfers between devices  15.6 us (14%)
    all_to_all x2, blocking collectives, spread(): return lax.all_to_all(many, axes, split_axis=0, concat_axis=0, tiled=False)  20.3 us
    all_to_all x1, blocking collectives, shards(): lax.all_to_all(half, ('x', 'y'), split_axis=0, concat_axis=0, tiled=False)  19.9 us
    all_to_all x1, blocking collectives, shards(): rows = lax.all_to_all(rows, 'z', split_axis=0, concat_axis=0, tiled=False)  10 us
    all_to_all x1, starting transfers between devices, shards(): lax.all_to_all(many, 'z', split_axis=0, concat_axis=0, tiled=False)  8.2 us
    all_to_all x1, waiting for transfers between devices, shards(): lax.all_to_all(many, 'z', split_axis=0, concat_axis=0, tiled=False)  7.39 us
    all_to_all x1, starting transfers between devices, shards(): lax.all_to_all(partial, ('c', 'y'), split_axis=0, concat_axis=0, tiled=Fa...  7.31 us
    pallas_call x1, Pallas kernels, shards(): pl.pallas_call(functools.partial(attend_kernel, HEADS // KV_HEADS), out_s...  6.03 us
    ppermute x3, starting transfers between devices, shards(): lax.ppermute(pack, 'x', [(i, (i + step) % nx) for i in range(nx)])  5.72 us
  transfers between devices with their start and end apart: 6, of which 3 were waited for; matrix products, arithmetic and copies ran while one was open for 0% of the time, Pallas kernels for 6%

profile of v2, /device:TPU:1, one launch (start us, length us, event | category | flops | bytes accessed | tf_op | source)
XLA Modules:
  0.0 109.1 jit_solution(15500274624782840060)
XLA Ops:
  0.6 0.5 fusion.11.place_ref
  1.2 2.7 %pack.1 = (bf16[16,160]{1,0:T(8,128)(2,1)}, bf16[176,640]{1,0:T(8,128)(2,1)}, bf16[176,640]{1,0:T(8,128)(2,1)}, bf16[176,640]{1,0:T(8,128)(2,1)}) custom-call(s32[4]{0:T(128)} %fusion.11.place_ref, bf16[160,640]{1,0:T(8,128)(2,1)} %bitcast.36, bf16[160,256]{1,0:T(8,128)(2,1)} %bitcast.38, f32[1,160]{1,0:T(1,128)} %bitcast.41), custom_call_target="tpu_custom_call" | custom-call | tf_op jit(solution)/shard_map/pack/pallas_call | solution.py:204
  3.8 2.1 %collective-permute-start = (bf16[176,640]{1,0:T(8,128)(2,1)}, bf16[176,640]{1,0:T(8,128)(2,1)S(1)}, u32[]{:S(2)}, u32[]{:S(2)}) collective-permute-start(bf16[176,640]{1,0:T(8,128)(2,1)} %get-tuple-element.12), channel_id=1, source_target_pairs={{0,8},{8,16},{16,24},{24,0},{1,9},{9,17},{17,25},{25,1},{2,10},{10... | collective-permute-start | bytes 675848 | tf_op jit(solution)/shard_map/ppermute | solution.py:219
  6.0 2.5 %collective-permute-start.1 = (bf16[176,640]{1,0:T(8,128)(2,1)}, bf16[176,640]{1,0:T(8,128)(2,1)S(1)}, u32[]{:S(2)}, u32[]{:S(2)}) collective-permute-start(bf16[176,640]{1,0:T(8,128)(2,1)} %get-tuple-element.13), channel_id=1, source_target_pairs={{0,16},{8,24},{16,0},{24,8},{1,17},{9,25},{17,1},{25,9},{2,18},{10... | collective-permute-start | bytes 675848 | tf_op jit(solution)/shard_map/ppermute | solution.py:219
  8.4 1.2 %collective-permute-start.2 = (bf16[176,640]{1,0:T(8,128)(2,1)}, bf16[176,640]{1,0:T(8,128)(2,1)S(1)}, u32[]{:S(2)}, u32[]{:S(2)}) collective-permute-start(bf16[176,640]{1,0:T(8,128)(2,1)} %get-tuple-element.14), channel_id=1, source_target_pairs={{0,24},{8,0},{16,8},{24,16},{1,25},{9,1},{17,9},{25,17},{2,26},{10... | collective-permute-start | bytes 675848 | tf_op jit(solution)/shard_map/ppermute | solution.py:219
  9.6 0.0 copy-start.2
  9.6 6.0 %attend.1 = bf16[8,8,640]{2,1,0:T(8,128)(2,1)} custom-call(s32[1]{0:T(128)} %bitcast.1.base_ref, s32[256]{0:T(256)} %lengths_ref.1, bf16[8,640]{1,0:T(8,128)(2,1)} %query_ref.1, bf16[8,2,128]{2,1,0:T(2,128)(2,1)} %new_ref.1, bf16[8,2,1024,128]{3,2,1,0:T(8,128)(2,1)} %cache_ref.1), custom_call_target="tpu_custom_call" | custom-call | tf_op jit(solution)/shard_map/attend/pallas_call | solution.py:224
  15.6 8.2 %all-to-all-start = ((bf16[8,8,640]{2,1,0:T(8,128)(2,1)}), bf16[8,8,640]{2,1,0:T(8,128)(2,1)S(1)}, u32[]{:S(2)}, u32[]{:S(2)}) async-start(bf16[8,8,640]{2,1,0:T(8,128)(2,1)} %attend.1), calls=%async_computation | async-start | bytes 163840 | tf_op jit(solution)/shard_map/all_to_all | solution.py:237
  23.8 0.0 collective-permute-done.refs_0_
  23.8 0.0 collective-permute-done.1.refs_1_
  23.9 0.0 collective-permute-done.2.refs_2_
  23.9 0.0 copy-start
  23.9 7.4 %all-to-all-done = bf16[8,8,640]{2,1,0:T(8,128)(2,1)S(1)} async-done(((bf16[8,8,640]{2,1,0:T(8,128)(2,1)}), bf16[8,8,640]{2,1,0:T(8,128)(2,1)S(1)}, u32[]{:S(2)}, u32[]{:S(2)}) %all-to-all-start) | async-done | bytes 81952 | tf_op jit(solution)/shard_map/all_to_all | solution.py:237
  31.3 0.0 copy-done.2
  31.3 1.1 fusion
  32.4 7.3 %all-to-all-start.1 = ((f32[8,8,640]{2,1,0:T(8,128)}), f32[8,8,640]{2,1,0:T(8,128)S(1)}, u32[]{:S(2)}, u32[]{:S(2)}) async-start(f32[8,8,640]{2,1,0:T(8,128)} %fusion), calls=%async_computation.1 | async-start | bytes 327680 | tf_op jit(solution)/shard_map/all_to_all | solution.py:243
  39.7 5.5 %all-to-all-done.1.partial_ref = f32[8,8,640]{2,1,0:T(8,128)S(1)} async-done(((f32[8,8,640]{2,1,0:T(8,128)}), f32[8,8,640]{2,1,0:T(8,128)S(1)}, u32[]{:S(2)}, u32[]{:S(2)}) %all-to-all-start.1) | async-done | bytes 163872 | tf_op jit(solution)/shard_map/all_to_all | solution.py:243
  45.2 0.0 copy-done
  45.2 0.2 resid.1
  45.4 10.0 %all_to_all.30.rows_ref = bf16[8,8,768]{2,1,0:T(8,128)(2,1)S(1)} all-to-all(bf16[8,8,768]{2,1,0:T(8,128)(2,1)S(1)} %resid.1), channel_id=1, replica_groups=mesh['z'=8,'x'=4,'y'=4,'c'=2] {'z'}, dimensions={0} | all-to-all | bytes 196608 | tf_op jit(solution)/shard_map/all_to_all | solution.py:254
  55.5 0.2 norm.1
  55.7 0.0 copy-start.3
  55.7 19.9 %all_to_all.31 = bf16[16,8,5120]{2,1,0:T(8,128)(2,1)S(1)} all-to-all(bf16[16,8,5120]{2,1,0:T(8,128)(2,1)S(1)} %norm.1), channel_id=1, replica_groups=mesh['z'=8,'x'=4,'y'=4,'c'=2] {'x','y'}, dimensions={0} | all-to-all | bytes 2621440 | tf_op jit(solution)/shard_map/all_to_all | solution.py:263
  75.6 3.4 %collective-permute-start.3 = (bf16[16,8,5120]{2,1,0:T(8,128)(2,1)S(1)}, bf16[16,8,5120]{2,1,0:T(8,128)(2,1)S(1)}, u32[]{:S(2)}, u32[]{:S(2)}) collective-permute-start(bf16[16,8,5120]{2,1,0:T(8,128)(2,1)S(1)} %all_to_all.31), channel_id=1, source_target_pairs={{0,1},{1,0},{2,3},{3,2},{4,5},{5,4},{6,7},{7,6},{8,9},{9,8},{10,11... | collective-permute-start | bytes 3932168 | tf_op jit(solution)/shard_map/ppermute | solution.py:264
  79.0 0.0 copy-done.3
  79.0 2.7 %collective-permute-done.3 = bf16[16,8,5120]{2,1,0:T(8,128)(2,1)S(1)} collective-permute-done((bf16[16,8,5120]{2,1,0:T(8,128)(2,1)S(1)}, bf16[16,8,5120]{2,1,0:T(8,128)(2,1)S(1)}, u32[]{:S(2)}, u32[]{:S(2)}) %collective-permute-start.3) | collective-permute-done | bytes 1310752 | tf_op jit(solution)/shard_map/ppermute | solution.py:264
  81.6 0.2 broadcast_select_fusion.1
  81.8 0.1 copy.17
  81.9 0.1 copy.18
  82.0 0.2 pad_maximum_fusion.rows_ref
  82.2 0.0 copy-start.1
  82.2 5.5 %logits.1 = (f32[594,256]{1,0:T(8,128)S(1)}, f32[2,256]{1,0:T(2,128)S(1)}) custom-call(bf16[594,5120]{1,0:T(8,128)(2,1)} %head_hbm.1, bf16[256,5120]{1,0:T(8,128)(2,1)S(1)} %pad_maximum_fusion.rows_ref, s32[1,256]{1,0:T(1,128)S(1)} %bitcast.30), custom_call_target="tpu_custom_call" | custom-call | tf_op jit(solution)/shard_map/logits/pallas_call | solution.py:275
  87.8 11.2 %all_to_all.32 = f32[32,2,256]{2,1,0:T(2,128)S(1)} all-to-all(f32[32,2,256]{2,1,0:T(2,128)S(1)} %broadcast_in_dim.32), channel_id=1, replica_groups=mesh['z'=8,'x'=4,'y'=4,'c'=2] {'x','y','c'}, dimensions={0} | all-to-all | bytes 131072 | tf_op jit(solution)/shard_map/all_to_all | solution.py:191
  99.0 0.1 slice_reduce_fusion.1
  99.2 9.0 %all_to_all.33.stats_ref = f32[8,2,256]{2,1,0:T(2,128)S(1)} all-to-all(f32[8,2,256]{2,1,0:T(2,128)S(1)} %broadcast_in_dim.33), channel_id=1, replica_groups=mesh['z'=8,'x'=4,'y'=4,'c'=2] {'z'}, dimensions={0} | all-to-all | bytes 32768 | tf_op jit(solution)/shard_map/all_to_all | solution.py:191
  108.2 0.0 copy-done.1
  108.2 0.9 final.1
  (9 shorter events, 0.1 us)
Async XLA Ops:
  3.8 20.0 %collective-permute-start = (bf16[176,640]{1,0:T(8,128)(2,1)}, bf16[176,640]{1,0:T(8,128)(2,1)S(1)}, u32[]{:S(2)}, u32[]{:S(2)}) collective-permute-start(bf16[176,640]{1,0:T(8,128)(2,1)} %get-tuple-element.12), channel_id=1, source_target_pairs={{0,8},{8,16},{16,24},{24,0},{1,9},{9,17},{17,25},{25,1},{2,10},{10... | collective-permute-start | bytes 675848 | tf_op jit(solution)/shard_map/ppermute | solution.py:219
  6.0 17.9 %collective-permute-start.1 = (bf16[176,640]{1,0:T(8,128)(2,1)}, bf16[176,640]{1,0:T(8,128)(2,1)S(1)}, u32[]{:S(2)}, u32[]{:S(2)}) collective-permute-start(bf16[176,640]{1,0:T(8,128)(2,1)} %get-tuple-element.13), channel_id=1, source_target_pairs={{0,16},{8,24},{16,0},{24,8},{1,17},{9,25},{17,1},{25,9},{2,18},{10... | collective-permute-start | bytes 675848 | tf_op jit(solution)/shard_map/ppermute | solution.py:219
  8.4 15.5 %collective-permute-start.2 = (bf16[176,640]{1,0:T(8,128)(2,1)}, bf16[176,640]{1,0:T(8,128)(2,1)S(1)}, u32[]{:S(2)}, u32[]{:S(2)}) collective-permute-start(bf16[176,640]{1,0:T(8,128)(2,1)} %get-tuple-element.14), channel_id=1, source_target_pairs={{0,24},{8,0},{16,8},{24,16},{1,25},{9,1},{17,9},{25,17},{2,26},{10... | collective-permute-start | bytes 675848 | tf_op jit(solution)/shard_map/ppermute | solution.py:219
  9.6 21.7 %copy-start.2 = (bf16[640,160]{0,1:T(8,128)(2,1)S(1)}, bf16[640,160]{0,1:T(8,128)(2,1)}, u32[]{:S(2)}) copy-start(bf16[640,160]{0,1:T(8,128)(2,1)} %param.15) | copy-start | bytes 614404
  15.6 15.7 %all-to-all-start = ((bf16[8,8,640]{2,1,0:T(8,128)(2,1)}), bf16[8,8,640]{2,1,0:T(8,128)(2,1)S(1)}, u32[]{:S(2)}, u32[]{:S(2)}) async-start(bf16[8,8,640]{2,1,0:T(8,128)(2,1)} %attend.1), calls=%async_computation | async-start | bytes 163840 | tf_op jit(solution)/shard_map/all_to_all | solution.py:237
  23.9 21.3 %copy-start = (bf16[16,160]{1,0:T(8,128)(2,1)S(1)}, bf16[16,160]{1,0:T(8,128)(2,1)}, u32[]{:S(2)}) copy-start(bf16[16,160]{1,0:T(8,128)(2,1)} %get-tuple-element.15.own_ref) | copy-start | bytes 15364
  32.4 12.8 %all-to-all-start.1 = ((f32[8,8,640]{2,1,0:T(8,128)}), f32[8,8,640]{2,1,0:T(8,128)S(1)}, u32[]{:S(2)}, u32[]{:S(2)}) async-start(f32[8,8,640]{2,1,0:T(8,128)} %fusion), calls=%async_computation.1 | async-start | bytes 327680 | tf_op jit(solution)/shard_map/all_to_all | solution.py:243
  55.7 23.3 %copy-start.3 = (s32[256]{0:T(256)S(1)}, s32[256]{0:T(256)}, u32[]{:S(2)}) copy-start(s32[256]{0:T(256)} %param.18) | copy-start | bytes 3076
  75.6 6.0 %collective-permute-start.3 = (bf16[16,8,5120]{2,1,0:T(8,128)(2,1)S(1)}, bf16[16,8,5120]{2,1,0:T(8,128)(2,1)S(1)}, u32[]{:S(2)}, u32[]{:S(2)}) collective-permute-start(bf16[16,8,5120]{2,1,0:T(8,128)(2,1)S(1)} %all_to_all.31), channel_id=1, source_target_pairs={{0,1},{1,0},{2,3},{3,2},{4,5},{5,4},{6,7},{7,6},{8,9},{9,8},{10,11... | collective-permute-start | bytes 3932168 | tf_op jit(solution)/shard_map/ppermute | solution.py:264
  82.2 26.0 %copy-start.1 = (f32[256]{0:T(256)S(1)}, f32[256]{0:T(256)}, u32[]{:S(2)}) copy-start(f32[256]{0:T(256)} %param.19) | copy-start | bytes 3076

commit v3 on v2

v3 whole, which is shorter than its diff:
```python
import functools
import math

import jax
import jax.numpy as jnp
import numpy as np
from jax import lax
from jax.experimental import pallas as pl
from jax.experimental.pallas import tpu as pltpu
from jax.sharding import Mesh
from jax.sharding import PartitionSpec as P

D = 5120
HEADS = 40
KV_HEADS = 8
HEAD_DIM = 128

masked_score = -1e30
epsilon = 1e-06
learn_rate = 0.1
target_bits = 5.0

bf16 = jnp.bfloat16
f32 = jnp.float32
LANES = 128

IN_VMEM = pl.BlockSpec(memory_space=pltpu.VMEM)
IN_SMEM = pl.BlockSpec(memory_space=pltpu.SMEM)
IN_PLACE = pl.BlockSpec(memory_space=pl.ANY)
SMALL = pltpu.CompilerParams(vmem_limit_bytes=20 << 20)
WIDE = pltpu.CompilerParams(vmem_limit_bytes=44 << 20)
WHOLE = pltpu.CompilerParams(vmem_limit_bytes=60 << 20)
TAIL = 16
CHUNK = 1280


def three_parts(wide):
    first = wide.astype(bf16).astype(f32)
    rest = wide - first
    second = rest.astype(bf16).astype(f32)
    third = (rest - second).astype(bf16).astype(f32)
    return first, second, third


def tails_of(count, part, x, hidden_ref, gain_ref, tail_refs):
    columns, requests = hidden_ref.shape
    row = lax.broadcasted_iota(jnp.int32, (count, requests), 0)
    lane = lax.broadcasted_iota(jnp.int32, (count, requests), 1)
    parts = three_parts(gain_ref[...])
    below = jnp.concatenate(parts + (jnp.zeros((TAIL - count - 3, columns), f32),), axis=0)
    for step, tail_ref in enumerate(tail_refs):
        target = lax.rem(x + step, len(tail_refs))
        place = (part * len(tail_refs) + target) * count
        chosen = jnp.where(lane == row + place, 1.0, 0.0).astype(bf16)
        hidden = lax.dot_general(
            chosen, hidden_ref[...], (((1,), (1,)), ((), ())), preferred_element_type=f32
        )
        tail_ref[...] = jnp.concatenate([hidden, below], axis=0).astype(bf16)


def attend_kernel(group, sizes, lengths_ref, query_ref, new_ref, hidden_ref, gain_ref, cache_ref, *refs):
    out_ref, tail_refs, (slots_ref, rows_ref, sums_ref, sems) = refs[0], refs[1:-4], refs[-4:]
    count, _, slots, head_dim = cache_ref.shape
    z, x, y, c = (lax.axis_index(a) for a in ("z", "x", "y", "c"))
    scale = head_dim ** (-0.5)
    loads = [
        [
            pltpu.make_async_copy(cache_ref.at[r, kind], slots_ref.at[r, kind], sems.at[kind, r])
            for r in range(count)
        ]
        for kind in range(2)
    ]
    for load in loads[0] + loads[1]:
        load.start()
    tails_of(count, c * sizes["y"] + y, x, hidden_ref, gain_ref, tail_refs)

    query = query_ref[...].astype(f32)
    fresh = new_ref[...].astype(f32)
    rows_ref[...] = jnp.zeros_like(rows_ref)
    for g in range(group):
        rows_ref[pl.ds(g, count, stride=8), :] = query[:, g * head_dim : (g + 1) * head_dim]
    heads = rows_ref[...]
    new_keys = jnp.concatenate([jnp.broadcast_to(fresh[r, 0:1], (8, head_dim)) for r in range(count)], axis=0)
    own_score = jnp.sum(heads * new_keys, axis=1, keepdims=True) * scale
    heads = heads.astype(bf16)
    position = lax.broadcasted_iota(jnp.int32, (8, slots), 1)
    base = (z * sizes["x"] + x) * count
    for load in loads[0]:
        load.wait()
    scores = []
    for r in range(count):
        score = lax.dot_general(
            heads[8 * r : 8 * r + 8],
            slots_ref[r, 0],
            (((1,), (1,)), ((), ())),
            preferred_element_type=f32,
        )
        scores.append(jnp.where(position < lengths_ref[base + r], score * scale, masked_score))
    scores = jnp.concatenate(scores, axis=0)
    top = jnp.maximum(jnp.max(scores, axis=1, keepdims=True), own_score)
    weights = jnp.exp(scores - top)
    own_weight = jnp.exp(own_score - top)
    mass = jnp.sum(weights, axis=1, keepdims=True) + own_weight
    parts = three_parts(weights)
    for load in loads[1]:
        load.wait()
    for r in range(count):
        span = slice(8 * r, 8 * r + 8)
        stacked = jnp.concatenate([part[span] for part in parts], axis=0).astype(bf16)
        sums = jnp.dot(stacked, slots_ref[r, 1], preferred_element_type=f32)
        total = sums[:8] + sums[8:16] + sums[16:24] + own_weight[span] * fresh[r, 1:2]
        sums_ref[span] = total / mass[span]
    done = jnp.concatenate([sums_ref[pl.ds(g, count, stride=8), :] for g in range(group)], axis=1).astype(bf16)
    for k in range(out_ref.shape[0]):
        out_ref[k] = done


def resid_kernel(partial_ref, *refs):
    tails, out_ref = refs[:-1], refs[-1]
    count, width = partial_ref.shape[1:]
    columns = width // len(tails)
    total = partial_ref[0]
    for k in range(1, partial_ref.shape[0]):
        total = total + partial_ref[k]
    squares = jnp.zeros((count, 1), f32)
    blocks = []
    for step, tail_ref in enumerate(tails):
        tail = tail_ref[...].astype(f32)
        gain = tail[count : count + 1] + tail[count + 1 : count + 2] + tail[count + 2 : count + 3]
        resid = total[:, step * columns : (step + 1) * columns] + tail[:count]
        resid = resid.astype(bf16).astype(f32)
        squares = squares + jnp.sum(resid * resid, axis=1, keepdims=True)
        blocks.append(resid * gain)
    shift = lax.rem(lax.axis_index("x") + 1, len(tails)) * columns
    ordered = pltpu.roll(jnp.concatenate(blocks[::-1], axis=1), shift, 1)
    lane = lax.broadcasted_iota(jnp.int32, (count, LANES), 1)
    spare = jnp.zeros((count, LANES), f32)
    for k, part in enumerate(three_parts(squares)):
        spare = jnp.where(lane == k, part, spare)
    done = jnp.concatenate([ordered, spare], axis=1).astype(bf16)
    for k in range(out_ref.shape[0]):
        out_ref[k] = done


def norm_kernel(rows_ref, out_ref):
    blocks, count, padded = rows_ref.shape
    width = padded - LANES
    squares = jnp.zeros((count, LANES), f32)
    for k in range(blocks):
        squares = squares + rows_ref[k, :, width:].astype(f32)
    factor = lax.rsqrt(jnp.sum(squares, axis=1, keepdims=True) / D + epsilon)
    for k in range(blocks):
        done = (rows_ref[k, :, :width].astype(f32) * factor).astype(bf16)
        for copy in range(out_ref.shape[0]):
            out_ref[copy, :, k * width : (k + 1) * width] = done


def fetch_kernel(head_hbm, after_ref, head_ref, sem):
    load = pltpu.make_async_copy(head_hbm, head_ref, sem)
    load.start()
    load.wait()


def logits_kernel(head_ref, rows_ref, ids_ref, logits_ref, stats_ref):
    depth = head_ref.shape[1]
    for k in range(depth // CHUNK):
        span = slice(k * CHUNK, (k + 1) * CHUNK)
        product = lax.dot_general(
            head_ref[:, span], rows_ref[:, span], (((1,), (1,)), ((), ())), preferred_element_type=f32
        )
        if k == 0:
            logits_ref[...] = product
        else:
            logits_ref[...] += product
    logits = logits_ref[...]
    top = jnp.max(logits, axis=0, keepdims=True)
    log_mass = top + jnp.log(jnp.sum(jnp.exp(logits - top), axis=0, keepdims=True))
    hits = lax.broadcasted_iota(jnp.int32, logits.shape, 0) == ids_ref[...]
    picked = jnp.sum(jnp.where(hits, logits, 0.0), axis=0, keepdims=True)
    stats_ref[...] = jnp.concatenate([log_mass, picked], axis=0)


def final_kernel(logits_ref, stats_ref, mu_ref, logprobs_ref, surprise_ref, mu_next_ref):
    masses = stats_ref[:, 0]
    top = jnp.max(masses, axis=0, keepdims=True)
    log_mass = top + jnp.log(jnp.sum(jnp.exp(masses - top), axis=0, keepdims=True))
    picked = jnp.sum(stats_ref[:, 1], axis=0, keepdims=True)
    logprobs_ref[...] = logits_ref[...] - log_mass
    surprise = (log_mass - picked) / math.log(2.0)
    surprise_ref[...] = surprise
    mu_next_ref[...] = mu_ref[...] - learn_rate * (surprise - target_bits)


def spread(block, axes, count):
    many = jnp.broadcast_to(block[None], (count,) + block.shape)
    return lax.all_to_all(many, axes, split_axis=0, concat_axis=0, tiled=False)


def shards(query, cache, new_kv, lengths, hidden_in, out_proj, final_gain, lm_head, tokens, mu):
    nz, nx, ny, nc = (lax.axis_size(a) for a in ("z", "x", "y", "c"))
    z, x, y, c = (lax.axis_index(a) for a in ("z", "x", "y", "c"))
    count = query.shape[0]
    heads, columns = out_proj.shape
    sizes = {"z": nz, "x": nx, "y": ny, "c": nc}

    def from_along_x(block, step):
        return lax.ppermute(block, "x", [(i, (i + step) % nx) for i in range(nx)])

    table = jnp.concatenate([out_proj.T] + [from_along_x(out_proj.T, k) for k in range(1, nx)], axis=0)
    many, *tails = pl.pallas_call(
        functools.partial(attend_kernel, HEADS // KV_HEADS, sizes),
        out_shape=[jax.ShapeDtypeStruct((nz,) + query.shape, bf16)]
        + [jax.ShapeDtypeStruct((TAIL, columns), bf16)] * nx,
        in_specs=[IN_SMEM] + [IN_VMEM] * 4 + [IN_PLACE],
        out_specs=[IN_VMEM] * (nx + 1),
        scratch_shapes=[
            pltpu.VMEM(cache.shape, bf16),
            pltpu.VMEM((count * 8, HEAD_DIM), f32),
            pltpu.VMEM((count * 8, HEAD_DIM), f32),
            pltpu.SemaphoreType.DMA((2, count)),
        ],
        compiler_params=WHOLE,
        name="attend",
    )(lengths, query, new_kv, hidden_in.T, final_gain[None], cache)
    tails = [tails[0]] + [from_along_x(tails[k], k) for k in range(1, nx)]
    gathered = lax.all_to_all(many, "z", split_axis=0, concat_axis=0, tiled=False)
    gathered = gathered.reshape(nz * count, -1)
    partial = lax.dot_general(
        gathered, table, (((1,), (1,)), ((), ())), preferred_element_type=f32
    )
    partial = partial.reshape(nz, count, nx * columns)
    partial = lax.all_to_all(partial, ("c", "y"), split_axis=0, concat_axis=0, tiled=False)

    width = nx * columns
    rows = pl.pallas_call(
        resid_kernel,
        out_shape=jax.ShapeDtypeStruct((nz, count, width + LANES), bf16),
        in_specs=[IN_VMEM] * (nx + 1),
        out_specs=IN_VMEM,
        compiler_params=SMALL,
        name="resid",
    )(partial, *tails)
    rows = lax.all_to_all(rows, "z", split_axis=0, concat_axis=0, tiled=False)
    half = pl.pallas_call(
        norm_kernel,
        out_shape=jax.ShapeDtypeStruct((nx * ny, count, nz * width), bf16),
        in_specs=[IN_VMEM],
        out_specs=IN_VMEM,
        compiler_params=SMALL,
        name="norm",
    )(rows)
    half = lax.all_to_all(half, ("x", "y"), split_axis=0, concat_axis=0, tiled=False)
    other = lax.ppermute(half, "c", [(i, 1 - i) for i in range(2)])
    head = pl.pallas_call(
        fetch_kernel,
        out_shape=jax.ShapeDtypeStruct(lm_head.shape, bf16),
        in_specs=[IN_PLACE] * 2,
        out_specs=IN_VMEM,
        scratch_shapes=[pltpu.SemaphoreType.DMA],
        compiler_params=WIDE,
        name="fetch",
    )(lm_head, half)
    other, head = lax.optimization_barrier((other, head))
    half, other = (
        jnp.swapaxes(h.reshape(nx, ny, count, -1), 0, 1).reshape(nx * ny * count, -1) for h in (half, other)
    )
    first = jnp.where(c == 0, half, other)
    second = jnp.where(c == 0, other, half)
    everyone = jnp.concatenate([first, second], axis=0)

    vocab = lm_head.shape[0]
    requests = everyone.shape[0]
    offset = (((z * nx + x) * ny + y) * nc + c) * vocab
    logits, stats = pl.pallas_call(
        logits_kernel,
        out_shape=[jax.ShapeDtypeStruct((vocab, requests), f32), jax.ShapeDtypeStruct((2, requests), f32)],
        in_specs=[IN_VMEM] * 3,
        out_specs=[IN_VMEM] * 2,
        compiler_params=SMALL,
        name="logits",
    )(head, everyone, (tokens - offset)[None])

    stats = spread(stats, ("x", "y", "c"), nx * ny * nc)
    top = jnp.max(stats[:, 0], axis=0)
    log_mass = top + jnp.log(jnp.sum(jnp.exp(stats[:, 0] - top[None, :]), axis=0))
    picked = jnp.sum(stats[:, 1], axis=0)
    stats = spread(jnp.stack([log_mass, picked]), "z", nz)
    row_shape = jax.ShapeDtypeStruct((1, requests), f32)
    logprobs, surprise, mu_next = pl.pallas_call(
        final_kernel,
        out_shape=[jax.ShapeDtypeStruct((vocab, requests), f32), row_shape, row_shape],
        in_specs=[IN_VMEM] * 3,
        out_specs=[IN_VMEM] * 3,
        compiler_params=SMALL,
        name="final",
    )(logits, stats, mu[None])
    return (logprobs.T, surprise[0], mu_next[0])


def solution(mesh):
    grid = Mesh(np.asarray(mesh.devices).reshape(8, 4, 4, 2), ("z", "x", "y", "c"))
    dp, tensor = ("z", "x"), ("y", "c")
    placed = (
        P(dp, tensor),
        P(dp, None, None, tensor),
        P(dp, None, tensor),
        P(),
        P(None, dp),
        P(tensor, dp),
        P(dp),
        P(dp + tensor, None),
        P(),
        P(),
    )
    return jax.shard_map(
        shards,
        mesh=grid,
        in_specs=placed,
        out_specs=(P(None, dp + tensor), P(), P()),
        check_vma=False,
    )
```

time: 110 us -> 104 us (0.945)
  blocking collectives: 50.2 us -> 67.9 us
  waiting for transfers between devices: 15.6 us -> 2.05 us
  Pallas kernels: 15.6 us -> 10.7 us
  starting transfers between devices: 24.6 us -> 20.2 us
    all_to_all x0 -> x1, blocking collectives: none -> 15.7 us  [shards(): lax.all_to_all(many, 'z', split_axis=0, concat_axis=0, tiled=False)]
    all_to_all x1 -> x0, starting transfers between devices: 8.2 us -> none  [shards(): lax.all_to_all(many, 'z', split_axis=0, concat_axis=0, tiled=False)]
    all_to_all x1 -> x0, waiting for transfers between devices: 7.39 us -> none  [shards(): lax.all_to_all(many, 'z', split_axis=0, concat_axis=0, tiled=False)]
    all_to_all x1, waiting for transfers between devices: 5.51 us -> 0.01 us  [shards(): lax.all_to_all(partial, ('c', 'y'), split_axis=0, concat_axis=0, tiled=Fa...]
    pallas_call x1, Pallas kernels: 5.55 us -> 2 us  [shards(): pl.pallas_call(logits_kernel, out_shape=[jax.ShapeDtypeStruct((vocab, req...]
    ppermute x3 -> x6, starting transfers between devices: 5.72 us -> 8.54 us  [from_along_x(): return lax.ppermute(block, 'x', [(i, (i + step) % nx) for i in range(nx)])]
    ppermute x1, waiting for transfers between devices: 2.66 us -> 0.01 us  [shards(): other = lax.ppermute(half, 'c', [(i, 1 - i) for i in range(2)])]
    all_to_all x1, blocking collectives: 19.9 us -> 22.1 us  [shards(): lax.all_to_all(half, ('x', 'y'), split_axis=0, concat_axis=0, tiled=False)]
  transfers between devices with their start and end apart: 6 -> 8, of which waited for: 3 -> 2; matrix products, arithmetic and copies ran while one was open for 0% -> 0% of each run, Pallas kernels for 6% -> 7%
where the time goes in v3:
time: 104 us; the launch traced here: 103 us
  blocking collectives  67.9 us (65%)
  starting transfers between devices  20.2 us (19%)
  Pallas kernels  10.7 us (10%)
  waiting for transfers between devices  2.05 us (2%)
  matrix products  1.06 us (1%)
    all_to_all x1, blocking collectives, shards(): lax.all_to_all(half, ('x', 'y'), split_axis=0, concat_axis=0, tiled=False)  22.1 us
    all_to_all x2, blocking collectives, spread(): return lax.all_to_all(many, axes, split_axis=0, concat_axis=0, tiled=False)  20.1 us
    all_to_all x1, blocking collectives, shards(): lax.all_to_all(many, 'z', split_axis=0, concat_axis=0, tiled=False)  15.7 us
    all_to_all x1, blocking collectives, shards(): rows = lax.all_to_all(rows, 'z', split_axis=0, concat_axis=0, tiled=False)  9.95 us
    ppermute x6, starting transfers between devices, from_along_x(): return lax.ppermute(block, 'x', [(i, (i + step) % nx) for i in range(nx)])  8.54 us
    all_to_all x1, starting transfers between devices, shards(): lax.all_to_all(partial, ('c', 'y'), split_axis=0, concat_axis=0, tiled=Fa...  7.31 us
    pallas_call x1, Pallas kernels, shards(): pl.pallas_call(functools.partial(attend_kernel, HEADS // KV_HEADS, sizes)...  4.55 us
    ppermute x1, starting transfers between devices, shards(): other = lax.ppermute(half, 'c', [(i, 1 - i) for i in range(2)])  4.31 us
  transfers between devices with their start and end apart: 8, of which 2 were waited for; matrix products, arithmetic and copies ran while one was open for 0% of the time, Pallas kernels for 7%

profile of v3, /device:TPU:1, one launch (start us, length us, event | category | flops | bytes accessed | tf_op | source)
XLA Modules:
  0.0 103.3 jit_solution(3876091127451275385)
XLA Ops:
  0.6 3.4 %collective-permute-start.2 = (bf16[160,640]{1,0:T(8,128)(2,1)}, bf16[160,640]{1,0:T(8,128)(2,1)S(1)}, u32[]{:S(2)}, u32[]{:S(2)}) collective-permute-start(bf16[160,640]{1,0:T(8,128)(2,1)} %bitcast.39), channel_id=1, source_target_pairs={{0,24},{8,0},{16,8},{24,16},{1,25},{9,1},{17,9},{25,17},{2,26},{10... | collective-permute-start | bytes 614408 | tf_op jit(solution)/shard_map/ppermute | solution.py:207
  4.0 0.5 collective-permute-start.1
  4.5 0.6 collective-permute-start
  5.1 0.0 copy-start.3
  5.1 4.5 %attend.1 = (bf16[8,8,640]{2,1,0:T(8,128)(2,1)}, bf16[16,160]{1,0:T(8,128)(2,1)}, bf16[16,160]{1,0:T(8,128)(2,1)}, bf16[16,160]{1,0:T(8,128)(2,1)}, bf16[16,160]{1,0:T(8,128)(2,1)}) custom-call(s32[256]{0:T(256)} %lengths_ref.1, bf16[8,640]{1,0:T(8,128)(2,1)} %query_ref.1, bf16[8,2,128]{2,1,0:T(2,128)(2,1)} %new_ref.1, bf16[160,256]{1,0:T(8,128)(2,1)} %bitcast.34, ...), custom_call_target="tpu_custom_call" | custom-call | tf_op jit(solution)/shard_map/attend/pallas_call | solution.py:210
  9.7 15.7 %all_to_all.30 = bf16[8,8,640]{2,1,0:T(8,128)(2,1)S(1)} all-to-all(bf16[8,8,640]{2,1,0:T(8,128)(2,1)} %get-tuple-element.15), channel_id=1, replica_groups=mesh['z'=8,'x'=4,'y'=4,'c'=2] {'z'}, dimensions={0} | all-to-all | bytes 163840 | tf_op jit(solution)/shard_map/all_to_all | solution.py:226
  25.4 0.0 copy-start.6
  25.4 0.0 copy-start.5
  25.4 0.0 copy-start.4
  25.4 0.0 copy-start
  25.4 0.0 collective-permute-done.2
  25.4 0.0 collective-permute-done.1
  25.4 0.0 collective-permute-done
  25.4 0.0 copy-done.3
  25.5 1.1 %fusion = f32[8,8,640]{2,1,0:T(8,128)} fusion(bf16[8,8,640]{2,1,0:T(8,128)(2,1)S(1)} %all_to_all.30, bf16[160,640]{1,0:T(8,128)(2,1)S(1)} %collective-permute-done.2, bf16[160,640]{1,0:T(8,128)(2,1)S(1)} %collective-permute-done.1, bf16[160,640]{1,0:T(8,128)(2,1)S(1)} %collective-permute-done, bf16[160,640]{1,0:T(8,128)(2,1)S(1)} %bitcast.42), kind=kOutput, calls=%fused_computation.4 | convolution fusion | flops 55705600 | bytes 1064960 | tf_op jit(solution)/shard_map/dot_general | solution.py:228
  26.5 7.3 %all-to-all-start.1 = ((f32[8,8,640]{2,1,0:T(8,128)}), f32[8,8,640]{2,1,0:T(8,128)S(1)}, u32[]{:S(2)}, u32[]{:S(2)}) async-start(f32[8,8,640]{2,1,0:T(8,128)} %fusion), calls=%async_computation.1 | async-start | bytes 327680 | tf_op jit(solution)/shard_map/all_to_all | solution.py:232
  33.8 0.0 copy-done.6
  33.8 1.5 %collective-permute-start.3 = (bf16[16,160]{1,0:T(8,128)(2,1)S(1)}, bf16[16,160]{1,0:T(8,128)(2,1)S(1)}, u32[]{:S(2)}, u32[]{:S(2)}) collective-permute-start(bf16[16,160]{1,0:T(8,128)(2,1)S(1)} %copy-done.6), channel_id=1, source_target_pairs={{0,8},{8,16},{16,24},{24,0},{1,9},{9,17},{17,25},{25,1},{2,10},{10... | collective-permute-start | bytes 15368 | tf_op jit(solution)/shard_map/ppermute | solution.py:207
  35.4 0.0 copy-done.5
  35.4 1.7 %collective-permute-start.4 = (bf16[16,160]{1,0:T(8,128)(2,1)S(1)}, bf16[16,160]{1,0:T(8,128)(2,1)S(1)}, u32[]{:S(2)}, u32[]{:S(2)}) collective-permute-start(bf16[16,160]{1,0:T(8,128)(2,1)S(1)} %copy-done.5), channel_id=1, source_target_pairs={{0,16},{8,24},{16,0},{24,8},{1,17},{9,25},{17,1},{25,9},{2,18},{10... | collective-permute-start | bytes 15368 | tf_op jit(solution)/shard_map/ppermute | solution.py:207
  37.1 0.0 copy-done.4
  37.1 0.8 collective-permute-start.5
  37.9 0.0 collective-permute-done.3.refs_1_
  37.9 1.5 %collective-permute-done.4.refs_2_ = bf16[16,160]{1,0:T(8,128)(2,1)S(1)} collective-permute-done((bf16[16,160]{1,0:T(8,128)(2,1)S(1)}, bf16[16,160]{1,0:T(8,128)(2,1)S(1)}, u32[]{:S(2)}, u32[]{:S(2)}) %collective-permute-start.4) | collective-permute-done | bytes 5152 | tf_op jit(solution)/shard_map/ppermute | solution.py:207
  39.4 0.5 collective-permute-done.5.refs_3_
  39.9 0.0 all-to-all-done.1.partial_ref
  39.9 0.0 copy-done
  39.9 0.2 resid.1
  40.1 10.0 %all_to_all.31.rows_ref = bf16[8,8,768]{2,1,0:T(8,128)(2,1)S(1)} all-to-all(bf16[8,8,768]{2,1,0:T(8,128)(2,1)S(1)} %resid.1), channel_id=1, replica_groups=mesh['z'=8,'x'=4,'y'=4,'c'=2] {'z'}, dimensions={0} | all-to-all | bytes 196608 | tf_op jit(solution)/shard_map/all_to_all | solution.py:243
  50.1 0.2 norm.1
  50.3 0.0 copy-start.2
  50.3 22.1 %all_to_all.32.after_ref = bf16[16,8,5120]{2,1,0:T(8,128)(2,1)S(1)} all-to-all(bf16[16,8,5120]{2,1,0:T(8,128)(2,1)S(1)} %norm.1), channel_id=1, replica_groups=mesh['z'=8,'x'=4,'y'=4,'c'=2] {'x','y'}, dimensions={0} | all-to-all | bytes 2621440 | tf_op jit(solution)/shard_map/all_to_all | solution.py:252
  72.5 4.3 %collective-permute-start.6 = (bf16[16,8,5120]{2,1,0:T(8,128)(2,1)S(1)}, bf16[16,8,5120]{2,1,0:T(8,128)(2,1)S(1)}, u32[]{:S(2)}, u32[]{:S(2)}) collective-permute-start(bf16[16,8,5120]{2,1,0:T(8,128)(2,1)S(1)} %all_to_all.32.after_ref), channel_id=1, source_target_pairs={{0,1},{1,0},{2,3},{3,2},{4,5},{5,4},{6,7},{7,6},{8,9},{9,8},{10,11... | collective-permute-start | bytes 3932168 | tf_op jit(solution)/shard_map/ppermute | solution.py:253
  76.8 0.0 copy-done.2
  76.8 2.8 %fetch.1.head_ref = bf16[594,5120]{1,0:T(8,128)(2,1)S(1)} custom-call(bf16[594,5120]{1,0:T(8,128)(2,1)} %head_hbm.1, bf16[16,8,5120]{2,1,0:T(8,128)(2,1)S(1)} %all_to_all.32.after_ref), custom_call_target="tpu_custom_call" | custom-call | tf_op jit(solution)/shard_map/fetch/pallas_call | solution.py:254
  79.6 0.0 collective-permute-done.6
  79.6 0.2 broadcast_select_fusion.1
  79.7 0.1 copy.17
  79.8 0.1 copy.18
  79.9 0.2 pad_maximum_fusion.rows_ref
  80.1 0.0 copy-start.1
  80.1 2.0 %logits.1 = (f32[594,256]{1,0:T(8,128)S(1)}, f32[2,256]{1,0:T(2,128)S(1)}) custom-call(bf16[594,5120]{1,0:T(8,128)(2,1)S(1)} %fetch.1.head_ref, bf16[256,5120]{1,0:T(8,128)(2,1)S(1)} %pad_maximum_fusion.rows_ref, s32[1,256]{1,0:T(1,128)S(1)} %bitcast.28), custom_call_target="tpu_custom_call" | custom-call | tf_op jit(solution)/shard_map/logits/pallas_call | solution.py:274
  82.2 11.1 %all_to_all.33 = f32[32,2,256]{2,1,0:T(2,128)S(1)} all-to-all(f32[32,2,256]{2,1,0:T(2,128)S(1)} %broadcast_in_dim.24), channel_id=1, replica_groups=mesh['z'=8,'x'=4,'y'=4,'c'=2] {'x','y','c'}, dimensions={0} | all-to-all | bytes 131072 | tf_op jit(solution)/shard_map/all_to_all | solution.py:196
  93.3 0.1 slice_reduce_fusion.1
  93.4 9.0 %all_to_all.34.stats_ref = f32[8,2,256]{2,1,0:T(2,128)S(1)} all-to-all(f32[8,2,256]{2,1,0:T(2,128)S(1)} %broadcast_in_dim.25), channel_id=1, replica_groups=mesh['z'=8,'x'=4,'y'=4,'c'=2] {'z'}, dimensions={0} | all-to-all | bytes 32768 | tf_op jit(solution)/shard_map/all_to_all | solution.py:196
  102.4 0.0 copy-done.1
  102.4 0.9 final.1
  (6 shorter events, 0.1 us)
Async XLA Ops:
  0.6 24.8 %collective-permute-start.2 = (bf16[160,640]{1,0:T(8,128)(2,1)}, bf16[160,640]{1,0:T(8,128)(2,1)S(1)}, u32[]{:S(2)}, u32[]{:S(2)}) collective-permute-start(bf16[160,640]{1,0:T(8,128)(2,1)} %bitcast.39), channel_id=1, source_target_pairs={{0,24},{8,0},{16,8},{24,16},{1,25},{9,1},{17,9},{25,17},{2,26},{10... | collective-permute-start | bytes 614408 | tf_op jit(solution)/shard_map/ppermute | solution.py:207
  4.0 21.4 %collective-permute-start.1 = (bf16[160,640]{1,0:T(8,128)(2,1)}, bf16[160,640]{1,0:T(8,128)(2,1)S(1)}, u32[]{:S(2)}, u32[]{:S(2)}) collective-permute-start(bf16[160,640]{1,0:T(8,128)(2,1)} %bitcast.40), channel_id=1, source_target_pairs={{0,16},{8,24},{16,0},{24,8},{1,17},{9,25},{17,1},{25,9},{2,18},{10... | collective-permute-start | bytes 614408 | tf_op jit(solution)/shard_map/ppermute | solution.py:207
  4.5 20.9 %collective-permute-start = (bf16[160,640]{1,0:T(8,128)(2,1)}, bf16[160,640]{1,0:T(8,128)(2,1)S(1)}, u32[]{:S(2)}, u32[]{:S(2)}) collective-permute-start(bf16[160,640]{1,0:T(8,128)(2,1)} %bitcast.41), channel_id=1, source_target_pairs={{0,8},{8,16},{16,24},{24,0},{1,9},{9,17},{17,25},{25,1},{2,10},{10... | collective-permute-start | bytes 614408 | tf_op jit(solution)/shard_map/ppermute | solution.py:207
  5.1 20.3 %copy-start.3 = (bf16[640,160]{0,1:T(8,128)(2,1)S(1)}, bf16[640,160]{0,1:T(8,128)(2,1)}, u32[]{:S(2)}) copy-start(bf16[640,160]{0,1:T(8,128)(2,1)} %param.15) | copy-start | bytes 614404
  25.4 8.4 %copy-start.6 = (bf16[16,160]{1,0:T(8,128)(2,1)S(1)}, bf16[16,160]{1,0:T(8,128)(2,1)}, u32[]{:S(2)}) copy-start(bf16[16,160]{1,0:T(8,128)(2,1)} %get-tuple-element.17) | copy-start | bytes 15364
  25.4 10.0 %copy-start.5 = (bf16[16,160]{1,0:T(8,128)(2,1)S(1)}, bf16[16,160]{1,0:T(8,128)(2,1)}, u32[]{:S(2)}) copy-start(bf16[16,160]{1,0:T(8,128)(2,1)} %get-tuple-element.18) | copy-start | bytes 15364
  25.4 11.7 %copy-start.4 = (bf16[16,160]{1,0:T(8,128)(2,1)S(1)}, bf16[16,160]{1,0:T(8,128)(2,1)}, u32[]{:S(2)}) copy-start(bf16[16,160]{1,0:T(8,128)(2,1)} %get-tuple-element.19) | copy-start | bytes 15364
  25.4 14.5 %copy-start = (bf16[16,160]{1,0:T(8,128)(2,1)S(1)}, bf16[16,160]{1,0:T(8,128)(2,1)}, u32[]{:S(2)}) copy-start(bf16[16,160]{1,0:T(8,128)(2,1)} %get-tuple-element.16.refs_0_) | copy-start | bytes 15364
  26.5 13.4 %all-to-all-start.1 = ((f32[8,8,640]{2,1,0:T(8,128)}), f32[8,8,640]{2,1,0:T(8,128)S(1)}, u32[]{:S(2)}, u32[]{:S(2)}) async-start(f32[8,8,640]{2,1,0:T(8,128)} %fusion), calls=%async_computation.1 | async-start | bytes 327680 | tf_op jit(solution)/shard_map/all_to_all | solution.py:232
  33.8 4.0 %collective-permute-start.3 = (bf16[16,160]{1,0:T(8,128)(2,1)S(1)}, bf16[16,160]{1,0:T(8,128)(2,1)S(1)}, u32[]{:S(2)}, u32[]{:S(2)}) collective-permute-start(bf16[16,160]{1,0:T(8,128)(2,1)S(1)} %copy-done.6), channel_id=1, source_target_pairs={{0,8},{8,16},{16,24},{24,0},{1,9},{9,17},{17,25},{25,1},{2,10},{10... | collective-permute-start | bytes 15368 | tf_op jit(solution)/shard_map/ppermute | solution.py:207
  35.4 4.0 %collective-permute-start.4 = (bf16[16,160]{1,0:T(8,128)(2,1)S(1)}, bf16[16,160]{1,0:T(8,128)(2,1)S(1)}, u32[]{:S(2)}, u32[]{:S(2)}) collective-permute-start(bf16[16,160]{1,0:T(8,128)(2,1)S(1)} %copy-done.5), channel_id=1, source_target_pairs={{0,16},{8,24},{16,0},{24,8},{1,17},{9,25},{17,1},{25,9},{2,18},{10... | collective-permute-start | bytes 15368 | tf_op jit(solution)/shard_map/ppermute | solution.py:207
  37.1 2.8 %collective-permute-start.5 = (bf16[16,160]{1,0:T(8,128)(2,1)S(1)}, bf16[16,160]{1,0:T(8,128)(2,1)S(1)}, u32[]{:S(2)}, u32[]{:S(2)}) collective-permute-start(bf16[16,160]{1,0:T(8,128)(2,1)S(1)} %copy-done.4), channel_id=1, source_target_pairs={{0,24},{8,0},{16,8},{24,16},{1,25},{9,1},{17,9},{25,17},{2,26},{10... | collective-permute-start | bytes 15368 | tf_op jit(solution)/shard_map/ppermute | solution.py:207
  50.3 26.5 %copy-start.2 = (s32[256]{0:T(256)S(1)}, s32[256]{0:T(256)}, u32[]{:S(2)}) copy-start(s32[256]{0:T(256)} %param.18) | copy-start | bytes 3076
  72.5 7.1 %collective-permute-start.6 = (bf16[16,8,5120]{2,1,0:T(8,128)(2,1)S(1)}, bf16[16,8,5120]{2,1,0:T(8,128)(2,1)S(1)}, u32[]{:S(2)}, u32[]{:S(2)}) collective-permute-start(bf16[16,8,5120]{2,1,0:T(8,128)(2,1)S(1)} %all_to_all.32.after_ref), channel_id=1, source_target_pairs={{0,1},{1,0},{2,3},{3,2},{4,5},{5,4},{6,7},{7,6},{8,9},{9,8},{10,11... | collective-permute-start | bytes 3932168 | tf_op jit(solution)/shard_map/ppermute | solution.py:253
  80.1 22.3 %copy-start.1 = (f32[256]{0:T(256)S(1)}, f32[256]{0:T(256)}, u32[]{:S(2)}) copy-start(f32[256]{0:T(256)} %param.19) | copy-start | bytes 3076

commit v4 on v3

--- a/solution.py
+++ b/solution.py
@@ -70,7 +70,7 @@
         ]
         for kind in range(2)
     ]
-    for load in loads[0] + loads[1]:
+    for load in loads[0]:
         load.start()
     tails_of(count, c * sizes["y"] + y, x, hidden_ref, gain_ref, tail_refs)
 
@@ -87,6 +87,8 @@
     base = (z * sizes["x"] + x) * count
     for load in loads[0]:
         load.wait()
+    for load in loads[1]:
+        load.start()
     scores = []
     for r in range(count):
         score = lax.dot_general(
@@ -224,6 +226,7 @@
     )(lengths, query, new_kv, hidden_in.T, final_gain[None], cache)
     tails = [tails[0]] + [from_along_x(tails[k], k) for k in range(1, nx)]
     gathered = lax.all_to_all(many, "z", split_axis=0, concat_axis=0, tiled=False)
+    gathered, tails = lax.optimization_barrier((gathered, tails))
     gathered = gathered.reshape(nz * count, -1)
     partial = lax.dot_general(
         gathered, table, (((1,), (1,)), ((), ())), preferred_element_type=f32
@@ -249,7 +252,8 @@
         compiler_params=SMALL,
         name="norm",
     )(rows)
-    half = lax.all_to_all(half, ("x", "y"), split_axis=0, concat_axis=0, tiled=False)
+    half = lax.all_to_all(half, ("y", "x"), split_axis=0, concat_axis=0, tiled=False)
+    half = half.reshape(ny * nx * count, -1)
     other = lax.ppermute(half, "c", [(i, 1 - i) for i in range(2)])
     head = pl.pallas_call(
         fetch_kernel,
@@ -261,9 +265,6 @@
         name="fetch",
     )(lm_head, half)
     other, head = lax.optimization_barrier((other, head))
-    half, other = (
-        jnp.swapaxes(h.reshape(nx, ny, count, -1), 0, 1).reshape(nx * ny * count, -1) for h in (half, other)
-    )
     first = jnp.where(c == 0, half, other)
     second = jnp.where(c == 0, other, half)
     everyone = jnp.concatenate([first, second], axis=0)

time: 104 us -> 106 us (1.019)
  waiting for transfers between devices: 2.05 us -> 3.32 us
    all_to_all x1, blocking collectives: 9.95 us -> 14.1 us  [shards(): rows = lax.all_to_all(rows, 'z', split_axis=0, concat_axis=0, tiled=False)]
    all_to_all x2, blocking collectives: 37.8 us -> 34.9 us  [the longest x1 21.8 us: shards(): lax.all_to_all(half, ('y', 'x'), split_axis=0, concat_axis=0, tiled=False)]
  transfers between devices with their start and end apart: 8 -> 8, of which waited for: 2 -> 4; matrix products, arithmetic and copies ran while one was open for 0% -> 0% of each run, Pallas kernels for 7% -> 8%
where the time goes in v4:
time: 106 us; the launch traced here: 105 us
  blocking collectives  68.6 us (65%)
  starting transfers between devices  20.3 us (19%)
  Pallas kernels  11.3 us (11%)
  waiting for transfers between devices  3.32 us (3%)
    all_to_all x1, blocking collectives, shards(): lax.all_to_all(half, ('y', 'x'), split_axis=0, concat_axis=0, tiled=False)  21.8 us
    all_to_all x2, blocking collectives, spread(): return lax.all_to_all(many, axes, split_axis=0, concat_axis=0, tiled=False)  19.7 us
    all_to_all x1, blocking collectives, shards(): rows = lax.all_to_all(rows, 'z', split_axis=0, concat_axis=0, tiled=False)  14.1 us
    all_to_all x1, blocking collectives, shards(): lax.all_to_all(partial, ('c', 'y'), split_axis=0, concat_axis=0, tiled=Fa...  13.1 us
    ppermute x6, starting transfers between devices, from_along_x(): return lax.ppermute(block, 'x', [(i, (i + step) % nx) for i in range(nx)])  8.7 us
    all_to_all x1, starting transfers between devices, shards(): lax.all_to_all(many, 'z', split_axis=0, concat_axis=0, tiled=False)  8.2 us
    pallas_call x1, Pallas kernels, shards(): pl.pallas_call(functools.partial(attend_kernel, HEADS // KV_HEADS, sizes)...  5.2 us
    ppermute x1, starting transfers between devices, shards(): other = lax.ppermute(half, 'c', [(i, 1 - i) for i in range(2)])  3.4 us
  transfers between devices with their start and end apart: 8, of which 4 were waited for; matrix products, arithmetic and copies ran while one was open for 0% of the time, Pallas kernels for 8%

profile of v4, /device:TPU:1, one launch (start us, length us, event | category | flops | bytes accessed | tf_op | source)
XLA Modules:
  0.0 105.2 jit_solution(12400343568907548802)
XLA Ops:
  0.6 3.4 %collective-permute-start.5 = (bf16[160,640]{1,0:T(8,128)(2,1)}, bf16[160,640]{1,0:T(8,128)(2,1)S(1)}, u32[]{:S(2)}, u32[]{:S(2)}) collective-permute-start(bf16[160,640]{1,0:T(8,128)(2,1)} %bitcast.32), channel_id=1, source_target_pairs={{0,24},{8,0},{16,8},{24,16},{1,25},{9,1},{17,9},{25,17},{2,26},{10... | collective-permute-start | bytes 614408 | tf_op jit(solution)/shard_map/ppermute | solution.py:209
  4.0 0.5 collective-permute-start.4
  4.5 0.6 collective-permute-start.3
  5.1 0.0 copy-start.3
  5.1 5.2 %attend.1 = (bf16[8,8,640]{2,1,0:T(8,128)(2,1)}, bf16[16,160]{1,0:T(8,128)(2,1)}, bf16[16,160]{1,0:T(8,128)(2,1)}, bf16[16,160]{1,0:T(8,128)(2,1)}, bf16[16,160]{1,0:T(8,128)(2,1)}) custom-call(s32[256]{0:T(256)} %lengths_ref.1, bf16[8,640]{1,0:T(8,128)(2,1)} %query_ref.1, bf16[8,2,128]{2,1,0:T(2,128)(2,1)} %new_ref.1, bf16[160,256]{1,0:T(8,128)(2,1)} %bitcast.27, ...), custom_call_target="tpu_custom_call" | custom-call | tf_op jit(solution)/shard_map/attend/pallas_call | solution.py:212
  10.4 8.2 %all-to-all-start = ((bf16[8,8,640]{2,1,0:T(8,128)(2,1)}), bf16[8,8,640]{2,1,0:T(8,128)(2,1)S(1)}, u32[]{:S(2)}, u32[]{:S(2)}) async-start(bf16[8,8,640]{2,1,0:T(8,128)(2,1)} %get-tuple-element.20), calls=%async_computation | async-start | bytes 163840 | tf_op jit(solution)/shard_map/all_to_all | solution.py:228
  18.6 0.0 copy-start
  18.6 1.6 %collective-permute-start = (bf16[16,160]{1,0:T(8,128)(2,1)}, bf16[16,160]{1,0:T(8,128)(2,1)S(1)}, u32[]{:S(2)}, u32[]{:S(2)}) collective-permute-start(bf16[16,160]{1,0:T(8,128)(2,1)} %get-tuple-element.22), channel_id=1, source_target_pairs={{0,8},{8,16},{16,24},{24,0},{1,9},{9,17},{17,25},{25,1},{2,10},{10... | collective-permute-start | bytes 15368 | tf_op jit(solution)/shard_map/ppermute | solution.py:209
  20.2 1.7 %collective-permute-start.1 = (bf16[16,160]{1,0:T(8,128)(2,1)}, bf16[16,160]{1,0:T(8,128)(2,1)S(1)}, u32[]{:S(2)}, u32[]{:S(2)}) collective-permute-start(bf16[16,160]{1,0:T(8,128)(2,1)} %get-tuple-element.23), channel_id=1, source_target_pairs={{0,16},{8,24},{16,0},{24,8},{1,17},{9,25},{17,1},{25,9},{2,18},{10... | collective-permute-start | bytes 15368 | tf_op jit(solution)/shard_map/ppermute | solution.py:209
  21.9 0.7 collective-permute-done.refs_1_
  22.6 0.9 collective-permute-start.2
  23.4 1.0 collective-permute-done.1.refs_2_
  24.4 1.2 %collective-permute-done.2.refs_3_ = bf16[16,160]{1,0:T(8,128)(2,1)S(1)} collective-permute-done((bf16[16,160]{1,0:T(8,128)(2,1)}, bf16[16,160]{1,0:T(8,128)(2,1)S(1)}, u32[]{:S(2)}, u32[]{:S(2)}) %collective-permute-start.2) | collective-permute-done | bytes 5152 | tf_op jit(solution)/shard_map/ppermute | solution.py:209
  25.6 0.5 all-to-all-done
  26.1 0.0 collective-permute-done.5
  26.1 0.0 collective-permute-done.4
  26.1 0.0 collective-permute-done.3
  26.1 0.0 copy-done.3
  26.1 0.4 fusion
  26.5 13.1 %all_to_all.30.partial_ref = f32[8,8,640]{2,1,0:T(8,128)S(1)} all-to-all(f32[8,8,640]{2,1,0:T(8,128)S(1)} %fusion), channel_id=1, replica_groups=mesh['z'=8,'x'=4,'y'=4,'c'=2] {'c','y'}, dimensions={0} | all-to-all | bytes 327680 | tf_op jit(solution)/shard_map/all_to_all | solution.py:235
  39.5 0.0 copy-done
  39.6 0.2 resid.1
  39.8 14.1 %all_to_all.31.rows_ref = bf16[8,8,768]{2,1,0:T(8,128)(2,1)S(1)} all-to-all(bf16[8,8,768]{2,1,0:T(8,128)(2,1)S(1)} %resid.1), channel_id=1, replica_groups=mesh['z'=8,'x'=4,'y'=4,'c'=2] {'z'}, dimensions={0} | all-to-all | bytes 196608 | tf_op jit(solution)/shard_map/all_to_all | solution.py:246
  53.9 0.2 norm.1
  54.1 0.0 copy-start.2
  54.1 21.8 %all_to_all.32 = bf16[16,8,5120]{2,1,0:T(8,128)(2,1)S(1)} all-to-all(bf16[16,8,5120]{2,1,0:T(8,128)(2,1)S(1)} %norm.1), channel_id=1, replica_groups=mesh['z'=8,'x'=4,'y'=4,'c'=2] {'y','x'}, dimensions={0} | all-to-all | bytes 2621440 | tf_op jit(solution)/shard_map/all_to_all | solution.py:255
  75.9 3.4 %collective-permute-start.6 = (bf16[128,5120]{1,0:T(8,128)(2,1)S(1)}, bf16[128,5120]{1,0:T(8,128)(2,1)S(1)}, u32[]{:S(2)}, u32[]{:S(2)}) collective-permute-start(bf16[128,5120]{1,0:T(8,128)(2,1)S(1)} %bitcast.23), channel_id=1, source_target_pairs={{0,1},{1,0},{2,3},{3,2},{4,5},{5,4},{6,7},{7,6},{8,9},{9,8},{10,11... | collective-permute-start | bytes 3932168 | tf_op jit(solution)/shard_map/ppermute | solution.py:257
  79.3 0.0 copy-done.2
  79.3 2.8 %fetch.1.head_ref = bf16[594,5120]{1,0:T(8,128)(2,1)S(1)} custom-call(bf16[594,5120]{1,0:T(8,128)(2,1)} %head_hbm.1, bf16[128,5120]{1,0:T(8,128)(2,1)S(1)} %bitcast.24), custom_call_target="tpu_custom_call" | custom-call | tf_op jit(solution)/shard_map/fetch/pallas_call | solution.py:258
  82.1 0.0 collective-permute-done.6
  82.1 0.2 broadcast_select_fusion.1
  82.3 0.2 pad_maximum_fusion.rows_ref
  82.4 0.0 copy-start.1
  82.5 2.0 %logits.1 = (f32[594,256]{1,0:T(8,128)S(1)}, f32[2,256]{1,0:T(2,128)S(1)}) custom-call(bf16[594,5120]{1,0:T(8,128)(2,1)S(1)} %fetch.1.head_ref, bf16[256,5120]{1,0:T(8,128)(2,1)S(1)} %pad_maximum_fusion.rows_ref, s32[1,256]{1,0:T(1,128)S(1)} %bitcast.25), custom_call_target="tpu_custom_call" | custom-call | tf_op jit(solution)/shard_map/logits/pallas_call | solution.py:275
  84.5 10.7 %all_to_all.33 = f32[32,2,256]{2,1,0:T(2,128)S(1)} all-to-all(f32[32,2,256]{2,1,0:T(2,128)S(1)} %broadcast_in_dim.24), channel_id=1, replica_groups=mesh['z'=8,'x'=4,'y'=4,'c'=2] {'x','y','c'}, dimensions={0} | all-to-all | bytes 131072 | tf_op jit(solution)/shard_map/all_to_all | solution.py:198
  95.2 0.1 slice_reduce_fusion.1
  95.3 9.0 %all_to_all.34.stats_ref = f32[8,2,256]{2,1,0:T(2,128)S(1)} all-to-all(f32[8,2,256]{2,1,0:T(2,128)S(1)} %broadcast_in_dim.25), channel_id=1, replica_groups=mesh['z'=8,'x'=4,'y'=4,'c'=2] {'z'}, dimensions={0} | all-to-all | bytes 32768 | tf_op jit(solution)/shard_map/all_to_all | solution.py:198
  104.3 0.0 copy-done.1
  104.3 0.9 final.1
  (6 shorter events, 0.1 us)
Async XLA Ops:
  0.6 25.4 %collective-permute-start.5 = (bf16[160,640]{1,0:T(8,128)(2,1)}, bf16[160,640]{1,0:T(8,128)(2,1)S(1)}, u32[]{:S(2)}, u32[]{:S(2)}) collective-permute-start(bf16[160,640]{1,0:T(8,128)(2,1)} %bitcast.32), channel_id=1, source_target_pairs={{0,24},{8,0},{16,8},{24,16},{1,25},{9,1},{17,9},{25,17},{2,26},{10... | collective-permute-start | bytes 614408 | tf_op jit(solution)/shard_map/ppermute | solution.py:209
  4.0 22.1 %collective-permute-start.4 = (bf16[160,640]{1,0:T(8,128)(2,1)}, bf16[160,640]{1,0:T(8,128)(2,1)S(1)}, u32[]{:S(2)}, u32[]{:S(2)}) collective-permute-start(bf16[160,640]{1,0:T(8,128)(2,1)} %bitcast.33), channel_id=1, source_target_pairs={{0,16},{8,24},{16,0},{24,8},{1,17},{9,25},{17,1},{25,9},{2,18},{10... | collective-permute-start | bytes 614408 | tf_op jit(solution)/shard_map/ppermute | solution.py:209
  4.5 21.5 %collective-permute-start.3 = (bf16[160,640]{1,0:T(8,128)(2,1)}, bf16[160,640]{1,0:T(8,128)(2,1)S(1)}, u32[]{:S(2)}, u32[]{:S(2)}) collective-permute-start(bf16[160,640]{1,0:T(8,128)(2,1)} %bitcast.34), channel_id=1, source_target_pairs={{0,8},{8,16},{16,24},{24,0},{1,9},{9,17},{17,25},{25,1},{2,10},{10... | collective-permute-start | bytes 614408 | tf_op jit(solution)/shard_map/ppermute | solution.py:209
  5.1 20.9 %copy-start.3 = (bf16[640,160]{0,1:T(8,128)(2,1)S(1)}, bf16[640,160]{0,1:T(8,128)(2,1)}, u32[]{:S(2)}) copy-start(bf16[640,160]{0,1:T(8,128)(2,1)} %param.15) | copy-start | bytes 614404
  10.4 15.7 %all-to-all-start = ((bf16[8,8,640]{2,1,0:T(8,128)(2,1)}), bf16[8,8,640]{2,1,0:T(8,128)(2,1)S(1)}, u32[]{:S(2)}, u32[]{:S(2)}) async-start(bf16[8,8,640]{2,1,0:T(8,128)(2,1)} %get-tuple-element.20), calls=%async_computation | async-start | bytes 163840 | tf_op jit(solution)/shard_map/all_to_all | solution.py:228
  18.6 21.0 %copy-start = (bf16[16,160]{1,0:T(8,128)(2,1)S(1)}, bf16[16,160]{1,0:T(8,128)(2,1)}, u32[]{:S(2)}) copy-start(bf16[16,160]{1,0:T(8,128)(2,1)} %get-tuple-element.26.refs_0_) | copy-start | bytes 15364
  18.6 4.0 %collective-permute-start = (bf16[16,160]{1,0:T(8,128)(2,1)}, bf16[16,160]{1,0:T(8,128)(2,1)S(1)}, u32[]{:S(2)}, u32[]{:S(2)}) collective-permute-start(bf16[16,160]{1,0:T(8,128)(2,1)} %get-tuple-element.22), channel_id=1, source_target_pairs={{0,8},{8,16},{16,24},{24,0},{1,9},{9,17},{17,25},{25,1},{2,10},{10... | collective-permute-start | bytes 15368 | tf_op jit(solution)/shard_map/ppermute | solution.py:209
  20.2 4.2 %collective-permute-start.1 = (bf16[16,160]{1,0:T(8,128)(2,1)}, bf16[16,160]{1,0:T(8,128)(2,1)S(1)}, u32[]{:S(2)}, u32[]{:S(2)}) collective-permute-start(bf16[16,160]{1,0:T(8,128)(2,1)} %get-tuple-element.23), channel_id=1, source_target_pairs={{0,16},{8,24},{16,0},{24,8},{1,17},{9,25},{17,1},{25,9},{2,18},{10... | collective-permute-start | bytes 15368 | tf_op jit(solution)/shard_map/ppermute | solution.py:209
  22.6 3.0 %collective-permute-start.2 = (bf16[16,160]{1,0:T(8,128)(2,1)}, bf16[16,160]{1,0:T(8,128)(2,1)S(1)}, u32[]{:S(2)}, u32[]{:S(2)}) collective-permute-start(bf16[16,160]{1,0:T(8,128)(2,1)} %get-tuple-element.24), channel_id=1, source_target_pairs={{0,24},{8,0},{16,8},{24,16},{1,25},{9,1},{17,9},{25,17},{2,26},{10... | collective-permute-start | bytes 15368 | tf_op jit(solution)/shard_map/ppermute | solution.py:209
  54.1 25.2 %copy-start.2 = (s32[256]{0:T(256)S(1)}, s32[256]{0:T(256)}, u32[]{:S(2)}) copy-start(s32[256]{0:T(256)} %param.18) | copy-start | bytes 3076
  75.9 6.2 %collective-permute-start.6 = (bf16[128,5120]{1,0:T(8,128)(2,1)S(1)}, bf16[128,5120]{1,0:T(8,128)(2,1)S(1)}, u32[]{:S(2)}, u32[]{:S(2)}) collective-permute-start(bf16[128,5120]{1,0:T(8,128)(2,1)S(1)} %bitcast.23), channel_id=1, source_target_pairs={{0,1},{1,0},{2,3},{3,2},{4,5},{5,4},{6,7},{7,6},{8,9},{9,8},{10,11... | collective-permute-start | bytes 3932168 | tf_op jit(solution)/shard_map/ppermute | solution.py:257
  82.4 21.9 %copy-start.1 = (f32[256]{0:T(256)S(1)}, f32[256]{0:T(256)}, u32[]{:S(2)}) copy-start(f32[256]{0:T(256)} %param.19) | copy-start | bytes 3076

commit v5 on v3

--- a/solution.py
+++ b/solution.py
@@ -30,7 +30,6 @@
 SMALL = pltpu.CompilerParams(vmem_limit_bytes=20 << 20)
 WIDE = pltpu.CompilerParams(vmem_limit_bytes=44 << 20)
 WHOLE = pltpu.CompilerParams(vmem_limit_bytes=60 << 20)
-TAIL = 16
 CHUNK = 1280
 
 
@@ -42,24 +41,26 @@
     return first, second, third
 
 
-def tails_of(count, part, x, hidden_ref, gain_ref, tail_refs):
+def side_by_side(rows):
+    return jnp.concatenate([rows[k : k + 8] for k in range(0, rows.shape[0], 8)], axis=1)
+
+
+def local_terms(part, hidden_ref, gain_ref, terms_ref):
     columns, requests = hidden_ref.shape
-    row = lax.broadcasted_iota(jnp.int32, (count, requests), 0)
-    lane = lax.broadcasted_iota(jnp.int32, (count, requests), 1)
-    parts = three_parts(gain_ref[...])
-    below = jnp.concatenate(parts + (jnp.zeros((TAIL - count - 3, columns), f32),), axis=0)
-    for step, tail_ref in enumerate(tail_refs):
-        target = lax.rem(x + step, len(tail_refs))
-        place = (part * len(tail_refs) + target) * count
-        chosen = jnp.where(lane == row + place, 1.0, 0.0).astype(bf16)
-        hidden = lax.dot_general(
-            chosen, hidden_ref[...], (((1,), (1,)), ((), ())), preferred_element_type=f32
-        )
-        tail_ref[...] = jnp.concatenate([hidden, below], axis=0).astype(bf16)
-
-
-def attend_kernel(group, sizes, lengths_ref, query_ref, new_ref, hidden_ref, gain_ref, cache_ref, *refs):
-    out_ref, tail_refs, (slots_ref, rows_ref, sums_ref, sems) = refs[0], refs[1:-4], refs[-4:]
+    groups = terms_ref.shape[1] // columns
+    rows = groups * 8
+    row = lax.broadcasted_iota(jnp.int32, (rows, requests), 0)
+    lane = lax.broadcasted_iota(jnp.int32, (rows, requests), 1)
+    chosen = jnp.where(lane == row + part * rows, 1.0, 0.0).astype(bf16)
+    hidden = lax.dot_general(
+        chosen, hidden_ref[...], (((1,), (1,)), ((), ())), preferred_element_type=f32
+    )
+    terms_ref[:8] = side_by_side(hidden)
+    gain = jnp.broadcast_to(gain_ref[...], (8, columns))
+    terms_ref[8:] = jnp.concatenate([gain] * groups, axis=1)
+
+
+def attend_kernel(group, sizes, lengths_ref, query_ref, new_ref, hidden_ref, gain_ref, cache_ref, out_ref, terms_ref, slots_ref, rows_ref, sums_ref, sems):
     count, _, slots, head_dim = cache_ref.shape
     z, x, y, c = (lax.axis_index(a) for a in ("z", "x", "y", "c"))
     scale = head_dim ** (-0.5)
@@ -72,7 +73,7 @@
     ]
     for load in loads[0] + loads[1]:
         load.start()
-    tails_of(count, c * sizes["y"] + y, x, hidden_ref, gain_ref, tail_refs)
+    local_terms(c * sizes["y"] + y, hidden_ref, gain_ref, terms_ref)
 
     query = query_ref[...].astype(f32)
     fresh = new_ref[...].astype(f32)
@@ -115,44 +116,50 @@
         out_ref[k] = done
 
 
-def resid_kernel(partial_ref, *refs):
-    tails, out_ref = refs[:-1], refs[-1]
+def project_kernel(rows_ref, table_ref, out_ref):
+    product = lax.dot_general(
+        rows_ref[...], table_ref[...], (((1,), (1,)), ((), ())), preferred_element_type=f32
+    )
+    size = product.shape[0] // out_ref.shape[0]
+    for k in range(out_ref.shape[0]):
+        out_ref[k] = side_by_side(product[k * size : (k + 1) * size])
+
+
+def resid_kernel(columns, partial_ref, terms_ref, out_ref):
     count, width = partial_ref.shape[1:]
-    columns = width // len(tails)
     total = partial_ref[0]
     for k in range(1, partial_ref.shape[0]):
         total = total + partial_ref[k]
-    squares = jnp.zeros((count, 1), f32)
-    blocks = []
-    for step, tail_ref in enumerate(tails):
-        tail = tail_ref[...].astype(f32)
-        gain = tail[count : count + 1] + tail[count + 1 : count + 2] + tail[count + 2 : count + 3]
-        resid = total[:, step * columns : (step + 1) * columns] + tail[:count]
-        resid = resid.astype(bf16).astype(f32)
-        squares = squares + jnp.sum(resid * resid, axis=1, keepdims=True)
-        blocks.append(resid * gain)
-    shift = lax.rem(lax.axis_index("x") + 1, len(tails)) * columns
-    ordered = pltpu.roll(jnp.concatenate(blocks[::-1], axis=1), shift, 1)
+    resid = (total + terms_ref[:count]).astype(bf16).astype(f32)
     lane = lax.broadcasted_iota(jnp.int32, (count, LANES), 1)
     spare = jnp.zeros((count, LANES), f32)
-    for k, part in enumerate(three_parts(squares)):
-        spare = jnp.where(lane == k, part, spare)
-    done = jnp.concatenate([ordered, spare], axis=1).astype(bf16)
+    for g in range(width // columns):
+        piece = resid[:, g * columns : (g + 1) * columns]
+        for k, part in enumerate(three_parts(jnp.sum(piece * piece, axis=1, keepdims=True))):
+            spare = jnp.where(lane == 3 * g + k, part, spare)
+    done = jnp.concatenate([resid * terms_ref[count:], spare], axis=1).astype(bf16)
     for k in range(out_ref.shape[0]):
         out_ref[k] = done
 
 
-def norm_kernel(rows_ref, out_ref):
-    blocks, count, padded = rows_ref.shape
+def norm_kernel(columns, rows_ref, out_ref):
+    sources, count, padded = rows_ref.shape
     width = padded - LANES
     squares = jnp.zeros((count, LANES), f32)
-    for k in range(blocks):
+    for k in range(sources):
         squares = squares + rows_ref[k, :, width:].astype(f32)
-    factor = lax.rsqrt(jnp.sum(squares, axis=1, keepdims=True) / D + epsilon)
-    for k in range(blocks):
-        done = (rows_ref[k, :, :width].astype(f32) * factor).astype(bf16)
-        for copy in range(out_ref.shape[0]):
-            out_ref[copy, :, k * width : (k + 1) * width] = done
+    lane = lax.broadcasted_iota(jnp.int32, (count, LANES), 1)
+    factors = []
+    for g in range(width // columns):
+        mine = jnp.where((lane >= 3 * g) & (lane < 3 * g + 3), squares, 0.0)
+        factors.append(lax.rsqrt(jnp.sum(mine, axis=1, keepdims=True) / D + epsilon))
+    for k in range(0, sources, 4):
+        blocks = [rows_ref[k + i, :, :width].astype(f32) for i in range(4)]
+        rows = [
+            jnp.concatenate([b[:, g * columns : (g + 1) * columns] for b in blocks], axis=1) * factors[g]
+            for g in range(width // columns)
+        ]
+        out_ref[:, k * columns : (k + 4) * columns] = jnp.concatenate(rows, axis=0).astype(bf16)
 
 
 def fetch_kernel(head_hbm, after_ref, head_ref, sem):
@@ -161,8 +168,16 @@
     load.wait()
 
 
-def logits_kernel(head_ref, rows_ref, ids_ref, logits_ref, stats_ref):
+def logits_kernel(head_ref, ids_ref, *refs):
+    blocks, (logits_ref, stats_ref, rows_ref) = refs[:-3], refs[-3:]
+    y, c = lax.axis_index("y"), lax.axis_index("c")
     depth = head_ref.shape[1]
+    number = len(blocks) // 2
+    size = blocks[0].shape[0]
+    for k, block in enumerate(blocks):
+        core = c if k < number else 1 - c
+        place = core * number + lax.rem(y + k % number, number)
+        rows_ref[pl.ds(pl.multiple_of(place * size, size), size), :] = block[...]
     for k in range(depth // CHUNK):
         span = slice(k * CHUNK, (k + 1) * CHUNK)
         product = lax.dot_general(
@@ -201,18 +216,19 @@
     z, x, y, c = (lax.axis_index(a) for a in ("z", "x", "y", "c"))
     count = query.shape[0]
     heads, columns = out_proj.shape
+    requests = hidden_in.shape[0]
+    share = requests // (ny * nc)
+    width = share // 8 * columns
     sizes = {"z": nz, "x": nx, "y": ny, "c": nc}
 
-    def from_along_x(block, step):
-        return lax.ppermute(block, "x", [(i, (i + step) % nx) for i in range(nx)])
-
-    table = jnp.concatenate([out_proj.T] + [from_along_x(out_proj.T, k) for k in range(1, nx)], axis=0)
-    many, *tails = pl.pallas_call(
+    many, terms = pl.pallas_call(
         functools.partial(attend_kernel, HEADS // KV_HEADS, sizes),
-        out_shape=[jax.ShapeDtypeStruct((nz,) + query.shape, bf16)]
-        + [jax.ShapeDtypeStruct((TAIL, columns), bf16)] * nx,
+        out_shape=[
+            jax.ShapeDtypeStruct((nz * nx,) + query.shape, bf16),
+            jax.ShapeDtypeStruct((16, width), f32),
+        ],
         in_specs=[IN_SMEM] + [IN_VMEM] * 4 + [IN_PLACE],
-        out_specs=[IN_VMEM] * (nx + 1),
+        out_specs=[IN_VMEM] * 2,
         scratch_shapes=[
             pltpu.VMEM(cache.shape, bf16),
             pltpu.VMEM((count * 8, HEAD_DIM), f32),
@@ -222,35 +238,48 @@
         compiler_params=WHOLE,
         name="attend",
     )(lengths, query, new_kv, hidden_in.T, final_gain[None], cache)
-    tails = [tails[0]] + [from_along_x(tails[k], k) for k in range(1, nx)]
-    gathered = lax.all_to_all(many, "z", split_axis=0, concat_axis=0, tiled=False)
-    gathered = gathered.reshape(nz * count, -1)
-    partial = lax.dot_general(
-        gathered, table, (((1,), (1,)), ((), ())), preferred_element_type=f32
-    )
-    partial = partial.reshape(nz, count, nx * columns)
+    gathered = lax.all_to_all(many, ("z", "x"), split_axis=0, concat_axis=0, tiled=False)
+    partial = pl.pallas_call(
+        project_kernel,
+        out_shape=jax.ShapeDtypeStruct((ny * nc, 8, width), f32),
+        in_specs=[IN_VMEM] * 2,
+        out_specs=IN_VMEM,
+        compiler_params=SMALL,
+        name="project",
+    )(gathered.reshape(requests, heads), out_proj.T)
     partial = lax.all_to_all(partial, ("c", "y"), split_axis=0, concat_axis=0, tiled=False)
-
-    width = nx * columns
     rows = pl.pallas_call(
-        resid_kernel,
-        out_shape=jax.ShapeDtypeStruct((nz, count, width + LANES), bf16),
-        in_specs=[IN_VMEM] * (nx + 1),
+        functools.partial(resid_kernel, columns),
+        out_shape=jax.ShapeDtypeStruct((nz * nx, 8, width + LANES), bf16),
+        in_specs=[IN_VMEM] * 2,
         out_specs=IN_VMEM,
         compiler_params=SMALL,
         name="resid",
-    )(partial, *tails)
-    rows = lax.all_to_all(rows, "z", split_axis=0, concat_axis=0, tiled=False)
-    half = pl.pallas_call(
-        norm_kernel,
-        out_shape=jax.ShapeDtypeStruct((nx * ny, count, nz * width), bf16),
+    )(partial, terms)
+    rows = lax.all_to_all(rows, ("z", "x"), split_axis=0, concat_axis=0, tiled=False)
+    own = pl.pallas_call(
+        functools.partial(norm_kernel, columns),
+        out_shape=jax.ShapeDtypeStruct((share, nz * nx * columns), bf16),
         in_specs=[IN_VMEM],
         out_specs=IN_VMEM,
         compiler_params=SMALL,
         name="norm",
     )(rows)
-    half = lax.all_to_all(half, ("x", "y"), split_axis=0, concat_axis=0, tiled=False)
-    other = lax.ppermute(half, "c", [(i, 1 - i) for i in range(2)])
+
+    def along_y(block, step):
+        return lax.ppermute(block, "y", [(i, (i + step) % ny) for i in range(ny)])
+
+    def to_other_core(block):
+        return lax.ppermute(block, "c", [(i, 1 - i) for i in range(nc)])
+
+    before, after = along_y(own, 1), along_y(own, -1)
+    opposite = jnp.concatenate(
+        [along_y(after[: share // 2], -1), along_y(before[share // 2 :], 1)], axis=0
+    )
+    mine = [own, after, opposite, before]
+    other = jnp.split(to_other_core(jnp.concatenate([own, after, before], axis=0)), 3, axis=0)
+    last = to_other_core(opposite)
+    theirs = [other[0], other[1], last, other[2]]
     head = pl.pallas_call(
         fetch_kernel,
         out_shape=jax.ShapeDtypeStruct(lm_head.shape, bf16),
@@ -259,26 +288,20 @@
         scratch_shapes=[pltpu.SemaphoreType.DMA],
         compiler_params=WIDE,
         name="fetch",
-    )(lm_head, half)
-    other, head = lax.optimization_barrier((other, head))
-    half, other = (
-        jnp.swapaxes(h.reshape(nx, ny, count, -1), 0, 1).reshape(nx * ny * count, -1) for h in (half, other)
-    )
-    first = jnp.where(c == 0, half, other)
-    second = jnp.where(c == 0, other, half)
-    everyone = jnp.concatenate([first, second], axis=0)
+    )(lm_head, before)
+    theirs, head = lax.optimization_barrier((theirs, head))
 
     vocab = lm_head.shape[0]
-    requests = everyone.shape[0]
     offset = (((z * nx + x) * ny + y) * nc + c) * vocab
     logits, stats = pl.pallas_call(
         logits_kernel,
         out_shape=[jax.ShapeDtypeStruct((vocab, requests), f32), jax.ShapeDtypeStruct((2, requests), f32)],
-        in_specs=[IN_VMEM] * 3,
+        in_specs=[IN_VMEM] * (2 + 2 * ny),
         out_specs=[IN_VMEM] * 2,
+        scratch_shapes=[pltpu.VMEM((requests, lm_head.shape[1]), bf16)],
         compiler_params=SMALL,
         name="logits",
-    )(head, everyone, (tokens - offset)[None])
+    )(head, (tokens - offset)[None], *mine, *theirs)
 
     stats = spread(stats, ("x", "y", "c"), nx * ny * nc)
     top = jnp.max(stats[:, 0], axis=0)

time: 104 us -> 108 us (1.038)
  starting transfers between devices: 20.2 us -> 9.82 us
  blocking collectives: 67.9 us -> 77.4 us
  waiting for transfers between devices: 2.05 us -> 6.69 us
    all_to_all x1 -> x0, starting transfers between devices: 7.31 us -> none  [shards(): lax.all_to_all(partial, ('c', 'y'), split_axis=0, concat_axis=0, tiled=Fa...]
    all_to_all x3, blocking collectives: 47.8 us -> 54.2 us  [the longest x1 24.4 us: shards(): lax.all_to_all(many, ('z', 'x'), split_axis=0, concat_axis=0, tiled=False)]
    ppermute x7 -> x6, waiting for transfers between devices: 2.04 us -> 6.69 us  [the longest x4 5.37 us: along_y(): return lax.ppermute(block, 'y', [(i, (i + step) % ny) for i in range(ny)])]
    all_to_all x2, blocking collectives: 20.1 us -> 23.2 us  [spread(): return lax.all_to_all(many, axes, split_axis=0, concat_axis=0, tiled=False)]
    ppermute x7 -> x6, starting transfers between devices: 12.9 us -> 9.82 us  [the longest x4 5.57 us: along_y(): return lax.ppermute(block, 'y', [(i, (i + step) % ny) for i in range(ny)])]
  transfers between devices with their start and end apart: 8 -> 6, of which waited for: 2 -> 2; matrix products, arithmetic and copies ran while one was open for 0% -> 0% of each run, Pallas kernels for 7% -> 3%
where the time goes in v5:
time: 108 us; the launch traced here: 107 us
  blocking collectives  77.4 us (72%)
  Pallas kernels  11.3 us (10%)
  starting transfers between devices  9.82 us (9%)
  waiting for transfers between devices  6.69 us (6%)
    all_to_all x1, blocking collectives, shards(): lax.all_to_all(many, ('z', 'x'), split_axis=0, concat_axis=0, tiled=False)  24.4 us
    all_to_all x2, blocking collectives, spread(): return lax.all_to_all(many, axes, split_axis=0, concat_axis=0, tiled=False)  23.2 us
    all_to_all x1, blocking collectives, shards(): lax.all_to_all(rows, ('z', 'x'), split_axis=0, concat_axis=0, tiled=False)  17.6 us
    all_to_all x1, blocking collectives, shards(): lax.all_to_all(partial, ('c', 'y'), split_axis=0, concat_axis=0, tiled=Fa...  12.2 us
    ppermute x4, starting transfers between devices, along_y(): return lax.ppermute(block, 'y', [(i, (i + step) % ny) for i in range(ny)])  5.57 us
    ppermute x4, waiting for transfers between devices, along_y(): return lax.ppermute(block, 'y', [(i, (i + step) % ny) for i in range(ny)])  5.37 us
    pallas_call x1, Pallas kernels, shards(): pl.pallas_call(functools.partial(attend_kernel, HEADS // KV_HEADS, sizes)...  4.72 us
    ppermute x2, starting transfers between devices, to_other_core(): return lax.ppermute(block, 'c', [(i, 1 - i) for i in range(nc)])  4.26 us
  transfers between devices with their start and end apart: 6, of which 2 were waited for; matrix products, arithmetic and copies ran while one was open for 0% of the time, Pallas kernels for 3%

profile of v5, /device:TPU:1, one launch (start us, length us, event | category | flops | bytes accessed | tf_op | source)
XLA Modules:
  0.0 107.1 jit_solution(2019799188443639522)
XLA Ops:
  0.6 0.0 copy-start
  0.6 4.7 %attend.1 = (bf16[32,8,640]{2,1,0:T(8,128)(2,1)}, f32[16,640]{1,0:T(8,128)}) custom-call(s32[256]{0:T(256)} %lengths_ref.1, bf16[8,640]{1,0:T(8,128)(2,1)} %query_ref.1, bf16[8,2,128]{2,1,0:T(2,128)(2,1)} %new_ref.1, bf16[160,256]{1,0:T(8,128)(2,1)} %bitcast.21, f32[1,160]{1,0:T(1,128)} %bitcast.24, bf16[8,2,1024,128]{3,2,1,0:T(8,128)(2,1)} %cache_ref.1), custom_call_target="tpu_custom_call" | custom-call | tf_op jit(solution)/shard_map/attend/pallas_call | solution.py:224
  5.4 0.0 copy-start.3
  5.4 24.4 %all_to_all.25 = bf16[32,8,640]{2,1,0:T(8,128)(2,1)S(1)} all-to-all(bf16[32,8,640]{2,1,0:T(8,128)(2,1)} %get-tuple-element.15), channel_id=1, replica_groups=mesh['z'=8,'x'=4,'y'=4,'c'=2] {'z','x'}, dimensions={0} | all-to-all | bytes 655360 | tf_op jit(solution)/shard_map/all_to_all | solution.py:241
  29.8 0.0 copy-done
  29.8 0.4 project.1
  30.2 12.2 %all_to_all.26.partial_ref = f32[8,8,640]{2,1,0:T(8,128)S(1)} all-to-all(f32[8,8,640]{2,1,0:T(8,128)S(1)} %project.1), channel_id=1, replica_groups=mesh['z'=8,'x'=4,'y'=4,'c'=2] {'c','y'}, dimensions={0} | all-to-all | bytes 327680 | tf_op jit(solution)/shard_map/all_to_all | solution.py:250
  42.3 0.0 copy-start.1
  42.4 0.8 copy-done.1
  43.1 0.2 resid.1
  43.3 17.6 %all_to_all.27.rows_ref = bf16[32,8,768]{2,1,0:T(8,128)(2,1)S(1)} all-to-all(bf16[32,8,768]{2,1,0:T(8,128)(2,1)S(1)} %resid.1), channel_id=1, replica_groups=mesh['z'=8,'x'=4,'y'=4,'c'=2] {'z','x'}, dimensions={0} | all-to-all | bytes 786432 | tf_op jit(solution)/shard_map/all_to_all | solution.py:259
  60.9 0.2 norm.1.refs_0_
  61.1 0.7 collective-permute-start.1
  61.9 2.0 %collective-permute-start = (bf16[32,5120]{1,0:T(8,128)(2,1)S(1)}, bf16[32,5120]{1,0:T(8,128)(2,1)S(1)}, u32[]{:S(2)}, u32[]{:S(2)}) collective-permute-start(bf16[32,5120]{1,0:T(8,128)(2,1)S(1)} %norm.1.refs_0_), channel_id=1, source_target_pairs={{0,6},{2,0},{4,2},{6,4},{1,7},{3,1},{5,3},{7,5},{8,14},{10,8},{12,... | collective-permute-start | bytes 983048 | tf_op jit(solution)/shard_map/ppermute | solution.py:270
  63.9 0.0 copy-done.3
  63.9 5.4 %collective-permute-done.1.after_ref.refs_3_ = bf16[32,5120]{1,0:T(8,128)(2,1)S(1)} collective-permute-done((bf16[32,5120]{1,0:T(8,128)(2,1)S(1)}, bf16[32,5120]{1,0:T(8,128)(2,1)S(1)}, u32[]{:S(2)}, u32[]{:S(2)}) %collective-permute-start.1) | collective-permute-done | bytes 327712 | tf_op jit(solution)/shard_map/ppermute | solution.py:270
  69.3 0.1 collective-permute-start.4
  69.4 0.0 collective-permute-done.refs_1_
  69.4 2.7 %collective-permute-start.3 = (bf16[16,5120]{1,0:T(8,128)(2,1)S(1)}, bf16[16,5120]{1,0:T(8,128)(2,1)S(1)}, u32[]{:S(2)}, u32[]{:S(2)}) collective-permute-start(bf16[16,5120]{1,0:T(8,128)(2,1)S(1)} %slice.17), channel_id=1, source_target_pairs={{0,6},{2,0},{4,2},{6,4},{1,7},{3,1},{5,3},{7,5},{8,14},{10,8},{12,... | collective-permute-start | bytes 491528 | tf_op jit(solution)/shard_map/ppermute | solution.py:270
  72.1 0.1 pad_maximum_fusion
  72.2 3.9 %collective-permute-start.2 = (bf16[96,5120]{1,0:T(8,128)(2,1)S(1)}, bf16[96,5120]{1,0:T(8,128)(2,1)S(1)}, u32[]{:S(2)}, u32[]{:S(2)}) collective-permute-start(bf16[96,5120]{1,0:T(8,128)(2,1)S(1)} %pad_maximum_fusion), channel_id=1, source_target_pairs={{0,1},{1,0},{2,3},{3,2},{4,5},{5,4},{6,7},{7,6},{8,9},{9,8},{10,11... | collective-permute-start | bytes 2949128 | tf_op jit(solution)/shard_map/ppermute | solution.py:273
  76.1 2.8 %fetch.1.head_ref = bf16[594,5120]{1,0:T(8,128)(2,1)S(1)} custom-call(bf16[594,5120]{1,0:T(8,128)(2,1)} %head_hbm.1, bf16[32,5120]{1,0:T(8,128)(2,1)S(1)} %collective-permute-done.1.after_ref.refs_3_), custom_call_target="tpu_custom_call" | custom-call | tf_op jit(solution)/shard_map/fetch/pallas_call | solution.py:283
  78.9 0.0 collective-permute-done.3
  78.9 0.0 collective-permute-done.4
  78.9 0.3 collective-permute-start.5
  79.3 0.0 collective-permute-done.2
  79.3 0.1 fusion.2
  79.3 1.3 %collective-permute-done.5.refs_6_ = bf16[32,5120]{1,0:T(8,128)(2,1)S(1)} collective-permute-done((bf16[32,5120]{1,0:T(8,128)(2,1)S(1)}, bf16[32,5120]{1,0:T(8,128)(2,1)S(1)}, u32[]{:S(2)}, u32[]{:S(2)}) %collective-permute-start.5) | collective-permute-done | bytes 327712 | tf_op jit(solution)/shard_map/ppermute | solution.py:273
  80.7 0.0 copy-start.2
  80.7 2.2 %logits.1 = (f32[594,256]{1,0:T(8,128)S(1)}, f32[2,256]{1,0:T(2,128)S(1)}) custom-call(bf16[594,5120]{1,0:T(8,128)(2,1)S(1)} %fetch.1.head_ref, s32[1,256]{1,0:T(1,128)S(1)} %bitcast.19, bf16[32,5120]{1,0:T(8,128)(2,1)S(1)} %norm.1.refs_0_, bf16[32,5120]{1,0:T(8,128)(2,1)S(1)} %collective-permute-done.refs_1_, ...), custom_call_target="tpu_custom_call" | custom-call | tf_op jit(solution)/shard_map/logits/pallas_call | solution.py:296
  82.9 14.2 %all_to_all.28 = f32[32,2,256]{2,1,0:T(2,128)S(1)} all-to-all(f32[32,2,256]{2,1,0:T(2,128)S(1)} %broadcast_in_dim.24), channel_id=1, replica_groups=mesh['z'=8,'x'=4,'y'=4,'c'=2] {'x','y','c'}, dimensions={0} | all-to-all | bytes 131072 | tf_op jit(solution)/shard_map/all_to_all | solution.py:211
  97.1 0.1 slice_reduce_fusion.1
  97.3 9.0 %all_to_all.29.stats_ref = f32[8,2,256]{2,1,0:T(2,128)S(1)} all-to-all(f32[8,2,256]{2,1,0:T(2,128)S(1)} %broadcast_in_dim.25), channel_id=1, replica_groups=mesh['z'=8,'x'=4,'y'=4,'c'=2] {'z'}, dimensions={0} | all-to-all | bytes 32768 | tf_op jit(solution)/shard_map/all_to_all | solution.py:211
  106.2 0.0 copy-done.2
  106.2 0.9 final.1
  (10 shorter events, 0.1 us)
Async XLA Ops:
  0.6 29.2 %copy-start = (bf16[640,160]{0,1:T(8,128)(2,1)S(1)}, bf16[640,160]{0,1:T(8,128)(2,1)}, u32[]{:S(2)}) copy-start(bf16[640,160]{0,1:T(8,128)(2,1)} %param.15) | copy-start | bytes 614404
  5.4 58.5 %copy-start.3 = (s32[256]{0:T(256)S(1)}, s32[256]{0:T(256)}, u32[]{:S(2)}) copy-start(s32[256]{0:T(256)} %param.18) | copy-start | bytes 3076
  42.3 0.8 copy-start.1
  61.1 8.1 %collective-permute-start.1 = (bf16[32,5120]{1,0:T(8,128)(2,1)S(1)}, bf16[32,5120]{1,0:T(8,128)(2,1)S(1)}, u32[]{:S(2)}, u32[]{:S(2)}) collective-permute-start(bf16[32,5120]{1,0:T(8,128)(2,1)S(1)} %norm.1.refs_0_), channel_id=1, source_target_pairs={{0,2},{2,4},{4,6},{6,0},{1,3},{3,5},{5,7},{7,1},{8,10},{10,12},{12... | collective-permute-start | bytes 983048 | tf_op jit(solution)/shard_map/ppermute | solution.py:270
  61.9 7.5 %collective-permute-start = (bf16[32,5120]{1,0:T(8,128)(2,1)S(1)}, bf16[32,5120]{1,0:T(8,128)(2,1)S(1)}, u32[]{:S(2)}, u32[]{:S(2)}) collective-permute-start(bf16[32,5120]{1,0:T(8,128)(2,1)S(1)} %norm.1.refs_0_), channel_id=1, source_target_pairs={{0,6},{2,0},{4,2},{6,4},{1,7},{3,1},{5,3},{7,5},{8,14},{10,8},{12,... | collective-permute-start | bytes 983048 | tf_op jit(solution)/shard_map/ppermute | solution.py:270
  69.3 9.7 %collective-permute-start.4 = (bf16[16,5120]{1,0:T(8,128)(2,1)S(1)}, bf16[16,5120]{1,0:T(8,128)(2,1)S(1)}, u32[]{:S(2)}, u32[]{:S(2)}) collective-permute-start(bf16[16,5120]{1,0:T(8,128)(2,1)S(1)} %slice.18), channel_id=1, source_target_pairs={{0,2},{2,4},{4,6},{6,0},{1,3},{3,5},{5,7},{7,1},{8,10},{10,12},{12... | collective-permute-start | bytes 491528 | tf_op jit(solution)/shard_map/ppermute | solution.py:270
  69.4 9.5 %collective-permute-start.3 = (bf16[16,5120]{1,0:T(8,128)(2,1)S(1)}, bf16[16,5120]{1,0:T(8,128)(2,1)S(1)}, u32[]{:S(2)}, u32[]{:S(2)}) collective-permute-start(bf16[16,5120]{1,0:T(8,128)(2,1)S(1)} %slice.17), channel_id=1, source_target_pairs={{0,6},{2,0},{4,2},{6,4},{1,7},{3,1},{5,3},{7,5},{8,14},{10,8},{12,... | collective-permute-start | bytes 491528 | tf_op jit(solution)/shard_map/ppermute | solution.py:270
  72.2 7.1 %collective-permute-start.2 = (bf16[96,5120]{1,0:T(8,128)(2,1)S(1)}, bf16[96,5120]{1,0:T(8,128)(2,1)S(1)}, u32[]{:S(2)}, u32[]{:S(2)}) collective-permute-start(bf16[96,5120]{1,0:T(8,128)(2,1)S(1)} %pad_maximum_fusion), channel_id=1, source_target_pairs={{0,1},{1,0},{2,3},{3,2},{4,5},{5,4},{6,7},{7,6},{8,9},{9,8},{10,11... | collective-permute-start | bytes 2949128 | tf_op jit(solution)/shard_map/ppermute | solution.py:273
  78.9 1.7 %collective-permute-start.5 = (bf16[32,5120]{1,0:T(8,128)(2,1)S(1)}, bf16[32,5120]{1,0:T(8,128)(2,1)S(1)}, u32[]{:S(2)}, u32[]{:S(2)}) collective-permute-start(bf16[32,5120]{1,0:T(8,128)(2,1)S(1)} %constant_dynamic-update-slice_fusion.refs_2_), channel_id=1, source_target_pairs={{0,1},{1,0},{2,3},{3,2},{4,5},{5,4},{6,7},{7,6},{8,9},{9,8},{10,11... | collective-permute-start | bytes 983048 | tf_op jit(solution)/shard_map/ppermute | solution.py:273
  80.7 25.6 %copy-start.2 = (f32[256]{0:T(256)S(1)}, f32[256]{0:T(256)}, u32[]{:S(2)}) copy-start(f32[256]{0:T(256)} %param.19) | copy-start | bytes 3076

commit v6 on v3

--- a/solution.py
+++ b/solution.py
@@ -150,9 +150,21 @@
         squares = squares + rows_ref[k, :, width:].astype(f32)
     factor = lax.rsqrt(jnp.sum(squares, axis=1, keepdims=True) / D + epsilon)
     for k in range(blocks):
-        done = (rows_ref[k, :, :width].astype(f32) * factor).astype(bf16)
-        for copy in range(out_ref.shape[0]):
-            out_ref[copy, :, k * width : (k + 1) * width] = done
+        out_ref[:, k * width : (k + 1) * width] = (rows_ref[k, :, :width].astype(f32) * factor).astype(bf16)
+
+
+def order_kernel(*refs):
+    blocks, out_ref = [ref[...].astype(f32) for ref in refs[:-1]], refs[-1]
+    x = lax.axis_index("x")
+    number = len(blocks)
+    ordered = []
+    for k in range(number):
+        ahead = lax.rem(k + number - x, number)
+        piece = blocks[0]
+        for step in range(1, number):
+            piece = jnp.where(ahead == step, blocks[step], piece)
+        ordered.append(piece)
+    out_ref[...] = jnp.concatenate(ordered, axis=0).astype(bf16)
 
 
 def fetch_kernel(head_hbm, after_ref, head_ref, sem):
@@ -161,8 +173,16 @@
     load.wait()
 
 
-def logits_kernel(head_ref, rows_ref, ids_ref, logits_ref, stats_ref):
+def logits_kernel(head_ref, ids_ref, *refs):
+    blocks, (logits_ref, stats_ref, rows_ref) = refs[:-3], refs[-3:]
+    y, c = lax.axis_index("y"), lax.axis_index("c")
     depth = head_ref.shape[1]
+    number = len(blocks) // 2
+    size = blocks[0].shape[0]
+    for k, block in enumerate(blocks):
+        core = c if k < number else 1 - c
+        place = core * number + lax.rem(y + k % number, number)
+        rows_ref[pl.ds(pl.multiple_of(place * size, size), size), :] = block[...]
     for k in range(depth // CHUNK):
         span = slice(k * CHUNK, (k + 1) * CHUNK)
         product = lax.dot_general(
@@ -241,16 +261,31 @@
         name="resid",
     )(partial, *tails)
     rows = lax.all_to_all(rows, "z", split_axis=0, concat_axis=0, tiled=False)
-    half = pl.pallas_call(
+    normed = pl.pallas_call(
         norm_kernel,
-        out_shape=jax.ShapeDtypeStruct((nx * ny, count, nz * width), bf16),
+        out_shape=jax.ShapeDtypeStruct((count, nz * width), bf16),
         in_specs=[IN_VMEM],
         out_specs=IN_VMEM,
         compiler_params=SMALL,
         name="norm",
     )(rows)
-    half = lax.all_to_all(half, ("x", "y"), split_axis=0, concat_axis=0, tiled=False)
-    other = lax.ppermute(half, "c", [(i, 1 - i) for i in range(2)])
+    share = nx * count
+    own = pl.pallas_call(
+        order_kernel,
+        out_shape=jax.ShapeDtypeStruct((share, nz * width), bf16),
+        in_specs=[IN_VMEM] * nx,
+        out_specs=IN_VMEM,
+        compiler_params=SMALL,
+        name="order",
+    )(normed, *(from_along_x(normed, nx - k) for k in range(1, nx)))
+
+    def along_y(block, step):
+        return lax.ppermute(block, "y", [(i, (i + step) % ny) for i in range(ny)])
+
+    def to_other_core(block):
+        return lax.ppermute(block, "c", [(i, 1 - i) for i in range(nc)])
+
+    before, after = along_y(own, 1), along_y(own, -1)
     head = pl.pallas_call(
         fetch_kernel,
         out_shape=jax.ShapeDtypeStruct(lm_head.shape, bf16),
@@ -259,26 +294,28 @@
         scratch_shapes=[pltpu.SemaphoreType.DMA],
         compiler_params=WIDE,
         name="fetch",
-    )(lm_head, half)
-    other, head = lax.optimization_barrier((other, head))
-    half, other = (
-        jnp.swapaxes(h.reshape(nx, ny, count, -1), 0, 1).reshape(nx * ny * count, -1) for h in (half, other)
+    )(lm_head, own)
+    before, after, head = lax.optimization_barrier((before, after, head))
+    opposite = jnp.concatenate(
+        [along_y(after[: share // 2], -1), along_y(before[share // 2 :], 1)], axis=0
     )
-    first = jnp.where(c == 0, half, other)
-    second = jnp.where(c == 0, other, half)
-    everyone = jnp.concatenate([first, second], axis=0)
+    mine = [own, after, opposite, before]
+    other = jnp.split(to_other_core(jnp.concatenate([own, after, before], axis=0)), 3, axis=0)
+    last = to_other_core(opposite)
+    theirs = [other[0], other[1], last, other[2]]
 
     vocab = lm_head.shape[0]
-    requests = everyone.shape[0]
+    requests = hidden_in.shape[0]
     offset = (((z * nx + x) * ny + y) * nc + c) * vocab
     logits, stats = pl.pallas_call(
         logits_kernel,
         out_shape=[jax.ShapeDtypeStruct((vocab, requests), f32), jax.ShapeDtypeStruct((2, requests), f32)],
-        in_specs=[IN_VMEM] * 3,
+        in_specs=[IN_VMEM] * (2 + 2 * ny),
         out_specs=[IN_VMEM] * 2,
+        scratch_shapes=[pltpu.VMEM((requests, lm_head.shape[1]), bf16)],
         compiler_params=SMALL,
         name="logits",
-    )(head, everyone, (tokens - offset)[None])
+    )(head, (tokens - offset)[None], *mine, *theirs)
 
     stats = spread(stats, ("x", "y", "c"), nx * ny * nc)
     top = jnp.max(stats[:, 0], axis=0)

time: 104 us -> 108 us (1.038)
  blocking collectives: 67.9 us -> 45.2 us
  waiting for transfers between devices: 2.05 us -> 19.4 us
  starting transfers between devices: 20.2 us -> 29.8 us
    all_to_all x1 -> x0, blocking collectives: 22.1 us -> none  [shards(): lax.all_to_all(half, ('x', 'y'), split_axis=0, concat_axis=0, tiled=False)]
    ppermute x1 -> x6, waiting for transfers between devices: 0.01 us -> 12 us  [the longest x4 10.8 us: along_y(): return lax.ppermute(block, 'y', [(i, (i + step) % ny) for i in range(ny)])]
    ppermute x1 -> x6, starting transfers between devices: 4.31 us -> 11.8 us  [the longest x2 8.4 us: to_other_core(): return lax.ppermute(block, 'c', [(i, 1 - i) for i in range(nc)])]
    ppermute x6 -> x9, waiting for transfers between devices: 2.04 us -> 6.63 us  [from_along_x(): return lax.ppermute(block, 'x', [(i, (i + step) % nx) for i in range(nx)])]
    ppermute x6 -> x9, starting transfers between devices: 8.54 us -> 10.8 us  [from_along_x(): return lax.ppermute(block, 'x', [(i, (i + step) % nx) for i in range(nx)])]
  transfers between devices with their start and end apart: 8 -> 16, of which waited for: 2 -> 11; matrix products, arithmetic and copies ran while one was open for 0% -> 0% of each run, Pallas kernels for 7% -> 7%
where the time goes in v6:
time: 108 us
  blocking collectives  45.2 us (42%)
  starting transfers between devices  29.8 us (28%)
  waiting for transfers between devices  19.4 us (18%)
  Pallas kernels  10.8 us (10%)
    all_to_all x2, blocking collectives, spread(): return lax.all_to_all(many, axes, split_axis=0, concat_axis=0, tiled=False)  19.5 us
    all_to_all x1, blocking collectives, shards(): lax.all_to_all(many, 'z', split_axis=0, concat_axis=0, tiled=False)  15.8 us
    ppermute x4, waiting for transfers between devices, along_y(): return lax.ppermute(block, 'y', [(i, (i + step) % ny) for i in range(ny)])  10.8 us
    ppermute x9, starting transfers between devices, from_along_x(): return lax.ppermute(block, 'x', [(i, (i + step) % nx) for i in range(nx)])  10.8 us
    all_to_all x1, blocking collectives, shards(): rows = lax.all_to_all(rows, 'z', split_axis=0, concat_axis=0, tiled=False)  9.94 us
    ppermute x2, starting transfers between devices, to_other_core(): return lax.ppermute(block, 'c', [(i, 1 - i) for i in range(nc)])  8.4 us
    all_to_all x1, starting transfers between devices, shards(): lax.all_to_all(partial, ('c', 'y'), split_axis=0, concat_axis=0, tiled=Fa...  7.31 us
    ppermute x9, waiting for transfers between devices, from_along_x(): return lax.ppermute(block, 'x', [(i, (i + step) % nx) for i in range(nx)])  6.63 us
  transfers between devices with their start and end apart: 16, of which 11 were waited for; matrix products, arithmetic and copies ran while one was open for 0% of the time, Pallas kernels for 7%

profile of v6, /device:TPU:1, one launch (start us, length us, event | category | flops | bytes accessed | tf_op | source)
XLA Modules:
  0.0 107.5 jit_solution(4073024797871129234)
XLA Ops:
  0.6 2.1 %collective-permute-start = (bf16[160,640]{1,0:T(8,128)(2,1)}, bf16[160,640]{1,0:T(8,128)(2,1)S(1)}, u32[]{:S(2)}, u32[]{:S(2)}) collective-permute-start(bf16[160,640]{1,0:T(8,128)(2,1)} %bitcast.27), channel_id=1, source_target_pairs={{0,8},{8,16},{16,24},{24,0},{1,9},{9,17},{17,25},{25,1},{2,10},{10... | collective-permute-start | bytes 614408 | tf_op jit(solution)/shard_map/ppermute | solution.py:227
  2.8 2.5 %collective-permute-start.1 = (bf16[160,640]{1,0:T(8,128)(2,1)}, bf16[160,640]{1,0:T(8,128)(2,1)S(1)}, u32[]{:S(2)}, u32[]{:S(2)}) collective-permute-start(bf16[160,640]{1,0:T(8,128)(2,1)} %bitcast.28), channel_id=1, source_target_pairs={{0,16},{8,24},{16,0},{24,8},{1,17},{9,25},{17,1},{25,9},{2,18},{10... | collective-permute-start | bytes 614408 | tf_op jit(solution)/shard_map/ppermute | solution.py:227
  5.2 1.2 %collective-permute-start.2 = (bf16[160,640]{1,0:T(8,128)(2,1)}, bf16[160,640]{1,0:T(8,128)(2,1)S(1)}, u32[]{:S(2)}, u32[]{:S(2)}) collective-permute-start(bf16[160,640]{1,0:T(8,128)(2,1)} %bitcast.29), channel_id=1, source_target_pairs={{0,24},{8,0},{16,8},{24,16},{1,25},{9,1},{17,9},{25,17},{2,26},{10... | collective-permute-start | bytes 614408 | tf_op jit(solution)/shard_map/ppermute | solution.py:227
  6.4 4.5 %attend.1 = (bf16[8,8,640]{2,1,0:T(8,128)(2,1)}, bf16[16,160]{1,0:T(8,128)(2,1)}, bf16[16,160]{1,0:T(8,128)(2,1)}, bf16[16,160]{1,0:T(8,128)(2,1)}, bf16[16,160]{1,0:T(8,128)(2,1)}) custom-call(s32[256]{0:T(256)} %lengths_ref.1, bf16[8,640]{1,0:T(8,128)(2,1)} %query_ref.1, bf16[8,2,128]{2,1,0:T(2,128)(2,1)} %new_ref.1, bf16[160,256]{1,0:T(8,128)(2,1)} %bitcast.22, ...), custom_call_target="tpu_custom_call" | custom-call | tf_op jit(solution)/shard_map/attend/pallas_call | solution.py:230
  11.0 15.8 %all_to_all.25 = bf16[8,8,640]{2,1,0:T(8,128)(2,1)S(1)} all-to-all(bf16[8,8,640]{2,1,0:T(8,128)(2,1)} %get-tuple-element.16), channel_id=1, replica_groups=mesh['z'=8,'x'=4,'y'=4,'c'=2] {'z'}, dimensions={0} | all-to-all | bytes 163840 | tf_op jit(solution)/shard_map/all_to_all | solution.py:246
  26.8 0.0 collective-permute-done
  26.8 0.0 collective-permute-done.1
  26.8 0.0 collective-permute-done.2
  26.8 1.1 fusion
  27.9 7.3 %all-to-all-start.1 = ((f32[8,8,640]{2,1,0:T(8,128)}), f32[8,8,640]{2,1,0:T(8,128)S(1)}, u32[]{:S(2)}, u32[]{:S(2)}) async-start(f32[8,8,640]{2,1,0:T(8,128)} %fusion), calls=%async_computation.1 | async-start | bytes 327680 | tf_op jit(solution)/shard_map/all_to_all | solution.py:252
  35.2 0.3 collective-permute-start.3
  35.5 0.6 collective-permute-start.4
  36.1 1.9 %collective-permute-start.5 = (bf16[16,160]{1,0:T(8,128)(2,1)S(1)}, bf16[16,160]{1,0:T(8,128)(2,1)S(1)}, u32[]{:S(2)}, u32[]{:S(2)}) collective-permute-start(bf16[16,160]{1,0:T(8,128)(2,1)S(1)} %copy-done.4), channel_id=1, source_target_pairs={{0,24},{8,0},{16,8},{24,16},{1,25},{9,1},{17,9},{25,17},{2,26},{10... | collective-permute-start | bytes 15368 | tf_op jit(solution)/shard_map/ppermute | solution.py:227
  38.0 0.9 collective-permute-done.3.refs_1_
  38.9 0.9 collective-permute-done.4.refs_2_
  39.8 0.1 collective-permute-done.5.refs_3_
  39.9 0.8 all-to-all-done.1.partial_ref
  40.7 0.0 copy-done
  40.7 0.2 resid.1
  40.9 9.9 %all_to_all.26.rows_ref = bf16[8,8,768]{2,1,0:T(8,128)(2,1)S(1)} all-to-all(bf16[8,8,768]{2,1,0:T(8,128)(2,1)S(1)} %resid.1), channel_id=1, replica_groups=mesh['z'=8,'x'=4,'y'=4,'c'=2] {'z'}, dimensions={0} | all-to-all | bytes 196608 | tf_op jit(solution)/shard_map/all_to_all | solution.py:263
  50.9 0.1 norm.1.refs_0_
  51.0 1.3 %collective-permute-start.6 = (bf16[8,5120]{1,0:T(8,128)(2,1)S(1)}, bf16[8,5120]{1,0:T(8,128)(2,1)S(1)}, u32[]{:S(2)}, u32[]{:S(2)}) collective-permute-start(bf16[8,5120]{1,0:T(8,128)(2,1)S(1)} %norm.1.refs_0_), channel_id=1, source_target_pairs={{0,24},{8,0},{16,8},{24,16},{1,25},{9,1},{17,9},{25,17},{2,26},{10... | collective-permute-start | bytes 245768 | tf_op jit(solution)/shard_map/ppermute | solution.py:227
  52.3 0.9 collective-permute-start.7
  53.2 0.0 collective-permute-start.8
  53.2 1.2 %collective-permute-done.6.refs_1_ = bf16[8,5120]{1,0:T(8,128)(2,1)S(1)} collective-permute-done((bf16[8,5120]{1,0:T(8,128)(2,1)S(1)}, bf16[8,5120]{1,0:T(8,128)(2,1)S(1)}, u32[]{:S(2)}, u32[]{:S(2)}) %collective-permute-start.6) | collective-permute-done | bytes 81952 | tf_op jit(solution)/shard_map/ppermute | solution.py:227
  54.4 2.7 %collective-permute-done.7.refs_2_ = bf16[8,5120]{1,0:T(8,128)(2,1)S(1)} collective-permute-done((bf16[8,5120]{1,0:T(8,128)(2,1)S(1)}, bf16[8,5120]{1,0:T(8,128)(2,1)S(1)}, u32[]{:S(2)}, u32[]{:S(2)}) %collective-permute-start.7) | collective-permute-done | bytes 81952 | tf_op jit(solution)/shard_map/ppermute | solution.py:227
  57.1 0.9 collective-permute-done.8.refs_3_
  58.0 0.1 order.1.after_ref.refs_0_
  58.1 2.7 %collective-permute-start.10 = (bf16[32,5120]{1,0:T(8,128)(2,1)S(1)}, bf16[32,5120]{1,0:T(8,128)(2,1)S(1)}, u32[]{:S(2)}, u32[]{:S(2)}) collective-permute-start(bf16[32,5120]{1,0:T(8,128)(2,1)S(1)} %order.1.after_ref.refs_0_), channel_id=1, source_target_pairs={{0,6},{2,0},{4,2},{6,4},{1,7},{3,1},{5,3},{7,5},{8,14},{10,8},{12,... | collective-permute-start | bytes 983048 | tf_op jit(solution)/shard_map/ppermute | solution.py:283
  60.8 0.0 collective-permute-start.9
  60.8 2.8 %fetch.1.head_ref = bf16[594,5120]{1,0:T(8,128)(2,1)S(1)} custom-call(bf16[594,5120]{1,0:T(8,128)(2,1)} %head_hbm.1, bf16[32,5120]{1,0:T(8,128)(2,1)S(1)} %order.1.after_ref.refs_0_), custom_call_target="tpu_custom_call" | custom-call | tf_op jit(solution)/shard_map/fetch/pallas_call | solution.py:289
  63.6 1.2 %collective-permute-done.10.refs_1_ = bf16[32,5120]{1,0:T(8,128)(2,1)S(1)} collective-permute-done((bf16[32,5120]{1,0:T(8,128)(2,1)S(1)}, bf16[32,5120]{1,0:T(8,128)(2,1)S(1)}, u32[]{:S(2)}, u32[]{:S(2)}) %collective-permute-start.10) | collective-permute-done | bytes 327712 | tf_op jit(solution)/shard_map/ppermute | solution.py:283
  64.8 3.1 %collective-permute-done.9.refs_3_ = bf16[32,5120]{1,0:T(8,128)(2,1)S(1)} collective-permute-done((bf16[32,5120]{1,0:T(8,128)(2,1)S(1)}, bf16[32,5120]{1,0:T(8,128)(2,1)S(1)}, u32[]{:S(2)}, u32[]{:S(2)}) %collective-permute-start.9) | collective-permute-done | bytes 327712 | tf_op jit(solution)/shard_map/ppermute | solution.py:283
  68.0 0.1 collective-permute-start.11
  68.1 0.1 pad_maximum_fusion
  68.2 7.3 %collective-permute-start.13 = (bf16[96,5120]{1,0:T(8,128)(2,1)S(1)}, bf16[96,5120]{1,0:T(8,128)(2,1)S(1)}, u32[]{:S(2)}, u32[]{:S(2)}) collective-permute-start(bf16[96,5120]{1,0:T(8,128)(2,1)S(1)} %pad_maximum_fusion), channel_id=1, source_target_pairs={{0,1},{1,0},{2,3},{3,2},{4,5},{5,4},{6,7},{7,6},{8,9},{9,8},{10,11... | collective-permute-start | bytes 2949128 | tf_op jit(solution)/shard_map/ppermute | solution.py:286
  75.4 0.5 collective-permute-start.12
  76.0 0.0 collective-permute-done.11
  76.0 6.4 %collective-permute-done.12 = bf16[16,5120]{1,0:T(8,128)(2,1)S(1)} collective-permute-done((bf16[16,5120]{1,0:T(8,128)(2,1)S(1)}, bf16[16,5120]{1,0:T(8,128)(2,1)S(1)}, u32[]{:S(2)}, u32[]{:S(2)}) %collective-permute-start.12) | collective-permute-done | bytes 163872 | tf_op jit(solution)/shard_map/ppermute | solution.py:283
  82.4 1.1 %collective-permute-start.14 = (bf16[32,5120]{1,0:T(8,128)(2,1)S(1)}, bf16[32,5120]{1,0:T(8,128)(2,1)S(1)}, u32[]{:S(2)}, u32[]{:S(2)}) collective-permute-start(bf16[32,5120]{1,0:T(8,128)(2,1)S(1)} %constant_dynamic-update-slice_fusion.refs_2_), channel_id=1, source_target_pairs={{0,1},{1,0},{2,3},{3,2},{4,5},{5,4},{6,7},{7,6},{8,9},{9,8},{10,11... | collective-permute-start | bytes 983048 | tf_op jit(solution)/shard_map/ppermute | solution.py:286
  83.5 0.0 collective-permute-done.13
  83.5 0.1 fusion.10
  83.6 1.2 %collective-permute-done.14.refs_6_ = bf16[32,5120]{1,0:T(8,128)(2,1)S(1)} collective-permute-done((bf16[32,5120]{1,0:T(8,128)(2,1)S(1)}, bf16[32,5120]{1,0:T(8,128)(2,1)S(1)}, u32[]{:S(2)}, u32[]{:S(2)}) %collective-permute-start.14) | collective-permute-done | bytes 327712 | tf_op jit(solution)/shard_map/ppermute | solution.py:286
  84.8 2.2 %logits.1 = (f32[594,256]{1,0:T(8,128)S(1)}, f32[2,256]{1,0:T(2,128)S(1)}) custom-call(bf16[594,5120]{1,0:T(8,128)(2,1)S(1)} %fetch.1.head_ref, s32[1,256]{1,0:T(1,128)S(1)} %bitcast.20, bf16[32,5120]{1,0:T(8,128)(2,1)S(1)} %order.1.after_ref.refs_0_, bf16[32,5120]{1,0:T(8,128)(2,1)S(1)} %collective-permute-done.10.refs_1_, ...), custom_call_target="tpu_custom_call" | custom-call | tf_op jit(solution)/shard_map/logits/pallas_call | solution.py:310
  87.0 10.5 %all_to_all.27 = f32[32,2,256]{2,1,0:T(2,128)S(1)} all-to-all(f32[32,2,256]{2,1,0:T(2,128)S(1)} %broadcast_in_dim.24), channel_id=1, replica_groups=mesh['z'=8,'x'=4,'y'=4,'c'=2] {'x','y','c'}, dimensions={0} | all-to-all | bytes 131072 | tf_op jit(solution)/shard_map/all_to_all | solution.py:216
  97.5 0.1 slice_reduce_fusion.1
  97.6 9.0 %all_to_all.28.stats_ref = f32[8,2,256]{2,1,0:T(2,128)S(1)} all-to-all(f32[8,2,256]{2,1,0:T(2,128)S(1)} %broadcast_in_dim.25), channel_id=1, replica_groups=mesh['z'=8,'x'=4,'y'=4,'c'=2] {'z'}, dimensions={0} | all-to-all | bytes 32768 | tf_op jit(solution)/shard_map/all_to_all | solution.py:216
  106.6 0.9 final.1
  (23 shorter events, 0.2 us)
Async XLA Ops:
  0.6 26.2 %collective-permute-start = (bf16[160,640]{1,0:T(8,128)(2,1)}, bf16[160,640]{1,0:T(8,128)(2,1)S(1)}, u32[]{:S(2)}, u32[]{:S(2)}) collective-permute-start(bf16[160,640]{1,0:T(8,128)(2,1)} %bitcast.27), channel_id=1, source_target_pairs={{0,8},{8,16},{16,24},{24,0},{1,9},{9,17},{17,25},{25,1},{2,10},{10... | collective-permute-start | bytes 614408 | tf_op jit(solution)/shard_map/ppermute | solution.py:227
  2.8 24.0 %collective-permute-start.1 = (bf16[160,640]{1,0:T(8,128)(2,1)}, bf16[160,640]{1,0:T(8,128)(2,1)S(1)}, u32[]{:S(2)}, u32[]{:S(2)}) collective-permute-start(bf16[160,640]{1,0:T(8,128)(2,1)} %bitcast.28), channel_id=1, source_target_pairs={{0,16},{8,24},{16,0},{24,8},{1,17},{9,25},{17,1},{25,9},{2,18},{10... | collective-permute-start | bytes 614408 | tf_op jit(solution)/shard_map/ppermute | solution.py:227
  5.2 21.6 %collective-permute-start.2 = (bf16[160,640]{1,0:T(8,128)(2,1)}, bf16[160,640]{1,0:T(8,128)(2,1)S(1)}, u32[]{:S(2)}, u32[]{:S(2)}) collective-permute-start(bf16[160,640]{1,0:T(8,128)(2,1)} %bitcast.29), channel_id=1, source_target_pairs={{0,24},{8,0},{16,8},{24,16},{1,25},{9,1},{17,9},{25,17},{2,26},{10... | collective-permute-start | bytes 614408 | tf_op jit(solution)/shard_map/ppermute | solution.py:227
  6.4 20.5 %copy-start.3 = (bf16[640,160]{0,1:T(8,128)(2,1)S(1)}, bf16[640,160]{0,1:T(8,128)(2,1)}, u32[]{:S(2)}) copy-start(bf16[640,160]{0,1:T(8,128)(2,1)} %param.15) | copy-start | bytes 614404
  10.9 24.3 %copy-start.6 = (bf16[16,160]{1,0:T(8,128)(2,1)S(1)}, bf16[16,160]{1,0:T(8,128)(2,1)}, u32[]{:S(2)}) copy-start(bf16[16,160]{1,0:T(8,128)(2,1)} %get-tuple-element.18) | copy-start | bytes 15364
  10.9 24.6 %copy-start.5 = (bf16[16,160]{1,0:T(8,128)(2,1)S(1)}, bf16[16,160]{1,0:T(8,128)(2,1)}, u32[]{:S(2)}) copy-start(bf16[16,160]{1,0:T(8,128)(2,1)} %get-tuple-element.19) | copy-start | bytes 15364
  10.9 25.2 %copy-start.4 = (bf16[16,160]{1,0:T(8,128)(2,1)S(1)}, bf16[16,160]{1,0:T(8,128)(2,1)}, u32[]{:S(2)}) copy-start(bf16[16,160]{1,0:T(8,128)(2,1)} %get-tuple-element.20) | copy-start | bytes 15364
  10.9 29.7 %copy-start = (bf16[16,160]{1,0:T(8,128)(2,1)S(1)}, bf16[16,160]{1,0:T(8,128)(2,1)}, u32[]{:S(2)}) copy-start(bf16[16,160]{1,0:T(8,128)(2,1)} %get-tuple-element.17.refs_0_) | copy-start | bytes 15364
  26.8 34.0 %copy-start.2 = (s32[256]{0:T(256)S(1)}, s32[256]{0:T(256)}, u32[]{:S(2)}) copy-start(s32[256]{0:T(256)} %param.18) | copy-start | bytes 3076
  27.9 12.8 %all-to-all-start.1 = ((f32[8,8,640]{2,1,0:T(8,128)}), f32[8,8,640]{2,1,0:T(8,128)S(1)}, u32[]{:S(2)}, u32[]{:S(2)}) async-start(f32[8,8,640]{2,1,0:T(8,128)} %fusion), calls=%async_computation.1 | async-start | bytes 327680 | tf_op jit(solution)/shard_map/all_to_all | solution.py:252
  35.2 3.7 %collective-permute-start.3 = (bf16[16,160]{1,0:T(8,128)(2,1)S(1)}, bf16[16,160]{1,0:T(8,128)(2,1)S(1)}, u32[]{:S(2)}, u32[]{:S(2)}) collective-permute-start(bf16[16,160]{1,0:T(8,128)(2,1)S(1)} %copy-done.6), channel_id=1, source_target_pairs={{0,8},{8,16},{16,24},{24,0},{1,9},{9,17},{17,25},{25,1},{2,10},{10... | collective-permute-start | bytes 15368 | tf_op jit(solution)/shard_map/ppermute | solution.py:227
  35.5 4.3 %collective-permute-start.4 = (bf16[16,160]{1,0:T(8,128)(2,1)S(1)}, bf16[16,160]{1,0:T(8,128)(2,1)S(1)}, u32[]{:S(2)}, u32[]{:S(2)}) collective-permute-start(bf16[16,160]{1,0:T(8,128)(2,1)S(1)} %copy-done.5), channel_id=1, source_target_pairs={{0,16},{8,24},{16,0},{24,8},{1,17},{9,25},{17,1},{25,9},{2,18},{10... | collective-permute-start | bytes 15368 | tf_op jit(solution)/shard_map/ppermute | solution.py:227
  36.1 3.8 %collective-permute-start.5 = (bf16[16,160]{1,0:T(8,128)(2,1)S(1)}, bf16[16,160]{1,0:T(8,128)(2,1)S(1)}, u32[]{:S(2)}, u32[]{:S(2)}) collective-permute-start(bf16[16,160]{1,0:T(8,128)(2,1)S(1)} %copy-done.4), channel_id=1, source_target_pairs={{0,24},{8,0},{16,8},{24,16},{1,25},{9,1},{17,9},{25,17},{2,26},{10... | collective-permute-start | bytes 15368 | tf_op jit(solution)/shard_map/ppermute | solution.py:227
  51.0 3.4 %collective-permute-start.6 = (bf16[8,5120]{1,0:T(8,128)(2,1)S(1)}, bf16[8,5120]{1,0:T(8,128)(2,1)S(1)}, u32[]{:S(2)}, u32[]{:S(2)}) collective-permute-start(bf16[8,5120]{1,0:T(8,128)(2,1)S(1)} %norm.1.refs_0_), channel_id=1, source_target_pairs={{0,24},{8,0},{16,8},{24,16},{1,25},{9,1},{17,9},{25,17},{2,26},{10... | collective-permute-start | bytes 245768 | tf_op jit(solution)/shard_map/ppermute | solution.py:227
  52.3 4.8 %collective-permute-start.7 = (bf16[8,5120]{1,0:T(8,128)(2,1)S(1)}, bf16[8,5120]{1,0:T(8,128)(2,1)S(1)}, u32[]{:S(2)}, u32[]{:S(2)}) collective-permute-start(bf16[8,5120]{1,0:T(8,128)(2,1)S(1)} %norm.1.refs_0_), channel_id=1, source_target_pairs={{0,16},{8,24},{16,0},{24,8},{1,17},{9,25},{17,1},{25,9},{2,18},{10... | collective-permute-start | bytes 245768 | tf_op jit(solution)/shard_map/ppermute | solution.py:227
  53.2 4.8 %collective-permute-start.8 = (bf16[8,5120]{1,0:T(8,128)(2,1)S(1)}, bf16[8,5120]{1,0:T(8,128)(2,1)S(1)}, u32[]{:S(2)}, u32[]{:S(2)}) collective-permute-start(bf16[8,5120]{1,0:T(8,128)(2,1)S(1)} %norm.1.refs_0_), channel_id=1, source_target_pairs={{0,8},{8,16},{16,24},{24,0},{1,9},{9,17},{17,25},{25,1},{2,10},{10... | collective-permute-start | bytes 245768 | tf_op jit(solution)/shard_map/ppermute | solution.py:227
  58.1 6.7 %collective-permute-start.10 = (bf16[32,5120]{1,0:T(8,128)(2,1)S(1)}, bf16[32,5120]{1,0:T(8,128)(2,1)S(1)}, u32[]{:S(2)}, u32[]{:S(2)}) collective-permute-start(bf16[32,5120]{1,0:T(8,128)(2,1)S(1)} %order.1.after_ref.refs_0_), channel_id=1, source_target_pairs={{0,6},{2,0},{4,2},{6,4},{1,7},{3,1},{5,3},{7,5},{8,14},{10,8},{12,... | collective-permute-start | bytes 983048 | tf_op jit(solution)/shard_map/ppermute | solution.py:283
  60.8 7.1 %collective-permute-start.9 = (bf16[32,5120]{1,0:T(8,128)(2,1)S(1)}, bf16[32,5120]{1,0:T(8,128)(2,1)S(1)}, u32[]{:S(2)}, u32[]{:S(2)}) collective-permute-start(bf16[32,5120]{1,0:T(8,128)(2,1)S(1)} %order.1.after_ref.refs_0_), channel_id=1, source_target_pairs={{0,2},{2,4},{4,6},{6,0},{1,3},{3,5},{5,7},{7,1},{8,10},{10,12},{12... | collective-permute-start | bytes 983048 | tf_op jit(solution)/shard_map/ppermute | solution.py:283
  68.0 8.0 %collective-permute-start.11 = (bf16[16,5120]{1,0:T(8,128)(2,1)S(1)}, bf16[16,5120]{1,0:T(8,128)(2,1)S(1)}, u32[]{:S(2)}, u32[]{:S(2)}) collective-permute-start(bf16[16,5120]{1,0:T(8,128)(2,1)S(1)} %slice.13), channel_id=1, source_target_pairs={{0,6},{2,0},{4,2},{6,4},{1,7},{3,1},{5,3},{7,5},{8,14},{10,8},{12,... | collective-permute-start | bytes 491528 | tf_op jit(solution)/shard_map/ppermute | solution.py:283
  68.2 15.4 %collective-permute-start.13 = (bf16[96,5120]{1,0:T(8,128)(2,1)S(1)}, bf16[96,5120]{1,0:T(8,128)(2,1)S(1)}, u32[]{:S(2)}, u32[]{:S(2)}) collective-permute-start(bf16[96,5120]{1,0:T(8,128)(2,1)S(1)} %pad_maximum_fusion), channel_id=1, source_target_pairs={{0,1},{1,0},{2,3},{3,2},{4,5},{5,4},{6,7},{7,6},{8,9},{9,8},{10,11... | collective-permute-start | bytes 2949128 | tf_op jit(solution)/shard_map/ppermute | solution.py:286
  75.4 7.0 %collective-permute-start.12 = (bf16[16,5120]{1,0:T(8,128)(2,1)S(1)}, bf16[16,5120]{1,0:T(8,128)(2,1)S(1)}, u32[]{:S(2)}, u32[]{:S(2)}) collective-permute-start(bf16[16,5120]{1,0:T(8,128)(2,1)S(1)} %slice.14), channel_id=1, source_target_pairs={{0,2},{2,4},{4,6},{6,0},{1,3},{3,5},{5,7},{7,1},{8,10},{10,12},{12... | collective-permute-start | bytes 491528 | tf_op jit(solution)/shard_map/ppermute | solution.py:283
  82.4 2.4 %collective-permute-start.14 = (bf16[32,5120]{1,0:T(8,128)(2,1)S(1)}, bf16[32,5120]{1,0:T(8,128)(2,1)S(1)}, u32[]{:S(2)}, u32[]{:S(2)}) collective-permute-start(bf16[32,5120]{1,0:T(8,128)(2,1)S(1)} %constant_dynamic-update-slice_fusion.refs_2_), channel_id=1, source_target_pairs={{0,1},{1,0},{2,3},{3,2},{4,5},{5,4},{6,7},{7,6},{8,9},{9,8},{10,11... | collective-permute-start | bytes 983048 | tf_op jit(solution)/shard_map/ppermute | solution.py:286
  84.8 21.8 %copy-start.1 = (f32[256]{0:T(256)S(1)}, f32[256]{0:T(256)}, u32[]{:S(2)}) copy-start(f32[256]{0:T(256)} %param.19) | copy-start | bytes 3076

commit v7 on v4

--- a/solution.py
+++ b/solution.py
@@ -42,37 +42,52 @@
     return first, second, third
 
 
-def tails_of(count, part, x, hidden_ref, gain_ref, tail_refs):
-    columns, requests = hidden_ref.shape
-    row = lax.broadcasted_iota(jnp.int32, (count, requests), 0)
-    lane = lax.broadcasted_iota(jnp.int32, (count, requests), 1)
-    parts = three_parts(gain_ref[...])
-    below = jnp.concatenate(parts + (jnp.zeros((TAIL - count - 3, columns), f32),), axis=0)
-    for step, tail_ref in enumerate(tail_refs):
-        target = lax.rem(x + step, len(tail_refs))
-        place = (part * len(tail_refs) + target) * count
-        chosen = jnp.where(lane == row + place, 1.0, 0.0).astype(bf16)
-        hidden = lax.dot_general(
-            chosen, hidden_ref[...], (((1,), (1,)), ((), ())), preferred_element_type=f32
-        )
-        tail_ref[...] = jnp.concatenate([hidden, below], axis=0).astype(bf16)
-
-
-def attend_kernel(group, sizes, lengths_ref, query_ref, new_ref, hidden_ref, gain_ref, cache_ref, *refs):
-    out_ref, tail_refs, (slots_ref, rows_ref, sums_ref, sems) = refs[0], refs[1:-4], refs[-4:]
+def side_by_side(rows):
+    return jnp.concatenate([rows[k : k + 8] for k in range(0, rows.shape[0], 8)], axis=1)
+
+
+def pack_kernel(sizes, table_hbm, hidden_hbm, gain_hbm, pack_hbm, hidden_ref, gain_ref, tail_ref, sems):
+    columns, heads = table_hbm.shape
+    table = pltpu.make_async_copy(table_hbm, pack_hbm.at[pl.ds(0, columns)], sems.at[0])
+    hidden = pltpu.make_async_copy(hidden_hbm, hidden_ref, sems.at[1])
+    gain = pltpu.make_async_copy(gain_hbm, gain_ref, sems.at[2])
+    hidden.start()
+    gain.start()
+    table.start()
+    rows, requests = heads // columns * 8, hidden_ref.shape[1]
+    part = lax.axis_index("c") * sizes["y"] + lax.axis_index("y")
+    row = lax.broadcasted_iota(jnp.int32, (rows, requests), 0)
+    lane = lax.broadcasted_iota(jnp.int32, (rows, requests), 1)
+    chosen = jnp.where(lane == row + part * rows, 1.0, 0.0).astype(bf16)
+    hidden.wait()
+    gain.wait()
+    picked = lax.dot_general(
+        chosen, hidden_ref[...], (((1,), (1,)), ((), ())), preferred_element_type=f32
+    )
+    below = jnp.concatenate(three_parts(gain_ref[...]) + (jnp.zeros((5, columns), f32),), axis=0)
+    below = jnp.concatenate([below, jnp.zeros((8, heads - columns), f32)], axis=1)
+    tail_ref[...] = jnp.concatenate([side_by_side(picked), below], axis=0).astype(bf16)
+    tail = pltpu.make_async_copy(tail_ref, pack_hbm.at[pl.ds(columns, TAIL)], sems.at[3])
+    tail.start()
+    table.wait()
+    tail.wait()
+
+
+def attend_kernel(group, sizes, lengths_ref, query_ref, new_ref, cache_ref, out_ref, slots_ref, rows_ref, sums_ref, sems):
     count, _, slots, head_dim = cache_ref.shape
-    z, x, y, c = (lax.axis_index(a) for a in ("z", "x", "y", "c"))
+    z, x = lax.axis_index("z"), lax.axis_index("x")
     scale = head_dim ** (-0.5)
+    portions = [range(k, k + count // 2) for k in (0, count // 2)]
     loads = [
         [
             pltpu.make_async_copy(cache_ref.at[r, kind], slots_ref.at[r, kind], sems.at[kind, r])
-            for r in range(count)
+            for r in portion
         ]
+        for portion in portions
         for kind in range(2)
     ]
-    for load in loads[0]:
+    for load in sum(loads, []):
         load.start()
-    tails_of(count, c * sizes["y"] + y, x, hidden_ref, gain_ref, tail_refs)
 
     query = query_ref[...].astype(f32)
     fresh = new_ref[...].astype(f32)
@@ -81,59 +96,62 @@
         rows_ref[pl.ds(g, count, stride=8), :] = query[:, g * head_dim : (g + 1) * head_dim]
     heads = rows_ref[...]
     new_keys = jnp.concatenate([jnp.broadcast_to(fresh[r, 0:1], (8, head_dim)) for r in range(count)], axis=0)
-    own_score = jnp.sum(heads * new_keys, axis=1, keepdims=True) * scale
+    own_scores = jnp.sum(heads * new_keys, axis=1, keepdims=True) * scale
     heads = heads.astype(bf16)
     position = lax.broadcasted_iota(jnp.int32, (8, slots), 1)
     base = (z * sizes["x"] + x) * count
-    for load in loads[0]:
-        load.wait()
-    for load in loads[1]:
-        load.start()
-    scores = []
-    for r in range(count):
-        score = lax.dot_general(
-            heads[8 * r : 8 * r + 8],
-            slots_ref[r, 0],
-            (((1,), (1,)), ((), ())),
-            preferred_element_type=f32,
-        )
-        scores.append(jnp.where(position < lengths_ref[base + r], score * scale, masked_score))
-    scores = jnp.concatenate(scores, axis=0)
-    top = jnp.maximum(jnp.max(scores, axis=1, keepdims=True), own_score)
-    weights = jnp.exp(scores - top)
-    own_weight = jnp.exp(own_score - top)
-    mass = jnp.sum(weights, axis=1, keepdims=True) + own_weight
-    parts = three_parts(weights)
-    for load in loads[1]:
-        load.wait()
-    for r in range(count):
-        span = slice(8 * r, 8 * r + 8)
-        stacked = jnp.concatenate([part[span] for part in parts], axis=0).astype(bf16)
-        sums = jnp.dot(stacked, slots_ref[r, 1], preferred_element_type=f32)
-        total = sums[:8] + sums[8:16] + sums[16:24] + own_weight[span] * fresh[r, 1:2]
-        sums_ref[span] = total / mass[span]
+    for portion, key_loads, value_loads in zip(portions, loads[::2], loads[1::2]):
+        for load in key_loads:
+            load.wait()
+        scores = []
+        for r in portion:
+            score = lax.dot_general(
+                heads[8 * r : 8 * r + 8],
+                slots_ref[r, 0],
+                (((1,), (1,)), ((), ())),
+                preferred_element_type=f32,
+            )
+            scores.append(jnp.where(position < lengths_ref[base + r], score * scale, masked_score))
+        scores = jnp.concatenate(scores, axis=0)
+        own_score = own_scores[8 * portion[0] : 8 * portion[0] + scores.shape[0]]
+        top = jnp.maximum(jnp.max(scores, axis=1, keepdims=True), own_score)
+        weights = jnp.exp(scores - top)
+        own_weight = jnp.exp(own_score - top)
+        mass = jnp.sum(weights, axis=1, keepdims=True) + own_weight
+        coarse = weights.astype(bf16)
+        fine = (weights - coarse.astype(f32)).astype(bf16)
+        for load in value_loads:
+            load.wait()
+        for k, r in enumerate(portion):
+            span = slice(8 * k, 8 * k + 8)
+            stacked = jnp.concatenate([coarse[span].astype(f32), fine[span].astype(f32)], axis=0).astype(bf16)
+            sums = jnp.dot(stacked, slots_ref[r, 1], preferred_element_type=f32)
+            total = sums[:8] + sums[8:16] + own_weight[span] * fresh[r, 1:2]
+            sums_ref[8 * r : 8 * r + 8] = total / mass[span]
     done = jnp.concatenate([sums_ref[pl.ds(g, count, stride=8), :] for g in range(group)], axis=1).astype(bf16)
     for k in range(out_ref.shape[0]):
         out_ref[k] = done
 
 
 def resid_kernel(partial_ref, *refs):
-    tails, out_ref = refs[:-1], refs[-1]
+    packs, out_ref = refs[:-1], refs[-1]
     count, width = partial_ref.shape[1:]
-    columns = width // len(tails)
+    columns = width // len(packs)
+    back = lax.rem(len(packs) - lax.axis_index("x"), len(packs)) * columns
     total = partial_ref[0]
     for k in range(1, partial_ref.shape[0]):
         total = total + partial_ref[k]
     squares = jnp.zeros((count, 1), f32)
     blocks = []
-    for step, tail_ref in enumerate(tails):
-        tail = tail_ref[...].astype(f32)
-        gain = tail[count : count + 1] + tail[count + 1 : count + 2] + tail[count + 2 : count + 3]
-        resid = total[:, step * columns : (step + 1) * columns] + tail[:count]
+    for step, pack_ref in enumerate(packs):
+        tail = pack_ref[columns:].astype(f32)
+        gain = (tail[count : count + 1] + tail[count + 1 : count + 2] + tail[count + 2 : count + 3])[:, :columns]
+        hidden = pltpu.roll(tail[:count], back, 1)[:, :columns]
+        resid = total[:, step * columns : (step + 1) * columns] + hidden
         resid = resid.astype(bf16).astype(f32)
         squares = squares + jnp.sum(resid * resid, axis=1, keepdims=True)
         blocks.append(resid * gain)
-    shift = lax.rem(lax.axis_index("x") + 1, len(tails)) * columns
+    shift = lax.rem(lax.axis_index("x") + 1, len(packs)) * columns
     ordered = pltpu.roll(jnp.concatenate(blocks[::-1], axis=1), shift, 1)
     lane = lax.broadcasted_iota(jnp.int32, (count, LANES), 1)
     spare = jnp.zeros((count, LANES), f32)
@@ -208,13 +226,27 @@
     def from_along_x(block, step):
         return lax.ppermute(block, "x", [(i, (i + step) % nx) for i in range(nx)])
 
-    table = jnp.concatenate([out_proj.T] + [from_along_x(out_proj.T, k) for k in range(1, nx)], axis=0)
-    many, *tails = pl.pallas_call(
+    pack = pl.pallas_call(
+        functools.partial(pack_kernel, sizes),
+        out_shape=jax.ShapeDtypeStruct((columns + TAIL, heads), bf16),
+        in_specs=[IN_PLACE] * 3,
+        out_specs=IN_PLACE,
+        scratch_shapes=[
+            pltpu.VMEM((columns, hidden_in.shape[0]), bf16),
+            pltpu.VMEM((1, columns), f32),
+            pltpu.VMEM((TAIL, heads), bf16),
+            pltpu.SemaphoreType.DMA((4,)),
+        ],
+        compiler_params=WHOLE,
+        name="pack",
+    )(out_proj.T, hidden_in.T, final_gain[None])
+    packs = [pack] + [from_along_x(pack, k) for k in range(1, nx)]
+    table = jnp.concatenate([out_proj.T] + [p[:columns] for p in packs[1:]], axis=0)
+    many = pl.pallas_call(
         functools.partial(attend_kernel, HEADS // KV_HEADS, sizes),
-        out_shape=[jax.ShapeDtypeStruct((nz,) + query.shape, bf16)]
-        + [jax.ShapeDtypeStruct((TAIL, columns), bf16)] * nx,
-        in_specs=[IN_SMEM] + [IN_VMEM] * 4 + [IN_PLACE],
-        out_specs=[IN_VMEM] * (nx + 1),
+        out_shape=jax.ShapeDtypeStruct((nz,) + query.shape, bf16),
+        in_specs=[IN_SMEM] + [IN_VMEM] * 2 + [IN_PLACE],
+        out_specs=IN_VMEM,
         scratch_shapes=[
             pltpu.VMEM(cache.shape, bf16),
             pltpu.VMEM((count * 8, HEAD_DIM), f32),
@@ -223,10 +255,8 @@
         ],
         compiler_params=WHOLE,
         name="attend",
-    )(lengths, query, new_kv, hidden_in.T, final_gain[None], cache)
-    tails = [tails[0]] + [from_along_x(tails[k], k) for k in range(1, nx)]
+    )(lengths, query, new_kv, cache)
     gathered = lax.all_to_all(many, "z", split_axis=0, concat_axis=0, tiled=False)
-    gathered, tails = lax.optimization_barrier((gathered, tails))
     gathered = gathered.reshape(nz * count, -1)
     partial = lax.dot_general(
         gathered, table, (((1,), (1,)), ((), ())), preferred_element_type=f32
@@ -242,7 +272,7 @@
         out_specs=IN_VMEM,
         compiler_params=SMALL,
         name="resid",
-    )(partial, *tails)
+    )(partial, *packs)
     rows = lax.all_to_all(rows, "z", split_axis=0, concat_axis=0, tiled=False)
     half = pl.pallas_call(
         norm_kernel,

time: 106 us -> 108 us (1.019)
  Pallas kernels: 11.3 us -> 17.9 us
  blocking collectives: 68.6 us -> 63.9 us
  starting transfers between devices: 20.3 us -> 16.1 us
  waiting for transfers between devices: 3.32 us -> 7.41 us
    pallas_call x0 -> x1, Pallas kernels: none -> 7.34 us  [shards(): pl.pallas_call(functools.partial(pack_kernel, sizes), out_shape=jax.Shape...]
    all_to_all x1, waiting for transfers between devices: 0.49 us -> 7.17 us  [shards(): lax.all_to_all(many, 'z', split_axis=0, concat_axis=0, tiled=False)]
    ppermute x6 -> x3, starting transfers between devices: 8.7 us -> 4.51 us  [from_along_x(): return lax.ppermute(block, 'x', [(i, (i + step) % nx) for i in range(nx)])]
    all_to_all x1, blocking collectives: 14.1 us -> 10 us  [shards(): rows = lax.all_to_all(rows, 'z', split_axis=0, concat_axis=0, tiled=False)]
    ppermute x6 -> x3, waiting for transfers between devices: 2.82 us -> 0.24 us  [from_along_x(): return lax.ppermute(block, 'x', [(i, (i + step) % nx) for i in range(nx)])]
  transfers between devices with their start and end apart: 8 -> 5, of which waited for: 4 -> 2; matrix products, arithmetic and copies ran while one was open for 0% -> 0% of each run, Pallas kernels for 8% -> 7%
where the time goes in v7:
time: 108 us; the launch traced here: 107 us
  blocking collectives  63.9 us (59%)
  Pallas kernels  17.9 us (17%)
  starting transfers between devices  16.1 us (15%)
  waiting for transfers between devices  7.41 us (7%)
    all_to_all x1, blocking collectives, shards(): lax.all_to_all(half, ('y', 'x'), split_axis=0, concat_axis=0, tiled=False)  21.7 us
    all_to_all x2, blocking collectives, spread(): return lax.all_to_all(many, axes, split_axis=0, concat_axis=0, tiled=False)  19.6 us
    all_to_all x1, blocking collectives, shards(): lax.all_to_all(partial, ('c', 'y'), split_axis=0, concat_axis=0, tiled=Fa...  12.6 us
    all_to_all x1, blocking collectives, shards(): rows = lax.all_to_all(rows, 'z', split_axis=0, concat_axis=0, tiled=False)  10 us
    all_to_all x1, starting transfers between devices, shards(): lax.all_to_all(many, 'z', split_axis=0, concat_axis=0, tiled=False)  8.2 us
    pallas_call x1, Pallas kernels, shards(): pl.pallas_call(functools.partial(pack_kernel, sizes), out_shape=jax.Shape...  7.34 us
    all_to_all x1, waiting for transfers between devices, shards(): lax.all_to_all(many, 'z', split_axis=0, concat_axis=0, tiled=False)  7.17 us
    ppermute x3, starting transfers between devices, from_along_x(): return lax.ppermute(block, 'x', [(i, (i + step) % nx) for i in range(nx)])  4.51 us
  transfers between devices with their start and end apart: 5, of which 2 were waited for; matrix products, arithmetic and copies ran while one was open for 0% of the time, Pallas kernels for 7%

profile of v7, /device:TPU:1, one launch (start us, length us, event | category | flops | bytes accessed | tf_op | source)
XLA Modules:
  0.0 107.1 jit_solution(10328714795051570407)
XLA Ops:
  0.6 7.3 %pack.1.refs_0_ = bf16[176,640]{1,0:T(8,128)(2,1)} custom-call(bf16[160,640]{1,0:T(8,128)(2,1)} %bitcast.27, bf16[160,256]{1,0:T(8,128)(2,1)} %bitcast.29, f32[1,160]{1,0:T(1,128)} %bitcast.32), custom_call_target="tpu_custom_call" | custom-call | tf_op jit(solution)/shard_map/pack/pallas_call | solution.py:229
  8.0 0.0 copy-start.2
  8.0 3.4 %collective-permute-start.2 = (bf16[176,640]{1,0:T(8,128)(2,1)}, bf16[176,640]{1,0:T(8,128)(2,1)S(1)}, u32[]{:S(2)}, u32[]{:S(2)}) collective-permute-start(bf16[176,640]{1,0:T(8,128)(2,1)} %pack.1.refs_0_), channel_id=1, source_target_pairs={{0,24},{8,0},{16,8},{24,16},{1,25},{9,1},{17,9},{25,17},{2,26},{10... | collective-permute-start | bytes 675848 | tf_op jit(solution)/shard_map/ppermute | solution.py:227
  11.4 0.5 collective-permute-start.1
  11.9 0.6 collective-permute-start
  12.5 4.3 %attend.1 = bf16[8,8,640]{2,1,0:T(8,128)(2,1)} custom-call(s32[256]{0:T(256)} %lengths_ref.1, bf16[8,640]{1,0:T(8,128)(2,1)} %query_ref.1, bf16[8,2,128]{2,1,0:T(2,128)(2,1)} %new_ref.1, bf16[8,2,1024,128]{3,2,1,0:T(8,128)(2,1)} %cache_ref.1), custom_call_target="tpu_custom_call" | custom-call | tf_op jit(solution)/shard_map/attend/pallas_call | solution.py:245
  16.9 8.2 %all-to-all-start = ((bf16[8,8,640]{2,1,0:T(8,128)(2,1)}), bf16[8,8,640]{2,1,0:T(8,128)(2,1)S(1)}, u32[]{:S(2)}, u32[]{:S(2)}) async-start(bf16[8,8,640]{2,1,0:T(8,128)(2,1)} %attend.1), calls=%async_computation | async-start | bytes 163840 | tf_op jit(solution)/shard_map/all_to_all | solution.py:259
  25.1 0.0 collective-permute-done.2.refs_3_
  25.1 0.0 collective-permute-done.1.refs_2_
  25.1 0.2 collective-permute-done.refs_1_
  25.4 0.0 copy-start
  25.4 7.2 %all-to-all-done = bf16[8,8,640]{2,1,0:T(8,128)(2,1)S(1)} async-done(((bf16[8,8,640]{2,1,0:T(8,128)(2,1)}), bf16[8,8,640]{2,1,0:T(8,128)(2,1)S(1)}, u32[]{:S(2)}, u32[]{:S(2)}) %all-to-all-start) | async-done | bytes 81952 | tf_op jit(solution)/shard_map/all_to_all | solution.py:259
  32.6 0.0 copy-done.2
  32.6 0.4 fusion
  32.9 12.6 %all_to_all.30.partial_ref = f32[8,8,640]{2,1,0:T(8,128)S(1)} all-to-all(f32[8,8,640]{2,1,0:T(8,128)S(1)} %fusion), channel_id=1, replica_groups=mesh['z'=8,'x'=4,'y'=4,'c'=2] {'c','y'}, dimensions={0} | all-to-all | bytes 327680 | tf_op jit(solution)/shard_map/all_to_all | solution.py:265
  45.6 0.0 copy-done
  45.6 0.3 resid.1
  45.9 10.0 %all_to_all.31.rows_ref = bf16[8,8,768]{2,1,0:T(8,128)(2,1)S(1)} all-to-all(bf16[8,8,768]{2,1,0:T(8,128)(2,1)S(1)} %resid.1), channel_id=1, replica_groups=mesh['z'=8,'x'=4,'y'=4,'c'=2] {'z'}, dimensions={0} | all-to-all | bytes 196608 | tf_op jit(solution)/shard_map/all_to_all | solution.py:276
  55.9 0.2 norm.1
  56.2 0.0 copy-start.3
  56.2 21.7 %all_to_all.32 = bf16[16,8,5120]{2,1,0:T(8,128)(2,1)S(1)} all-to-all(bf16[16,8,5120]{2,1,0:T(8,128)(2,1)S(1)} %norm.1), channel_id=1, replica_groups=mesh['z'=8,'x'=4,'y'=4,'c'=2] {'y','x'}, dimensions={0} | all-to-all | bytes 2621440 | tf_op jit(solution)/shard_map/all_to_all | solution.py:285
  77.8 3.4 %collective-permute-start.3 = (bf16[128,5120]{1,0:T(8,128)(2,1)S(1)}, bf16[128,5120]{1,0:T(8,128)(2,1)S(1)}, u32[]{:S(2)}, u32[]{:S(2)}) collective-permute-start(bf16[128,5120]{1,0:T(8,128)(2,1)S(1)} %bitcast.23), channel_id=1, source_target_pairs={{0,1},{1,0},{2,3},{3,2},{4,5},{5,4},{6,7},{7,6},{8,9},{9,8},{10,11... | collective-permute-start | bytes 3932168 | tf_op jit(solution)/shard_map/ppermute | solution.py:287
  81.2 0.0 copy-done.3
  81.2 2.8 %fetch.1.head_ref = bf16[594,5120]{1,0:T(8,128)(2,1)S(1)} custom-call(bf16[594,5120]{1,0:T(8,128)(2,1)} %head_hbm.1, bf16[128,5120]{1,0:T(8,128)(2,1)S(1)} %bitcast.24), custom_call_target="tpu_custom_call" | custom-call | tf_op jit(solution)/shard_map/fetch/pallas_call | solution.py:288
  84.0 0.0 collective-permute-done.3
  84.0 0.2 broadcast_select_fusion.1
  84.2 0.2 pad_maximum_fusion.rows_ref
  84.4 0.0 copy-start.1
  84.4 2.0 %logits.1 = (f32[594,256]{1,0:T(8,128)S(1)}, f32[2,256]{1,0:T(2,128)S(1)}) custom-call(bf16[594,5120]{1,0:T(8,128)(2,1)S(1)} %fetch.1.head_ref, bf16[256,5120]{1,0:T(8,128)(2,1)S(1)} %pad_maximum_fusion.rows_ref, s32[1,256]{1,0:T(1,128)S(1)} %bitcast.25), custom_call_target="tpu_custom_call" | custom-call | tf_op jit(solution)/shard_map/logits/pallas_call | solution.py:305
  86.4 10.6 %all_to_all.33 = f32[32,2,256]{2,1,0:T(2,128)S(1)} all-to-all(f32[32,2,256]{2,1,0:T(2,128)S(1)} %broadcast_in_dim.24), channel_id=1, replica_groups=mesh['z'=8,'x'=4,'y'=4,'c'=2] {'x','y','c'}, dimensions={0} | all-to-all | bytes 131072 | tf_op jit(solution)/shard_map/all_to_all | solution.py:216
  97.0 0.1 slice_reduce_fusion.1
  97.2 9.0 %all_to_all.34.stats_ref = f32[8,2,256]{2,1,0:T(2,128)S(1)} all-to-all(f32[8,2,256]{2,1,0:T(2,128)S(1)} %broadcast_in_dim.25), channel_id=1, replica_groups=mesh['z'=8,'x'=4,'y'=4,'c'=2] {'z'}, dimensions={0} | all-to-all | bytes 32768 | tf_op jit(solution)/shard_map/all_to_all | solution.py:216
  106.2 0.0 copy-done.1
  106.2 0.9 final.1
  (9 shorter events, 0.1 us)
Async XLA Ops:
  8.0 24.6 %copy-start.2 = (bf16[640,160]{0,1:T(8,128)(2,1)S(1)}, bf16[640,160]{0,1:T(8,128)(2,1)}, u32[]{:S(2)}) copy-start(bf16[640,160]{0,1:T(8,128)(2,1)} %param.15) | copy-start | bytes 614404
  8.0 17.1 %collective-permute-start.2 = (bf16[176,640]{1,0:T(8,128)(2,1)}, bf16[176,640]{1,0:T(8,128)(2,1)S(1)}, u32[]{:S(2)}, u32[]{:S(2)}) collective-permute-start(bf16[176,640]{1,0:T(8,128)(2,1)} %pack.1.refs_0_), channel_id=1, source_target_pairs={{0,24},{8,0},{16,8},{24,16},{1,25},{9,1},{17,9},{25,17},{2,26},{10... | collective-permute-start | bytes 675848 | tf_op jit(solution)/shard_map/ppermute | solution.py:227
  11.4 13.7 %collective-permute-start.1 = (bf16[176,640]{1,0:T(8,128)(2,1)}, bf16[176,640]{1,0:T(8,128)(2,1)S(1)}, u32[]{:S(2)}, u32[]{:S(2)}) collective-permute-start(bf16[176,640]{1,0:T(8,128)(2,1)} %pack.1.refs_0_), channel_id=1, source_target_pairs={{0,16},{8,24},{16,0},{24,8},{1,17},{9,25},{17,1},{25,9},{2,18},{10... | collective-permute-start | bytes 675848 | tf_op jit(solution)/shard_map/ppermute | solution.py:227
  11.9 13.5 %collective-permute-start = (bf16[176,640]{1,0:T(8,128)(2,1)}, bf16[176,640]{1,0:T(8,128)(2,1)S(1)}, u32[]{:S(2)}, u32[]{:S(2)}) collective-permute-start(bf16[176,640]{1,0:T(8,128)(2,1)} %pack.1.refs_0_), channel_id=1, source_target_pairs={{0,8},{8,16},{16,24},{24,0},{1,9},{9,17},{17,25},{25,1},{2,10},{10... | collective-permute-start | bytes 675848 | tf_op jit(solution)/shard_map/ppermute | solution.py:227
  16.9 15.7 %all-to-all-start = ((bf16[8,8,640]{2,1,0:T(8,128)(2,1)}), bf16[8,8,640]{2,1,0:T(8,128)(2,1)S(1)}, u32[]{:S(2)}, u32[]{:S(2)}) async-start(bf16[8,8,640]{2,1,0:T(8,128)(2,1)} %attend.1), calls=%async_computation | async-start | bytes 163840 | tf_op jit(solution)/shard_map/all_to_all | solution.py:259
  25.4 20.2 %copy-start = (bf16[176,640]{1,0:T(8,128)(2,1)S(1)}, bf16[176,640]{1,0:T(8,128)(2,1)}, u32[]{:S(2)}) copy-start(bf16[176,640]{1,0:T(8,128)(2,1)} %pack.1.refs_0_) | copy-start | bytes 675844
  56.2 25.1 %copy-start.3 = (s32[256]{0:T(256)S(1)}, s32[256]{0:T(256)}, u32[]{:S(2)}) copy-start(s32[256]{0:T(256)} %param.18) | copy-start | bytes 3076
  77.8 6.2 %collective-permute-start.3 = (bf16[128,5120]{1,0:T(8,128)(2,1)S(1)}, bf16[128,5120]{1,0:T(8,128)(2,1)S(1)}, u32[]{:S(2)}, u32[]{:S(2)}) collective-permute-start(bf16[128,5120]{1,0:T(8,128)(2,1)S(1)} %bitcast.23), channel_id=1, source_target_pairs={{0,1},{1,0},{2,3},{3,2},{4,5},{5,4},{6,7},{7,6},{8,9},{9,8},{10,11... | collective-permute-start | bytes 3932168 | tf_op jit(solution)/shard_map/ppermute | solution.py:287
  84.4 21.8 %copy-start.1 = (f32[256]{0:T(256)S(1)}, f32[256]{0:T(256)}, u32[]{:S(2)}) copy-start(f32[256]{0:T(256)} %param.19) | copy-start | bytes 3076

commit v8 on v7

--- a/solution.py
+++ b/solution.py
@@ -46,9 +46,9 @@
     return jnp.concatenate([rows[k : k + 8] for k in range(0, rows.shape[0], 8)], axis=1)
 
 
-def pack_kernel(sizes, table_hbm, hidden_hbm, gain_hbm, pack_hbm, hidden_ref, gain_ref, tail_ref, sems):
+def pack_kernel(sizes, table_hbm, hidden_hbm, gain_hbm, pack_ref, hidden_ref, gain_ref, sems):
     columns, heads = table_hbm.shape
-    table = pltpu.make_async_copy(table_hbm, pack_hbm.at[pl.ds(0, columns)], sems.at[0])
+    table = pltpu.make_async_copy(table_hbm, pack_ref.at[pl.ds(0, columns)], sems.at[0])
     hidden = pltpu.make_async_copy(hidden_hbm, hidden_ref, sems.at[1])
     gain = pltpu.make_async_copy(gain_hbm, gain_ref, sems.at[2])
     hidden.start()
@@ -66,11 +66,8 @@
     )
     below = jnp.concatenate(three_parts(gain_ref[...]) + (jnp.zeros((5, columns), f32),), axis=0)
     below = jnp.concatenate([below, jnp.zeros((8, heads - columns), f32)], axis=1)
-    tail_ref[...] = jnp.concatenate([side_by_side(picked), below], axis=0).astype(bf16)
-    tail = pltpu.make_async_copy(tail_ref, pack_hbm.at[pl.ds(columns, TAIL)], sems.at[3])
-    tail.start()
+    pack_ref[columns:] = jnp.concatenate([side_by_side(picked), below], axis=0).astype(bf16)
     table.wait()
-    tail.wait()
 
 
 def attend_kernel(group, sizes, lengths_ref, query_ref, new_ref, cache_ref, out_ref, slots_ref, rows_ref, sums_ref, sems):
@@ -230,12 +227,11 @@
         functools.partial(pack_kernel, sizes),
         out_shape=jax.ShapeDtypeStruct((columns + TAIL, heads), bf16),
         in_specs=[IN_PLACE] * 3,
-        out_specs=IN_PLACE,
+        out_specs=IN_VMEM,
         scratch_shapes=[
             pltpu.VMEM((columns, hidden_in.shape[0]), bf16),
             pltpu.VMEM((1, columns), f32),
-            pltpu.VMEM((TAIL, heads), bf16),
-            pltpu.SemaphoreType.DMA((4,)),
+            pltpu.SemaphoreType.DMA((3,)),
         ],
         compiler_params=WHOLE,
         name="pack",

time: 108 us -> 102 us (0.944)
  Pallas kernels: 17.9 us -> 12.4 us
    pallas_call x1, Pallas kernels: 7.34 us -> 1.83 us  [shards(): pl.pallas_call(functools.partial(pack_kernel, sizes), out_shape=jax.Shape...]
where the time goes in v8:
time: 102 us
  blocking collectives  63.9 us (63%)
  starting transfers between devices  16.1 us (16%)
  Pallas kernels  12.4 us (12%)
  waiting for transfers between devices  7.41 us (7%)
    all_to_all x1, blocking collectives, shards(): lax.all_to_all(half, ('y', 'x'), split_axis=0, concat_axis=0, tiled=False)  21.6 us
    all_to_all x2, blocking collectives, spread(): return lax.all_to_all(many, axes, split_axis=0, concat_axis=0, tiled=False)  19.6 us
    all_to_all x1, blocking collectives, shards(): lax.all_to_all(partial, ('c', 'y'), split_axis=0, concat_axis=0, tiled=Fa...  12.6 us
    all_to_all x1, blocking collectives, shards(): rows = lax.all_to_all(rows, 'z', split_axis=0, concat_axis=0, tiled=False)  10 us
    all_to_all x1, starting transfers between devices, shards(): lax.all_to_all(many, 'z', split_axis=0, concat_axis=0, tiled=False)  8.2 us
    all_to_all x1, waiting for transfers between devices, shards(): lax.all_to_all(many, 'z', split_axis=0, concat_axis=0, tiled=False)  7.17 us
    ppermute x3, starting transfers between devices, from_along_x(): return lax.ppermute(block, 'x', [(i, (i + step) % nx) for i in range(nx)])  4.51 us
    pallas_call x1, Pallas kernels, shards(): pl.pallas_call(functools.partial(attend_kernel, HEADS // KV_HEADS, sizes)...  4.34 us
  transfers between devices with their start and end apart: 5, of which 2 were waited for; matrix products, arithmetic and copies ran while one was open for 0% of the time, Pallas kernels for 7%

profile of v8, /device:TPU:1, one launch (start us, length us, event | category | flops | bytes accessed | tf_op | source)
XLA Modules:
  0.0 101.6 jit_solution(756026799163126318)
XLA Ops:
  0.6 1.8 %pack.1.refs_0_ = bf16[176,640]{1,0:T(8,128)(2,1)} custom-call(bf16[160,640]{1,0:T(8,128)(2,1)} %bitcast.27, bf16[160,256]{1,0:T(8,128)(2,1)} %bitcast.29, f32[1,160]{1,0:T(1,128)} %bitcast.32), custom_call_target="tpu_custom_call" | custom-call | tf_op jit(solution)/shard_map/pack/pallas_call | solution.py:226
  2.5 0.0 copy-start.2
  2.5 3.4 %collective-permute-start.2 = (bf16[176,640]{1,0:T(8,128)(2,1)}, bf16[176,640]{1,0:T(8,128)(2,1)S(1)}, u32[]{:S(2)}, u32[]{:S(2)}) collective-permute-start(bf16[176,640]{1,0:T(8,128)(2,1)} %pack.1.refs_0_), channel_id=1, source_target_pairs={{0,24},{8,0},{16,8},{24,16},{1,25},{9,1},{17,9},{25,17},{2,26},{10... | collective-permute-start | bytes 675848 | tf_op jit(solution)/shard_map/ppermute | solution.py:224
  5.9 0.5 collective-permute-start.1
  6.4 0.6 collective-permute-start
  7.0 4.3 %attend.1 = bf16[8,8,640]{2,1,0:T(8,128)(2,1)} custom-call(s32[256]{0:T(256)} %lengths_ref.1, bf16[8,640]{1,0:T(8,128)(2,1)} %query_ref.1, bf16[8,2,128]{2,1,0:T(2,128)(2,1)} %new_ref.1, bf16[8,2,1024,128]{3,2,1,0:T(8,128)(2,1)} %cache_ref.1), custom_call_target="tpu_custom_call" | custom-call | tf_op jit(solution)/shard_map/attend/pallas_call | solution.py:241
  11.3 8.2 %all-to-all-start = ((bf16[8,8,640]{2,1,0:T(8,128)(2,1)}), bf16[8,8,640]{2,1,0:T(8,128)(2,1)S(1)}, u32[]{:S(2)}, u32[]{:S(2)}) async-start(bf16[8,8,640]{2,1,0:T(8,128)(2,1)} %attend.1), calls=%async_computation | async-start | bytes 163840 | tf_op jit(solution)/shard_map/all_to_all | solution.py:255
  19.5 0.0 collective-permute-done.2.refs_3_
  19.6 0.0 collective-permute-done.1.refs_2_
  19.6 0.2 collective-permute-done.refs_1_
  19.9 0.0 copy-start
  19.9 7.2 %all-to-all-done = bf16[8,8,640]{2,1,0:T(8,128)(2,1)S(1)} async-done(((bf16[8,8,640]{2,1,0:T(8,128)(2,1)}), bf16[8,8,640]{2,1,0:T(8,128)(2,1)S(1)}, u32[]{:S(2)}, u32[]{:S(2)}) %all-to-all-start) | async-done | bytes 81952 | tf_op jit(solution)/shard_map/all_to_all | solution.py:255
  27.1 0.0 copy-done.2
  27.1 0.4 fusion
  27.4 12.6 %all_to_all.30.partial_ref = f32[8,8,640]{2,1,0:T(8,128)S(1)} all-to-all(f32[8,8,640]{2,1,0:T(8,128)S(1)} %fusion), channel_id=1, replica_groups=mesh['z'=8,'x'=4,'y'=4,'c'=2] {'c','y'}, dimensions={0} | all-to-all | bytes 327680 | tf_op jit(solution)/shard_map/all_to_all | solution.py:261
  40.0 0.0 copy-done
  40.0 0.3 resid.1
  40.4 10.0 %all_to_all.31.rows_ref = bf16[8,8,768]{2,1,0:T(8,128)(2,1)S(1)} all-to-all(bf16[8,8,768]{2,1,0:T(8,128)(2,1)S(1)} %resid.1), channel_id=1, replica_groups=mesh['z'=8,'x'=4,'y'=4,'c'=2] {'z'}, dimensions={0} | all-to-all | bytes 196608 | tf_op jit(solution)/shard_map/all_to_all | solution.py:272
  50.4 0.2 norm.1
  50.6 0.0 copy-start.3
  50.7 21.6 %all_to_all.32 = bf16[16,8,5120]{2,1,0:T(8,128)(2,1)S(1)} all-to-all(bf16[16,8,5120]{2,1,0:T(8,128)(2,1)S(1)} %norm.1), channel_id=1, replica_groups=mesh['z'=8,'x'=4,'y'=4,'c'=2] {'y','x'}, dimensions={0} | all-to-all | bytes 2621440 | tf_op jit(solution)/shard_map/all_to_all | solution.py:281
  72.3 3.4 %collective-permute-start.3 = (bf16[128,5120]{1,0:T(8,128)(2,1)S(1)}, bf16[128,5120]{1,0:T(8,128)(2,1)S(1)}, u32[]{:S(2)}, u32[]{:S(2)}) collective-permute-start(bf16[128,5120]{1,0:T(8,128)(2,1)S(1)} %bitcast.23), channel_id=1, source_target_pairs={{0,1},{1,0},{2,3},{3,2},{4,5},{5,4},{6,7},{7,6},{8,9},{9,8},{10,11... | collective-permute-start | bytes 3932168 | tf_op jit(solution)/shard_map/ppermute | solution.py:283
  75.7 0.0 copy-done.3
  75.7 2.8 %fetch.1.head_ref = bf16[594,5120]{1,0:T(8,128)(2,1)S(1)} custom-call(bf16[594,5120]{1,0:T(8,128)(2,1)} %head_hbm.1, bf16[128,5120]{1,0:T(8,128)(2,1)S(1)} %bitcast.24), custom_call_target="tpu_custom_call" | custom-call | tf_op jit(solution)/shard_map/fetch/pallas_call | solution.py:284
  78.5 0.0 collective-permute-done.3
  78.5 0.2 broadcast_select_fusion.1
  78.7 0.2 pad_maximum_fusion.rows_ref
  78.9 0.0 copy-start.1
  78.9 2.0 %logits.1 = (f32[594,256]{1,0:T(8,128)S(1)}, f32[2,256]{1,0:T(2,128)S(1)}) custom-call(bf16[594,5120]{1,0:T(8,128)(2,1)S(1)} %fetch.1.head_ref, bf16[256,5120]{1,0:T(8,128)(2,1)S(1)} %pad_maximum_fusion.rows_ref, s32[1,256]{1,0:T(1,128)S(1)} %bitcast.25), custom_call_target="tpu_custom_call" | custom-call | tf_op jit(solution)/shard_map/logits/pallas_call | solution.py:301
  80.9 10.6 %all_to_all.33 = f32[32,2,256]{2,1,0:T(2,128)S(1)} all-to-all(f32[32,2,256]{2,1,0:T(2,128)S(1)} %broadcast_in_dim.24), channel_id=1, replica_groups=mesh['z'=8,'x'=4,'y'=4,'c'=2] {'x','y','c'}, dimensions={0} | all-to-all | bytes 131072 | tf_op jit(solution)/shard_map/all_to_all | solution.py:213
  91.5 0.1 slice_reduce_fusion.1
  91.7 9.0 %all_to_all.34.stats_ref = f32[8,2,256]{2,1,0:T(2,128)S(1)} all-to-all(f32[8,2,256]{2,1,0:T(2,128)S(1)} %broadcast_in_dim.25), channel_id=1, replica_groups=mesh['z'=8,'x'=4,'y'=4,'c'=2] {'z'}, dimensions={0} | all-to-all | bytes 32768 | tf_op jit(solution)/shard_map/all_to_all | solution.py:213
  100.7 0.0 copy-done.1
  100.7 0.9 final.1
  (9 shorter events, 0.1 us)
Async XLA Ops:
  2.5 24.6 %copy-start.2 = (bf16[640,160]{0,1:T(8,128)(2,1)S(1)}, bf16[640,160]{0,1:T(8,128)(2,1)}, u32[]{:S(2)}) copy-start(bf16[640,160]{0,1:T(8,128)(2,1)} %param.15) | copy-start | bytes 614404
  2.5 17.1 %collective-permute-start.2 = (bf16[176,640]{1,0:T(8,128)(2,1)}, bf16[176,640]{1,0:T(8,128)(2,1)S(1)}, u32[]{:S(2)}, u32[]{:S(2)}) collective-permute-start(bf16[176,640]{1,0:T(8,128)(2,1)} %pack.1.refs_0_), channel_id=1, source_target_pairs={{0,24},{8,0},{16,8},{24,16},{1,25},{9,1},{17,9},{25,17},{2,26},{10... | collective-permute-start | bytes 675848 | tf_op jit(solution)/shard_map/ppermute | solution.py:224
  5.9 13.7 %collective-permute-start.1 = (bf16[176,640]{1,0:T(8,128)(2,1)}, bf16[176,640]{1,0:T(8,128)(2,1)S(1)}, u32[]{:S(2)}, u32[]{:S(2)}) collective-permute-start(bf16[176,640]{1,0:T(8,128)(2,1)} %pack.1.refs_0_), channel_id=1, source_target_pairs={{0,16},{8,24},{16,0},{24,8},{1,17},{9,25},{17,1},{25,9},{2,18},{10... | collective-permute-start | bytes 675848 | tf_op jit(solution)/shard_map/ppermute | solution.py:224
  6.4 13.5 %collective-permute-start = (bf16[176,640]{1,0:T(8,128)(2,1)}, bf16[176,640]{1,0:T(8,128)(2,1)S(1)}, u32[]{:S(2)}, u32[]{:S(2)}) collective-permute-start(bf16[176,640]{1,0:T(8,128)(2,1)} %pack.1.refs_0_), channel_id=1, source_target_pairs={{0,8},{8,16},{16,24},{24,0},{1,9},{9,17},{17,25},{25,1},{2,10},{10... | collective-permute-start | bytes 675848 | tf_op jit(solution)/shard_map/ppermute | solution.py:224
  11.3 15.7 %all-to-all-start = ((bf16[8,8,640]{2,1,0:T(8,128)(2,1)}), bf16[8,8,640]{2,1,0:T(8,128)(2,1)S(1)}, u32[]{:S(2)}, u32[]{:S(2)}) async-start(bf16[8,8,640]{2,1,0:T(8,128)(2,1)} %attend.1), calls=%async_computation | async-start | bytes 163840 | tf_op jit(solution)/shard_map/all_to_all | solution.py:255
  19.9 20.2 %copy-start = (bf16[176,640]{1,0:T(8,128)(2,1)S(1)}, bf16[176,640]{1,0:T(8,128)(2,1)}, u32[]{:S(2)}) copy-start(bf16[176,640]{1,0:T(8,128)(2,1)} %pack.1.refs_0_) | copy-start | bytes 675844
  50.6 25.1 %copy-start.3 = (s32[256]{0:T(256)S(1)}, s32[256]{0:T(256)}, u32[]{:S(2)}) copy-start(s32[256]{0:T(256)} %param.18) | copy-start | bytes 3076
  72.3 6.2 %collective-permute-start.3 = (bf16[128,5120]{1,0:T(8,128)(2,1)S(1)}, bf16[128,5120]{1,0:T(8,128)(2,1)S(1)}, u32[]{:S(2)}, u32[]{:S(2)}) collective-permute-start(bf16[128,5120]{1,0:T(8,128)(2,1)S(1)} %bitcast.23), channel_id=1, source_target_pairs={{0,1},{1,0},{2,3},{3,2},{4,5},{5,4},{6,7},{7,6},{8,9},{9,8},{10,11... | collective-permute-start | bytes 3932168 | tf_op jit(solution)/shard_map/ppermute | solution.py:283
  78.9 21.8 %copy-start.1 = (f32[256]{0:T(256)S(1)}, f32[256]{0:T(256)}, u32[]{:S(2)}) copy-start(f32[256]{0:T(256)} %param.19) | copy-start | bytes 3076

commit v9 on v8

--- a/solution.py
+++ b/solution.py
@@ -46,34 +46,31 @@
     return jnp.concatenate([rows[k : k + 8] for k in range(0, rows.shape[0], 8)], axis=1)
 
 
-def pack_kernel(sizes, table_hbm, hidden_hbm, gain_hbm, pack_ref, hidden_ref, gain_ref, sems):
-    columns, heads = table_hbm.shape
-    table = pltpu.make_async_copy(table_hbm, pack_ref.at[pl.ds(0, columns)], sems.at[0])
-    hidden = pltpu.make_async_copy(hidden_hbm, hidden_ref, sems.at[1])
-    gain = pltpu.make_async_copy(gain_hbm, gain_ref, sems.at[2])
-    hidden.start()
-    gain.start()
-    table.start()
-    rows, requests = heads // columns * 8, hidden_ref.shape[1]
+def pack_tail(sizes, hidden_ref, gain_ref, pack_ref):
+    columns, requests = hidden_ref.shape
+    heads = pack_ref.shape[1]
+    rows = heads // columns * 8
     part = lax.axis_index("c") * sizes["y"] + lax.axis_index("y")
     row = lax.broadcasted_iota(jnp.int32, (rows, requests), 0)
     lane = lax.broadcasted_iota(jnp.int32, (rows, requests), 1)
     chosen = jnp.where(lane == row + part * rows, 1.0, 0.0).astype(bf16)
-    hidden.wait()
-    gain.wait()
     picked = lax.dot_general(
         chosen, hidden_ref[...], (((1,), (1,)), ((), ())), preferred_element_type=f32
     )
     below = jnp.concatenate(three_parts(gain_ref[...]) + (jnp.zeros((5, columns), f32),), axis=0)
     below = jnp.concatenate([below, jnp.zeros((8, heads - columns), f32)], axis=1)
     pack_ref[columns:] = jnp.concatenate([side_by_side(picked), below], axis=0).astype(bf16)
-    table.wait()
-
-
-def attend_kernel(group, sizes, lengths_ref, query_ref, new_ref, cache_ref, out_ref, slots_ref, rows_ref, sums_ref, sems):
+
+
+def attend_kernel(group, sizes, lengths_ref, query_ref, new_ref, cache_ref, table_hbm, hidden_hbm, gain_hbm, *refs):
+    out_ref, pack_ref, slots_ref, rows_ref, sums_ref, hidden_ref, gain_ref, sems, pack_sems = refs
     count, _, slots, head_dim = cache_ref.shape
+    columns = table_hbm.shape[0]
     z, x = lax.axis_index("z"), lax.axis_index("x")
     scale = head_dim ** (-0.5)
+    hidden = pltpu.make_async_copy(hidden_hbm, hidden_ref, pack_sems.at[0])
+    gain = pltpu.make_async_copy(gain_hbm, gain_ref, pack_sems.at[1])
+    table = pltpu.make_async_copy(table_hbm, pack_ref.at[pl.ds(0, columns)], pack_sems.at[2])
     portions = [range(k, k + count // 2) for k in (0, count // 2)]
     loads = [
         [
@@ -83,8 +80,14 @@
         for portion in portions
         for kind in range(2)
     ]
+    hidden.start()
+    gain.start()
     for load in sum(loads, []):
         load.start()
+    table.start()
+    hidden.wait()
+    gain.wait()
+    pack_tail(sizes, hidden_ref, gain_ref, pack_ref)
 
     query = query_ref[...].astype(f32)
     fresh = new_ref[...].astype(f32)
@@ -128,6 +131,7 @@
     done = jnp.concatenate([sums_ref[pl.ds(g, count, stride=8), :] for g in range(group)], axis=1).astype(bf16)
     for k in range(out_ref.shape[0]):
         out_ref[k] = done
+    table.wait()
 
 
 def resid_kernel(partial_ref, *refs):
@@ -223,35 +227,28 @@
     def from_along_x(block, step):
         return lax.ppermute(block, "x", [(i, (i + step) % nx) for i in range(nx)])
 
-    pack = pl.pallas_call(
-        functools.partial(pack_kernel, sizes),
-        out_shape=jax.ShapeDtypeStruct((columns + TAIL, heads), bf16),
-        in_specs=[IN_PLACE] * 3,
-        out_specs=IN_VMEM,
-        scratch_shapes=[
-            pltpu.VMEM((columns, hidden_in.shape[0]), bf16),
-            pltpu.VMEM((1, columns), f32),
-            pltpu.SemaphoreType.DMA((3,)),
+    many, pack = pl.pallas_call(
+        functools.partial(attend_kernel, HEADS // KV_HEADS, sizes),
+        out_shape=[
+            jax.ShapeDtypeStruct((nz,) + query.shape, bf16),
+            jax.ShapeDtypeStruct((columns + TAIL, heads), bf16),
         ],
-        compiler_params=WHOLE,
-        name="pack",
-    )(out_proj.T, hidden_in.T, final_gain[None])
-    packs = [pack] + [from_along_x(pack, k) for k in range(1, nx)]
-    table = jnp.concatenate([out_proj.T] + [p[:columns] for p in packs[1:]], axis=0)
-    many = pl.pallas_call(
-        functools.partial(attend_kernel, HEADS // KV_HEADS, sizes),
-        out_shape=jax.ShapeDtypeStruct((nz,) + query.shape, bf16),
-        in_specs=[IN_SMEM] + [IN_VMEM] * 2 + [IN_PLACE],
-        out_specs=IN_VMEM,
+        in_specs=[IN_SMEM] + [IN_VMEM] * 2 + [IN_PLACE] * 4,
+        out_specs=[IN_VMEM] * 2,
         scratch_shapes=[
             pltpu.VMEM(cache.shape, bf16),
             pltpu.VMEM((count * 8, HEAD_DIM), f32),
             pltpu.VMEM((count * 8, HEAD_DIM), f32),
+            pltpu.VMEM((columns, hidden_in.shape[0]), bf16),
+            pltpu.VMEM((1, columns), f32),
             pltpu.SemaphoreType.DMA((2, count)),
+            pltpu.SemaphoreType.DMA((3,)),
         ],
         compiler_params=WHOLE,
         name="attend",
-    )(lengths, query, new_kv, cache)
+    )(lengths, query, new_kv, cache, out_proj.T, hidden_in.T, final_gain[None])
+    packs = [pack] + [from_along_x(pack, k) for k in range(1, nx)]
+    table = jnp.concatenate([out_proj.T] + [p[:columns] for p in packs[1:]], axis=0)
     gathered = lax.all_to_all(many, "z", split_axis=0, concat_axis=0, tiled=False)
     gathered = gathered.reshape(nz * count, -1)
     partial = lax.dot_general(

time: 102 us -> 101 us (level)
    ppermute x3, waiting for transfers between devices: 0.24 us -> 4.61 us  [from_along_x(): return lax.ppermute(block, 'x', [(i, (i + step) % nx) for i in range(nx)])]
    all_to_all x1, waiting for transfers between devices: 7.17 us -> 2.8 us  [shards(): lax.all_to_all(many, 'z', split_axis=0, concat_axis=0, tiled=False)]
    pallas_call x1 -> x0, Pallas kernels: 1.83 us -> none  [shards(): pl.pallas_call(functools.partial(pack_kernel, sizes), out_shape=jax.Shape...]
    pallas_call x1, Pallas kernels: 4.34 us -> 5.57 us  [shards(): pl.pallas_call(functools.partial(attend_kernel, HEADS // KV_HEADS, sizes)...]
  transfers between devices with their start and end apart: 5 -> 5, of which waited for: 2 -> 2; matrix products, arithmetic and copies ran while one was open for 0% -> 0% of each run, Pallas kernels for 7% -> 3%
where the time goes in v9:
time: 101 us
  blocking collectives  63.9 us (63%)
  starting transfers between devices  16.1 us (16%)
  Pallas kernels  11.8 us (12%)
  waiting for transfers between devices  7.42 us (7%)
    all_to_all x1, blocking collectives, shards(): lax.all_to_all(half, ('y', 'x'), split_axis=0, concat_axis=0, tiled=False)  21.4 us
    all_to_all x2, blocking collectives, spread(): return lax.all_to_all(many, axes, split_axis=0, concat_axis=0, tiled=False)  19.6 us
    all_to_all x1, blocking collectives, shards(): lax.all_to_all(partial, ('c', 'y'), split_axis=0, concat_axis=0, tiled=Fa...  12.6 us
    all_to_all x1, blocking collectives, shards(): rows = lax.all_to_all(rows, 'z', split_axis=0, concat_axis=0, tiled=False)  10.3 us
    all_to_all x1, starting transfers between devices, shards(): lax.all_to_all(many, 'z', split_axis=0, concat_axis=0, tiled=False)  8.19 us
    pallas_call x1, Pallas kernels, shards(): pl.pallas_call(functools.partial(attend_kernel, HEADS // KV_HEADS, sizes)...  5.57 us
    ppermute x3, waiting for transfers between devices, from_along_x(): return lax.ppermute(block, 'x', [(i, (i + step) % nx) for i in range(nx)])  4.61 us
    ppermute x3, starting transfers between devices, from_along_x(): return lax.ppermute(block, 'x', [(i, (i + step) % nx) for i in range(nx)])  4.51 us
  transfers between devices with their start and end apart: 5, of which 2 were waited for; matrix products, arithmetic and copies ran while one was open for 0% of the time, Pallas kernels for 3%

profile of v9, /device:TPU:1, one launch (start us, length us, event | category | flops | bytes accessed | tf_op | source)
XLA Modules:
  0.0 100.9 jit_solution(15250076398503395777)
XLA Ops:
  0.6 0.0 copy-start.2
  0.6 5.6 %attend.1 = (bf16[8,8,640]{2,1,0:T(8,128)(2,1)}, bf16[176,640]{1,0:T(8,128)(2,1)}) custom-call(s32[256]{0:T(256)} %lengths_ref.1, bf16[8,640]{1,0:T(8,128)(2,1)} %query_ref.1, bf16[8,2,128]{2,1,0:T(2,128)(2,1)} %new_ref.1, bf16[8,2,1024,128]{3,2,1,0:T(8,128)(2,1)} %cache_ref.1, bf16[160,640]{1,0:T(8,128)(2,1)} %bitcast.27, bf16[160,256]{1,0:T(8,128)(2,1)} %bitcast.29, ...), custom_call_target="tpu_custom_call" | custom-call | tf_op jit(solution)/shard_map/attend/pallas_call | solution.py:230
  6.2 3.4 %collective-permute-start.2 = (bf16[176,640]{1,0:T(8,128)(2,1)}, bf16[176,640]{1,0:T(8,128)(2,1)S(1)}, u32[]{:S(2)}, u32[]{:S(2)}) collective-permute-start(bf16[176,640]{1,0:T(8,128)(2,1)} %get-tuple-element.13.refs_0_), channel_id=1, source_target_pairs={{0,24},{8,0},{16,8},{24,16},{1,25},{9,1},{17,9},{25,17},{2,26},{10... | collective-permute-start | bytes 675848 | tf_op jit(solution)/shard_map/ppermute | solution.py:228
  9.6 0.5 collective-permute-start.1
  10.1 0.6 collective-permute-start
  10.7 8.2 %all-to-all-start = ((bf16[8,8,640]{2,1,0:T(8,128)(2,1)}), bf16[8,8,640]{2,1,0:T(8,128)(2,1)S(1)}, u32[]{:S(2)}, u32[]{:S(2)}) async-start(bf16[8,8,640]{2,1,0:T(8,128)(2,1)} %get-tuple-element.12), calls=%async_computation | async-start | bytes 163840 | tf_op jit(solution)/shard_map/all_to_all | solution.py:252
  18.9 0.0 collective-permute-done.2.refs_3_
  19.0 0.0 collective-permute-done.1.refs_2_
  19.0 4.6 %collective-permute-done.refs_1_ = bf16[176,640]{1,0:T(8,128)(2,1)S(1)} collective-permute-done((bf16[176,640]{1,0:T(8,128)(2,1)}, bf16[176,640]{1,0:T(8,128)(2,1)S(1)}, u32[]{:S(2)}, u32[]{:S(2)}) %collective-permute-start) | collective-permute-done | bytes 225312 | tf_op jit(solution)/shard_map/ppermute | solution.py:228
  23.6 0.0 copy-start
  23.6 2.8 %all-to-all-done = bf16[8,8,640]{2,1,0:T(8,128)(2,1)S(1)} async-done(((bf16[8,8,640]{2,1,0:T(8,128)(2,1)}), bf16[8,8,640]{2,1,0:T(8,128)(2,1)S(1)}, u32[]{:S(2)}, u32[]{:S(2)}) %all-to-all-start) | async-done | bytes 81952 | tf_op jit(solution)/shard_map/all_to_all | solution.py:252
  26.4 0.0 copy-done.2
  26.4 0.4 fusion
  26.8 12.6 %all_to_all.30.partial_ref = f32[8,8,640]{2,1,0:T(8,128)S(1)} all-to-all(f32[8,8,640]{2,1,0:T(8,128)S(1)} %fusion), channel_id=1, replica_groups=mesh['z'=8,'x'=4,'y'=4,'c'=2] {'c','y'}, dimensions={0} | all-to-all | bytes 327680 | tf_op jit(solution)/shard_map/all_to_all | solution.py:258
  39.4 0.0 copy-done
  39.4 0.3 resid.1
  39.8 10.3 %all_to_all.31.rows_ref = bf16[8,8,768]{2,1,0:T(8,128)(2,1)S(1)} all-to-all(bf16[8,8,768]{2,1,0:T(8,128)(2,1)S(1)} %resid.1), channel_id=1, replica_groups=mesh['z'=8,'x'=4,'y'=4,'c'=2] {'z'}, dimensions={0} | all-to-all | bytes 196608 | tf_op jit(solution)/shard_map/all_to_all | solution.py:269
  50.1 0.2 norm.1
  50.3 0.0 copy-start.3
  50.3 21.4 %all_to_all.32 = bf16[16,8,5120]{2,1,0:T(8,128)(2,1)S(1)} all-to-all(bf16[16,8,5120]{2,1,0:T(8,128)(2,1)S(1)} %norm.1), channel_id=1, replica_groups=mesh['z'=8,'x'=4,'y'=4,'c'=2] {'y','x'}, dimensions={0} | all-to-all | bytes 2621440 | tf_op jit(solution)/shard_map/all_to_all | solution.py:278
  71.7 3.4 %collective-permute-start.3 = (bf16[128,5120]{1,0:T(8,128)(2,1)S(1)}, bf16[128,5120]{1,0:T(8,128)(2,1)S(1)}, u32[]{:S(2)}, u32[]{:S(2)}) collective-permute-start(bf16[128,5120]{1,0:T(8,128)(2,1)S(1)} %bitcast.23), channel_id=1, source_target_pairs={{0,1},{1,0},{2,3},{3,2},{4,5},{5,4},{6,7},{7,6},{8,9},{9,8},{10,11... | collective-permute-start | bytes 3932168 | tf_op jit(solution)/shard_map/ppermute | solution.py:280
  75.1 0.0 copy-done.3
  75.1 2.8 %fetch.1.head_ref = bf16[594,5120]{1,0:T(8,128)(2,1)S(1)} custom-call(bf16[594,5120]{1,0:T(8,128)(2,1)} %head_hbm.1, bf16[128,5120]{1,0:T(8,128)(2,1)S(1)} %bitcast.24), custom_call_target="tpu_custom_call" | custom-call | tf_op jit(solution)/shard_map/fetch/pallas_call | solution.py:281
  77.9 0.0 collective-permute-done.3
  77.9 0.2 broadcast_select_fusion.1
  78.1 0.2 pad_maximum_fusion.rows_ref
  78.2 0.0 copy-start.1
  78.2 2.0 %logits.1 = (f32[594,256]{1,0:T(8,128)S(1)}, f32[2,256]{1,0:T(2,128)S(1)}) custom-call(bf16[594,5120]{1,0:T(8,128)(2,1)S(1)} %fetch.1.head_ref, bf16[256,5120]{1,0:T(8,128)(2,1)S(1)} %pad_maximum_fusion.rows_ref, s32[1,256]{1,0:T(1,128)S(1)} %bitcast.25), custom_call_target="tpu_custom_call" | custom-call | tf_op jit(solution)/shard_map/logits/pallas_call | solution.py:298
  80.3 10.6 %all_to_all.33 = f32[32,2,256]{2,1,0:T(2,128)S(1)} all-to-all(f32[32,2,256]{2,1,0:T(2,128)S(1)} %broadcast_in_dim.24), channel_id=1, replica_groups=mesh['z'=8,'x'=4,'y'=4,'c'=2] {'x','y','c'}, dimensions={0} | all-to-all | bytes 131072 | tf_op jit(solution)/shard_map/all_to_all | solution.py:217
  90.9 0.1 slice_reduce_fusion.1
  91.1 9.0 %all_to_all.34.stats_ref = f32[8,2,256]{2,1,0:T(2,128)S(1)} all-to-all(f32[8,2,256]{2,1,0:T(2,128)S(1)} %broadcast_in_dim.25), channel_id=1, replica_groups=mesh['z'=8,'x'=4,'y'=4,'c'=2] {'z'}, dimensions={0} | all-to-all | bytes 32768 | tf_op jit(solution)/shard_map/all_to_all | solution.py:217
  100.0 0.0 copy-done.1
  100.0 0.9 final.1
  (9 shorter events, 0.1 us)
Async XLA Ops:
  0.6 25.8 %copy-start.2 = (bf16[640,160]{0,1:T(8,128)(2,1)S(1)}, bf16[640,160]{0,1:T(8,128)(2,1)}, u32[]{:S(2)}) copy-start(bf16[640,160]{0,1:T(8,128)(2,1)} %param.15) | copy-start | bytes 614404
  6.2 12.7 %collective-permute-start.2 = (bf16[176,640]{1,0:T(8,128)(2,1)}, bf16[176,640]{1,0:T(8,128)(2,1)S(1)}, u32[]{:S(2)}, u32[]{:S(2)}) collective-permute-start(bf16[176,640]{1,0:T(8,128)(2,1)} %get-tuple-element.13.refs_0_), channel_id=1, source_target_pairs={{0,24},{8,0},{16,8},{24,16},{1,25},{9,1},{17,9},{25,17},{2,26},{10... | collective-permute-start | bytes 675848 | tf_op jit(solution)/shard_map/ppermute | solution.py:228
  9.6 9.4 %collective-permute-start.1 = (bf16[176,640]{1,0:T(8,128)(2,1)}, bf16[176,640]{1,0:T(8,128)(2,1)S(1)}, u32[]{:S(2)}, u32[]{:S(2)}) collective-permute-start(bf16[176,640]{1,0:T(8,128)(2,1)} %get-tuple-element.13.refs_0_), channel_id=1, source_target_pairs={{0,16},{8,24},{16,0},{24,8},{1,17},{9,25},{17,1},{25,9},{2,18},{10... | collective-permute-start | bytes 675848 | tf_op jit(solution)/shard_map/ppermute | solution.py:228
  10.1 13.5 %collective-permute-start = (bf16[176,640]{1,0:T(8,128)(2,1)}, bf16[176,640]{1,0:T(8,128)(2,1)S(1)}, u32[]{:S(2)}, u32[]{:S(2)}) collective-permute-start(bf16[176,640]{1,0:T(8,128)(2,1)} %get-tuple-element.13.refs_0_), channel_id=1, source_target_pairs={{0,8},{8,16},{16,24},{24,0},{1,9},{9,17},{17,25},{25,1},{2,10},{10... | collective-permute-start | bytes 675848 | tf_op jit(solution)/shard_map/ppermute | solution.py:228
  10.7 15.7 %all-to-all-start = ((bf16[8,8,640]{2,1,0:T(8,128)(2,1)}), bf16[8,8,640]{2,1,0:T(8,128)(2,1)S(1)}, u32[]{:S(2)}, u32[]{:S(2)}) async-start(bf16[8,8,640]{2,1,0:T(8,128)(2,1)} %get-tuple-element.12), calls=%async_computation | async-start | bytes 163840 | tf_op jit(solution)/shard_map/all_to_all | solution.py:252
  23.6 15.8 %copy-start = (bf16[176,640]{1,0:T(8,128)(2,1)S(1)}, bf16[176,640]{1,0:T(8,128)(2,1)}, u32[]{:S(2)}) copy-start(bf16[176,640]{1,0:T(8,128)(2,1)} %get-tuple-element.13.refs_0_) | copy-start | bytes 675844
  50.3 24.8 %copy-start.3 = (s32[256]{0:T(256)S(1)}, s32[256]{0:T(256)}, u32[]{:S(2)}) copy-start(s32[256]{0:T(256)} %param.18) | copy-start | bytes 3076
  71.7 6.2 %collective-permute-start.3 = (bf16[128,5120]{1,0:T(8,128)(2,1)S(1)}, bf16[128,5120]{1,0:T(8,128)(2,1)S(1)}, u32[]{:S(2)}, u32[]{:S(2)}) collective-permute-start(bf16[128,5120]{1,0:T(8,128)(2,1)S(1)} %bitcast.23), channel_id=1, source_target_pairs={{0,1},{1,0},{2,3},{3,2},{4,5},{5,4},{6,7},{7,6},{8,9},{9,8},{10,11... | collective-permute-start | bytes 3932168 | tf_op jit(solution)/shard_map/ppermute | solution.py:280
  78.2 21.8 %copy-start.1 = (f32[256]{0:T(256)S(1)}, f32[256]{0:T(256)}, u32[]{:S(2)}) copy-start(f32[256]{0:T(256)} %param.19) | copy-start | bytes 3076

commit v10 on v9

--- a/solution.py
+++ b/solution.py
@@ -97,21 +97,23 @@
     heads = rows_ref[...]
     new_keys = jnp.concatenate([jnp.broadcast_to(fresh[r, 0:1], (8, head_dim)) for r in range(count)], axis=0)
     own_scores = jnp.sum(heads * new_keys, axis=1, keepdims=True) * scale
-    heads = heads.astype(bf16)
-    position = lax.broadcasted_iota(jnp.int32, (8, slots), 1)
+    position = lax.broadcasted_iota(jnp.int32, (16, slots), 1)
+    upper_slots = lax.broadcasted_iota(jnp.int32, (16, slots), 0) < 8
     base = (z * sizes["x"] + x) * count
     for portion, key_loads, value_loads in zip(portions, loads[::2], loads[1::2]):
         for load in key_loads:
             load.wait()
         scores = []
-        for r in portion:
+        for r in portion[::2]:
+            rows = heads[8 * r : 8 * r + 16]
+            upper = lax.broadcasted_iota(jnp.int32, rows.shape, 0) < 8
+            rows = jnp.concatenate([jnp.where(upper, rows, 0.0), jnp.where(upper, 0.0, rows)], axis=1)
+            keys = jnp.concatenate([slots_ref[r, 0], slots_ref[r + 1, 0]], axis=1)
             score = lax.dot_general(
-                heads[8 * r : 8 * r + 8],
-                slots_ref[r, 0],
-                (((1,), (1,)), ((), ())),
-                preferred_element_type=f32,
+                rows.astype(bf16), keys, (((1,), (1,)), ((), ())), preferred_element_type=f32
             )
-            scores.append(jnp.where(position < lengths_ref[base + r], score * scale, masked_score))
+            live = jnp.where(upper_slots, lengths_ref[base + r], lengths_ref[base + r + 1])
+            scores.append(jnp.where(position < live, score * scale, masked_score))
         scores = jnp.concatenate(scores, axis=0)
         own_score = own_scores[8 * portion[0] : 8 * portion[0] + scores.shape[0]]
         top = jnp.maximum(jnp.max(scores, axis=1, keepdims=True), own_score)
@@ -122,12 +124,17 @@
         fine = (weights - coarse.astype(f32)).astype(bf16)
         for load in value_loads:
             load.wait()
-        for k, r in enumerate(portion):
-            span = slice(8 * k, 8 * k + 8)
-            stacked = jnp.concatenate([coarse[span].astype(f32), fine[span].astype(f32)], axis=0).astype(bf16)
-            sums = jnp.dot(stacked, slots_ref[r, 1], preferred_element_type=f32)
-            total = sums[:8] + sums[8:16] + own_weight[span] * fresh[r, 1:2]
-            sums_ref[8 * r : 8 * r + 8] = total / mass[span]
+        for k, r in zip(range(0, len(portion), 2), portion[::2]):
+            span = slice(8 * k, 8 * k + 16)
+            stacked = jnp.concatenate([coarse[span], fine[span]], axis=0)
+            values = jnp.concatenate([slots_ref[r, 1], slots_ref[r + 1, 1]], axis=1)
+            sums = jnp.dot(stacked, values, preferred_element_type=f32)
+            sums = sums[:16] + sums[16:]
+            for i in range(2):
+                mine = slice(8 * (k + i), 8 * (k + i) + 8)
+                total = sums[8 * i : 8 * i + 8, i * head_dim : (i + 1) * head_dim]
+                total = total + own_weight[mine] * fresh[r + i, 1:2]
+                sums_ref[8 * (r + i) : 8 * (r + i) + 8] = total / mass[mine]
     done = jnp.concatenate([sums_ref[pl.ds(g, count, stride=8), :] for g in range(group)], axis=1).astype(bf16)
     for k in range(out_ref.shape[0]):
         out_ref[k] = done

time: 101 us -> 101 us (level)
  no operation moved by 1% of the time
where the time goes in v10:
time: 101 us
  blocking collectives  63.9 us (63%)
  starting transfers between devices  16.1 us (16%)
  Pallas kernels  11.8 us (12%)
  waiting for transfers between devices  7.42 us (7%)
    all_to_all x1, blocking collectives, shards(): lax.all_to_all(half, ('y', 'x'), split_axis=0, concat_axis=0, tiled=False)  21.4 us
    all_to_all x2, blocking collectives, spread(): return lax.all_to_all(many, axes, split_axis=0, concat_axis=0, tiled=False)  19.6 us
    all_to_all x1, blocking collectives, shards(): lax.all_to_all(partial, ('c', 'y'), split_axis=0, concat_axis=0, tiled=Fa...  12.6 us
    all_to_all x1, blocking collectives, shards(): rows = lax.all_to_all(rows, 'z', split_axis=0, concat_axis=0, tiled=False)  10.3 us
    all_to_all x1, starting transfers between devices, shards(): lax.all_to_all(many, 'z', split_axis=0, concat_axis=0, tiled=False)  8.19 us
    pallas_call x1, Pallas kernels, shards(): pl.pallas_call(functools.partial(attend_kernel, HEADS // KV_HEADS, sizes)...  5.61 us
    ppermute x3, waiting for transfers between devices, from_along_x(): return lax.ppermute(block, 'x', [(i, (i + step) % nx) for i in range(nx)])  4.61 us
    ppermute x3, starting transfers between devices, from_along_x(): return lax.ppermute(block, 'x', [(i, (i + step) % nx) for i in range(nx)])  4.51 us
  transfers between devices with their start and end apart: 5, of which 2 were waited for; matrix products, arithmetic and copies ran while one was open for 0% of the time, Pallas kernels for 3%

profile of v10, /device:TPU:1, one launch (start us, length us, event | category | flops | bytes accessed | tf_op | source)
XLA Modules:
  0.0 101.0 jit_solution(8223758960731813695)
XLA Ops:
  0.6 0.0 copy-start.2
  0.6 5.6 %attend.1 = (bf16[8,8,640]{2,1,0:T(8,128)(2,1)}, bf16[176,640]{1,0:T(8,128)(2,1)}) custom-call(s32[256]{0:T(256)} %lengths_ref.1, bf16[8,640]{1,0:T(8,128)(2,1)} %query_ref.1, bf16[8,2,128]{2,1,0:T(2,128)(2,1)} %new_ref.1, bf16[8,2,1024,128]{3,2,1,0:T(8,128)(2,1)} %cache_ref.1, bf16[160,640]{1,0:T(8,128)(2,1)} %bitcast.27, bf16[160,256]{1,0:T(8,128)(2,1)} %bitcast.29, ...), custom_call_target="tpu_custom_call" | custom-call | tf_op jit(solution)/shard_map/attend/pallas_call | solution.py:237
  6.3 3.4 %collective-permute-start.2 = (bf16[176,640]{1,0:T(8,128)(2,1)}, bf16[176,640]{1,0:T(8,128)(2,1)S(1)}, u32[]{:S(2)}, u32[]{:S(2)}) collective-permute-start(bf16[176,640]{1,0:T(8,128)(2,1)} %get-tuple-element.13.refs_0_), channel_id=1, source_target_pairs={{0,24},{8,0},{16,8},{24,16},{1,25},{9,1},{17,9},{25,17},{2,26},{10... | collective-permute-start | bytes 675848 | tf_op jit(solution)/shard_map/ppermute | solution.py:235
  9.6 0.5 collective-permute-start.1
  10.2 0.6 collective-permute-start
  10.8 8.2 %all-to-all-start = ((bf16[8,8,640]{2,1,0:T(8,128)(2,1)}), bf16[8,8,640]{2,1,0:T(8,128)(2,1)S(1)}, u32[]{:S(2)}, u32[]{:S(2)}) async-start(bf16[8,8,640]{2,1,0:T(8,128)(2,1)} %get-tuple-element.12), calls=%async_computation | async-start | bytes 163840 | tf_op jit(solution)/shard_map/all_to_all | solution.py:259
  19.0 0.0 collective-permute-done.2.refs_3_
  19.0 0.0 collective-permute-done.1.refs_2_
  19.1 4.6 %collective-permute-done.refs_1_ = bf16[176,640]{1,0:T(8,128)(2,1)S(1)} collective-permute-done((bf16[176,640]{1,0:T(8,128)(2,1)}, bf16[176,640]{1,0:T(8,128)(2,1)S(1)}, u32[]{:S(2)}, u32[]{:S(2)}) %collective-permute-start) | collective-permute-done | bytes 225312 | tf_op jit(solution)/shard_map/ppermute | solution.py:235
  23.6 0.0 copy-start
  23.7 2.8 %all-to-all-done = bf16[8,8,640]{2,1,0:T(8,128)(2,1)S(1)} async-done(((bf16[8,8,640]{2,1,0:T(8,128)(2,1)}), bf16[8,8,640]{2,1,0:T(8,128)(2,1)S(1)}, u32[]{:S(2)}, u32[]{:S(2)}) %all-to-all-start) | async-done | bytes 81952 | tf_op jit(solution)/shard_map/all_to_all | solution.py:259
  26.5 0.0 copy-done.2
  26.5 0.4 fusion
  26.8 12.6 %all_to_all.30.partial_ref = f32[8,8,640]{2,1,0:T(8,128)S(1)} all-to-all(f32[8,8,640]{2,1,0:T(8,128)S(1)} %fusion), channel_id=1, replica_groups=mesh['z'=8,'x'=4,'y'=4,'c'=2] {'c','y'}, dimensions={0} | all-to-all | bytes 327680 | tf_op jit(solution)/shard_map/all_to_all | solution.py:265
  39.5 0.0 copy-done
  39.5 0.3 resid.1
  39.8 10.3 %all_to_all.31.rows_ref = bf16[8,8,768]{2,1,0:T(8,128)(2,1)S(1)} all-to-all(bf16[8,8,768]{2,1,0:T(8,128)(2,1)S(1)} %resid.1), channel_id=1, replica_groups=mesh['z'=8,'x'=4,'y'=4,'c'=2] {'z'}, dimensions={0} | all-to-all | bytes 196608 | tf_op jit(solution)/shard_map/all_to_all | solution.py:276
  50.1 0.2 norm.1
  50.3 0.0 copy-start.3
  50.4 21.4 %all_to_all.32 = bf16[16,8,5120]{2,1,0:T(8,128)(2,1)S(1)} all-to-all(bf16[16,8,5120]{2,1,0:T(8,128)(2,1)S(1)} %norm.1), channel_id=1, replica_groups=mesh['z'=8,'x'=4,'y'=4,'c'=2] {'y','x'}, dimensions={0} | all-to-all | bytes 2621440 | tf_op jit(solution)/shard_map/all_to_all | solution.py:285
  71.7 3.4 %collective-permute-start.3 = (bf16[128,5120]{1,0:T(8,128)(2,1)S(1)}, bf16[128,5120]{1,0:T(8,128)(2,1)S(1)}, u32[]{:S(2)}, u32[]{:S(2)}) collective-permute-start(bf16[128,5120]{1,0:T(8,128)(2,1)S(1)} %bitcast.23), channel_id=1, source_target_pairs={{0,1},{1,0},{2,3},{3,2},{4,5},{5,4},{6,7},{7,6},{8,9},{9,8},{10,11... | collective-permute-start | bytes 3932168 | tf_op jit(solution)/shard_map/ppermute | solution.py:287
  75.1 0.0 copy-done.3
  75.1 2.8 %fetch.1.head_ref = bf16[594,5120]{1,0:T(8,128)(2,1)S(1)} custom-call(bf16[594,5120]{1,0:T(8,128)(2,1)} %head_hbm.1, bf16[128,5120]{1,0:T(8,128)(2,1)S(1)} %bitcast.24), custom_call_target="tpu_custom_call" | custom-call | tf_op jit(solution)/shard_map/fetch/pallas_call | solution.py:288
  77.9 0.0 collective-permute-done.3
  77.9 0.2 broadcast_select_fusion.1
  78.1 0.2 pad_maximum_fusion.rows_ref
  78.3 0.0 copy-start.1
  78.3 2.0 %logits.1 = (f32[594,256]{1,0:T(8,128)S(1)}, f32[2,256]{1,0:T(2,128)S(1)}) custom-call(bf16[594,5120]{1,0:T(8,128)(2,1)S(1)} %fetch.1.head_ref, bf16[256,5120]{1,0:T(8,128)(2,1)S(1)} %pad_maximum_fusion.rows_ref, s32[1,256]{1,0:T(1,128)S(1)} %bitcast.25), custom_call_target="tpu_custom_call" | custom-call | tf_op jit(solution)/shard_map/logits/pallas_call | solution.py:305
  80.3 10.6 %all_to_all.33 = f32[32,2,256]{2,1,0:T(2,128)S(1)} all-to-all(f32[32,2,256]{2,1,0:T(2,128)S(1)} %broadcast_in_dim.24), channel_id=1, replica_groups=mesh['z'=8,'x'=4,'y'=4,'c'=2] {'x','y','c'}, dimensions={0} | all-to-all | bytes 131072 | tf_op jit(solution)/shard_map/all_to_all | solution.py:224
  90.9 0.1 slice_reduce_fusion.1
  91.1 9.0 %all_to_all.34.stats_ref = f32[8,2,256]{2,1,0:T(2,128)S(1)} all-to-all(f32[8,2,256]{2,1,0:T(2,128)S(1)} %broadcast_in_dim.25), channel_id=1, replica_groups=mesh['z'=8,'x'=4,'y'=4,'c'=2] {'z'}, dimensions={0} | all-to-all | bytes 32768 | tf_op jit(solution)/shard_map/all_to_all | solution.py:224
  100.1 0.0 copy-done.1
  100.1 0.9 final.1
  (9 shorter events, 0.1 us)
Async XLA Ops:
  0.6 25.8 %copy-start.2 = (bf16[640,160]{0,1:T(8,128)(2,1)S(1)}, bf16[640,160]{0,1:T(8,128)(2,1)}, u32[]{:S(2)}) copy-start(bf16[640,160]{0,1:T(8,128)(2,1)} %param.15) | copy-start | bytes 614404
  6.3 12.7 %collective-permute-start.2 = (bf16[176,640]{1,0:T(8,128)(2,1)}, bf16[176,640]{1,0:T(8,128)(2,1)S(1)}, u32[]{:S(2)}, u32[]{:S(2)}) collective-permute-start(bf16[176,640]{1,0:T(8,128)(2,1)} %get-tuple-element.13.refs_0_), channel_id=1, source_target_pairs={{0,24},{8,0},{16,8},{24,16},{1,25},{9,1},{17,9},{25,17},{2,26},{10... | collective-permute-start | bytes 675848 | tf_op jit(solution)/shard_map/ppermute | solution.py:235
  9.6 9.4 %collective-permute-start.1 = (bf16[176,640]{1,0:T(8,128)(2,1)}, bf16[176,640]{1,0:T(8,128)(2,1)S(1)}, u32[]{:S(2)}, u32[]{:S(2)}) collective-permute-start(bf16[176,640]{1,0:T(8,128)(2,1)} %get-tuple-element.13.refs_0_), channel_id=1, source_target_pairs={{0,16},{8,24},{16,0},{24,8},{1,17},{9,25},{17,1},{25,9},{2,18},{10... | collective-permute-start | bytes 675848 | tf_op jit(solution)/shard_map/ppermute | solution.py:235
  10.2 13.5 %collective-permute-start = (bf16[176,640]{1,0:T(8,128)(2,1)}, bf16[176,640]{1,0:T(8,128)(2,1)S(1)}, u32[]{:S(2)}, u32[]{:S(2)}) collective-permute-start(bf16[176,640]{1,0:T(8,128)(2,1)} %get-tuple-element.13.refs_0_), channel_id=1, source_target_pairs={{0,8},{8,16},{16,24},{24,0},{1,9},{9,17},{17,25},{25,1},{2,10},{10... | collective-permute-start | bytes 675848 | tf_op jit(solution)/shard_map/ppermute | solution.py:235
  10.8 15.7 %all-to-all-start = ((bf16[8,8,640]{2,1,0:T(8,128)(2,1)}), bf16[8,8,640]{2,1,0:T(8,128)(2,1)S(1)}, u32[]{:S(2)}, u32[]{:S(2)}) async-start(bf16[8,8,640]{2,1,0:T(8,128)(2,1)} %get-tuple-element.12), calls=%async_computation | async-start | bytes 163840 | tf_op jit(solution)/shard_map/all_to_all | solution.py:259
  23.6 15.8 %copy-start = (bf16[176,640]{1,0:T(8,128)(2,1)S(1)}, bf16[176,640]{1,0:T(8,128)(2,1)}, u32[]{:S(2)}) copy-start(bf16[176,640]{1,0:T(8,128)(2,1)} %get-tuple-element.13.refs_0_) | copy-start | bytes 675844
  50.3 24.8 %copy-start.3 = (s32[256]{0:T(256)S(1)}, s32[256]{0:T(256)}, u32[]{:S(2)}) copy-start(s32[256]{0:T(256)} %param.18) | copy-start | bytes 3076
  71.7 6.2 %collective-permute-start.3 = (bf16[128,5120]{1,0:T(8,128)(2,1)S(1)}, bf16[128,5120]{1,0:T(8,128)(2,1)S(1)}, u32[]{:S(2)}, u32[]{:S(2)}) collective-permute-start(bf16[128,5120]{1,0:T(8,128)(2,1)S(1)} %bitcast.23), channel_id=1, source_target_pairs={{0,1},{1,0},{2,3},{3,2},{4,5},{5,4},{6,7},{7,6},{8,9},{9,8},{10,11... | collective-permute-start | bytes 3932168 | tf_op jit(solution)/shard_map/ppermute | solution.py:287
  78.3 21.8 %copy-start.1 = (f32[256]{0:T(256)S(1)}, f32[256]{0:T(256)}, u32[]{:S(2)}) copy-start(f32[256]{0:T(256)} %param.19) | copy-start | bytes 3076

commit v11 on v9

--- a/solution.py
+++ b/solution.py
@@ -62,15 +62,26 @@
     pack_ref[columns:] = jnp.concatenate([side_by_side(picked), below], axis=0).astype(bf16)
 
 
-def attend_kernel(group, sizes, lengths_ref, query_ref, new_ref, cache_ref, table_hbm, hidden_hbm, gain_hbm, *refs):
-    out_ref, pack_ref, slots_ref, rows_ref, sums_ref, hidden_ref, gain_ref, sems, pack_sems = refs
+def attend_kernel(group, sizes, lengths_ref, query_hbm, new_hbm, cache_ref, table_hbm, hidden_hbm, gain_hbm, *refs):
+    out_ref, pack_hbm, slots_ref, rows_ref, sums_ref, query_ref, new_ref, hidden_ref, gain_ref, pack_ref = refs[:-2]
+    sems, small_sems = refs[-2:]
     count, _, slots, head_dim = cache_ref.shape
     columns = table_hbm.shape[0]
     z, x = lax.axis_index("z"), lax.axis_index("x")
     scale = head_dim ** (-0.5)
-    hidden = pltpu.make_async_copy(hidden_hbm, hidden_ref, pack_sems.at[0])
-    gain = pltpu.make_async_copy(gain_hbm, gain_ref, pack_sems.at[1])
-    table = pltpu.make_async_copy(table_hbm, pack_ref.at[pl.ds(0, columns)], pack_sems.at[2])
+    small = [
+        pltpu.make_async_copy(source, target, small_sems.at[k])
+        for k, (source, target) in enumerate(
+            (
+                (query_hbm, query_ref),
+                (new_hbm, new_ref),
+                (hidden_hbm, hidden_ref),
+                (gain_hbm, gain_ref),
+                (table_hbm, pack_ref.at[pl.ds(0, columns)]),
+            )
+        )
+    ]
+    leave = pltpu.make_async_copy(pack_ref, pack_hbm, small_sems.at[len(small)])
     portions = [range(k, k + count // 2) for k in (0, count // 2)]
     loads = [
         [
@@ -80,14 +91,12 @@
         for portion in portions
         for kind in range(2)
     ]
-    hidden.start()
-    gain.start()
-    for load in sum(loads, []):
+    for load in small + sum(loads, []):
         load.start()
-    table.start()
-    hidden.wait()
-    gain.wait()
+    for load in small:
+        load.wait()
     pack_tail(sizes, hidden_ref, gain_ref, pack_ref)
+    leave.start()
 
     query = query_ref[...].astype(f32)
     fresh = new_ref[...].astype(f32)
@@ -131,7 +140,7 @@
     done = jnp.concatenate([sums_ref[pl.ds(g, count, stride=8), :] for g in range(group)], axis=1).astype(bf16)
     for k in range(out_ref.shape[0]):
         out_ref[k] = done
-    table.wait()
+    leave.wait()
 
 
 def resid_kernel(partial_ref, *refs):
@@ -233,16 +242,19 @@
             jax.ShapeDtypeStruct((nz,) + query.shape, bf16),
             jax.ShapeDtypeStruct((columns + TAIL, heads), bf16),
         ],
-        in_specs=[IN_SMEM] + [IN_VMEM] * 2 + [IN_PLACE] * 4,
-        out_specs=[IN_VMEM] * 2,
+        in_specs=[IN_SMEM] + [IN_PLACE] * 6,
+        out_specs=[IN_VMEM, IN_PLACE],
         scratch_shapes=[
             pltpu.VMEM(cache.shape, bf16),
             pltpu.VMEM((count * 8, HEAD_DIM), f32),
             pltpu.VMEM((count * 8, HEAD_DIM), f32),
+            pltpu.VMEM(query.shape, bf16),
+            pltpu.VMEM(new_kv.shape, bf16),
             pltpu.VMEM((columns, hidden_in.shape[0]), bf16),
             pltpu.VMEM((1, columns), f32),
+            pltpu.VMEM((columns + TAIL, heads), bf16),
             pltpu.SemaphoreType.DMA((2, count)),
-            pltpu.SemaphoreType.DMA((3,)),
+            pltpu.SemaphoreType.DMA((6,)),
         ],
         compiler_params=WHOLE,
         name="attend",

time: 101 us -> 102 us (level)
  no operation moved by 1% of the time
where the time goes in v11:
time: 102 us; the launch traced here: 101 us
  blocking collectives  63.9 us (63%)
  starting transfers between devices  16.1 us (16%)
  Pallas kernels  12 us (12%)
  waiting for transfers between devices  7.42 us (7%)
    all_to_all x1, blocking collectives, shards(): lax.all_to_all(half, ('y', 'x'), split_axis=0, concat_axis=0, tiled=False)  21.4 us
    all_to_all x2, blocking collectives, spread(): return lax.all_to_all(many, axes, split_axis=0, concat_axis=0, tiled=False)  19.6 us
    all_to_all x1, blocking collectives, shards(): lax.all_to_all(partial, ('c', 'y'), split_axis=0, concat_axis=0, tiled=Fa...  12.6 us
    all_to_all x1, blocking collectives, shards(): rows = lax.all_to_all(rows, 'z', split_axis=0, concat_axis=0, tiled=False)  10.3 us
    all_to_all x1, starting transfers between devices, shards(): lax.all_to_all(many, 'z', split_axis=0, concat_axis=0, tiled=False)  8.19 us
    pallas_call x1, Pallas kernels, shards(): pl.pallas_call(functools.partial(attend_kernel, HEADS // KV_HEADS, sizes)...  5.75 us
    ppermute x3, waiting for transfers between devices, from_along_x(): return lax.ppermute(block, 'x', [(i, (i + step) % nx) for i in range(nx)])  4.61 us
    ppermute x3, starting transfers between devices, from_along_x(): return lax.ppermute(block, 'x', [(i, (i + step) % nx) for i in range(nx)])  4.51 us
  transfers between devices with their start and end apart: 5, of which 2 were waited for; matrix products, arithmetic and copies ran while one was open for 0% of the time, Pallas kernels for 3%

profile of v11, /device:TPU:1, one launch (start us, length us, event | category | flops | bytes accessed | tf_op | source)
XLA Modules:
  0.0 101.1 jit_solution(13334947404587743155)
XLA Ops:
  0.6 0.0 copy-start.2
  0.6 5.8 %attend.1 = (bf16[8,8,640]{2,1,0:T(8,128)(2,1)}, bf16[176,640]{1,0:T(8,128)(2,1)}) custom-call(s32[256]{0:T(256)} %lengths_ref.1, bf16[8,640]{1,0:T(8,128)(2,1)} %query_hbm.1, bf16[8,2,128]{2,1,0:T(2,128)(2,1)} %new_hbm.1, bf16[8,2,1024,128]{3,2,1,0:T(8,128)(2,1)} %cache_ref.1, bf16[160,640]{1,0:T(8,128)(2,1)} %bitcast.27, bf16[160,256]{1,0:T(8,128)(2,1)} %bitcast.29, ...), custom_call_target="tpu_custom_call" | custom-call | tf_op jit(solution)/shard_map/attend/pallas_call | solution.py:239
  6.4 3.4 %collective-permute-start.2 = (bf16[176,640]{1,0:T(8,128)(2,1)}, bf16[176,640]{1,0:T(8,128)(2,1)S(1)}, u32[]{:S(2)}, u32[]{:S(2)}) collective-permute-start(bf16[176,640]{1,0:T(8,128)(2,1)} %get-tuple-element.13.refs_0_), channel_id=1, source_target_pairs={{0,24},{8,0},{16,8},{24,16},{1,25},{9,1},{17,9},{25,17},{2,26},{10... | collective-permute-start | bytes 675848 | tf_op jit(solution)/shard_map/ppermute | solution.py:237
  9.8 0.5 collective-permute-start.1
  10.3 0.6 collective-permute-start
  10.9 8.2 %all-to-all-start = ((bf16[8,8,640]{2,1,0:T(8,128)(2,1)}), bf16[8,8,640]{2,1,0:T(8,128)(2,1)S(1)}, u32[]{:S(2)}, u32[]{:S(2)}) async-start(bf16[8,8,640]{2,1,0:T(8,128)(2,1)} %get-tuple-element.12), calls=%async_computation | async-start | bytes 163840 | tf_op jit(solution)/shard_map/all_to_all | solution.py:264
  19.1 0.0 collective-permute-done.2.refs_3_
  19.2 0.0 collective-permute-done.1.refs_2_
  19.2 4.6 %collective-permute-done.refs_1_ = bf16[176,640]{1,0:T(8,128)(2,1)S(1)} collective-permute-done((bf16[176,640]{1,0:T(8,128)(2,1)}, bf16[176,640]{1,0:T(8,128)(2,1)S(1)}, u32[]{:S(2)}, u32[]{:S(2)}) %collective-permute-start) | collective-permute-done | bytes 225312 | tf_op jit(solution)/shard_map/ppermute | solution.py:237
  23.8 0.0 copy-start
  23.8 2.8 %all-to-all-done = bf16[8,8,640]{2,1,0:T(8,128)(2,1)S(1)} async-done(((bf16[8,8,640]{2,1,0:T(8,128)(2,1)}), bf16[8,8,640]{2,1,0:T(8,128)(2,1)S(1)}, u32[]{:S(2)}, u32[]{:S(2)}) %all-to-all-start) | async-done | bytes 81952 | tf_op jit(solution)/shard_map/all_to_all | solution.py:264
  26.6 0.0 copy-done.2
  26.6 0.4 fusion
  27.0 12.6 %all_to_all.30.partial_ref = f32[8,8,640]{2,1,0:T(8,128)S(1)} all-to-all(f32[8,8,640]{2,1,0:T(8,128)S(1)} %fusion), channel_id=1, replica_groups=mesh['z'=8,'x'=4,'y'=4,'c'=2] {'c','y'}, dimensions={0} | all-to-all | bytes 327680 | tf_op jit(solution)/shard_map/all_to_all | solution.py:270
  39.6 0.0 copy-done
  39.6 0.3 resid.1
  40.0 10.3 %all_to_all.31.rows_ref = bf16[8,8,768]{2,1,0:T(8,128)(2,1)S(1)} all-to-all(bf16[8,8,768]{2,1,0:T(8,128)(2,1)S(1)} %resid.1), channel_id=1, replica_groups=mesh['z'=8,'x'=4,'y'=4,'c'=2] {'z'}, dimensions={0} | all-to-all | bytes 196608 | tf_op jit(solution)/shard_map/all_to_all | solution.py:281
  50.3 0.2 norm.1
  50.5 0.0 copy-start.3
  50.5 21.4 %all_to_all.32 = bf16[16,8,5120]{2,1,0:T(8,128)(2,1)S(1)} all-to-all(bf16[16,8,5120]{2,1,0:T(8,128)(2,1)S(1)} %norm.1), channel_id=1, replica_groups=mesh['z'=8,'x'=4,'y'=4,'c'=2] {'y','x'}, dimensions={0} | all-to-all | bytes 2621440 | tf_op jit(solution)/shard_map/all_to_all | solution.py:290
  71.9 3.4 %collective-permute-start.3 = (bf16[128,5120]{1,0:T(8,128)(2,1)S(1)}, bf16[128,5120]{1,0:T(8,128)(2,1)S(1)}, u32[]{:S(2)}, u32[]{:S(2)}) collective-permute-start(bf16[128,5120]{1,0:T(8,128)(2,1)S(1)} %bitcast.23), channel_id=1, source_target_pairs={{0,1},{1,0},{2,3},{3,2},{4,5},{5,4},{6,7},{7,6},{8,9},{9,8},{10,11... | collective-permute-start | bytes 3932168 | tf_op jit(solution)/shard_map/ppermute | solution.py:292
  75.3 0.0 copy-done.3
  75.3 2.8 %fetch.1.head_ref = bf16[594,5120]{1,0:T(8,128)(2,1)S(1)} custom-call(bf16[594,5120]{1,0:T(8,128)(2,1)} %head_hbm.1, bf16[128,5120]{1,0:T(8,128)(2,1)S(1)} %bitcast.24), custom_call_target="tpu_custom_call" | custom-call | tf_op jit(solution)/shard_map/fetch/pallas_call | solution.py:293
  78.0 0.0 collective-permute-done.3
  78.0 0.2 broadcast_select_fusion.1
  78.2 0.2 pad_maximum_fusion.rows_ref
  78.4 0.0 copy-start.1
  78.4 2.0 %logits.1 = (f32[594,256]{1,0:T(8,128)S(1)}, f32[2,256]{1,0:T(2,128)S(1)}) custom-call(bf16[594,5120]{1,0:T(8,128)(2,1)S(1)} %fetch.1.head_ref, bf16[256,5120]{1,0:T(8,128)(2,1)S(1)} %pad_maximum_fusion.rows_ref, s32[1,256]{1,0:T(1,128)S(1)} %bitcast.25), custom_call_target="tpu_custom_call" | custom-call | tf_op jit(solution)/shard_map/logits/pallas_call | solution.py:310
  80.5 10.6 %all_to_all.33 = f32[32,2,256]{2,1,0:T(2,128)S(1)} all-to-all(f32[32,2,256]{2,1,0:T(2,128)S(1)} %broadcast_in_dim.24), channel_id=1, replica_groups=mesh['z'=8,'x'=4,'y'=4,'c'=2] {'x','y','c'}, dimensions={0} | all-to-all | bytes 131072 | tf_op jit(solution)/shard_map/all_to_all | solution.py:226
  91.1 0.1 slice_reduce_fusion.1
  91.2 9.0 %all_to_all.34.stats_ref = f32[8,2,256]{2,1,0:T(2,128)S(1)} all-to-all(f32[8,2,256]{2,1,0:T(2,128)S(1)} %broadcast_in_dim.25), channel_id=1, replica_groups=mesh['z'=8,'x'=4,'y'=4,'c'=2] {'z'}, dimensions={0} | all-to-all | bytes 32768 | tf_op jit(solution)/shard_map/all_to_all | solution.py:226
  100.2 0.0 copy-done.1
  100.2 0.9 final.1
  (9 shorter events, 0.1 us)
Async XLA Ops:
  0.6 26.0 %copy-start.2 = (bf16[640,160]{0,1:T(8,128)(2,1)S(1)}, bf16[640,160]{0,1:T(8,128)(2,1)}, u32[]{:S(2)}) copy-start(bf16[640,160]{0,1:T(8,128)(2,1)} %param.15) | copy-start | bytes 614404
  6.4 12.7 %collective-permute-start.2 = (bf16[176,640]{1,0:T(8,128)(2,1)}, bf16[176,640]{1,0:T(8,128)(2,1)S(1)}, u32[]{:S(2)}, u32[]{:S(2)}) collective-permute-start(bf16[176,640]{1,0:T(8,128)(2,1)} %get-tuple-element.13.refs_0_), channel_id=1, source_target_pairs={{0,24},{8,0},{16,8},{24,16},{1,25},{9,1},{17,9},{25,17},{2,26},{10... | collective-permute-start | bytes 675848 | tf_op jit(solution)/shard_map/ppermute | solution.py:237
  9.8 9.4 %collective-permute-start.1 = (bf16[176,640]{1,0:T(8,128)(2,1)}, bf16[176,640]{1,0:T(8,128)(2,1)S(1)}, u32[]{:S(2)}, u32[]{:S(2)}) collective-permute-start(bf16[176,640]{1,0:T(8,128)(2,1)} %get-tuple-element.13.refs_0_), channel_id=1, source_target_pairs={{0,16},{8,24},{16,0},{24,8},{1,17},{9,25},{17,1},{25,9},{2,18},{10... | collective-permute-start | bytes 675848 | tf_op jit(solution)/shard_map/ppermute | solution.py:237
  10.3 13.5 %collective-permute-start = (bf16[176,640]{1,0:T(8,128)(2,1)}, bf16[176,640]{1,0:T(8,128)(2,1)S(1)}, u32[]{:S(2)}, u32[]{:S(2)}) collective-permute-start(bf16[176,640]{1,0:T(8,128)(2,1)} %get-tuple-element.13.refs_0_), channel_id=1, source_target_pairs={{0,8},{8,16},{16,24},{24,0},{1,9},{9,17},{17,25},{25,1},{2,10},{10... | collective-permute-start | bytes 675848 | tf_op jit(solution)/shard_map/ppermute | solution.py:237
  10.9 15.7 %all-to-all-start = ((bf16[8,8,640]{2,1,0:T(8,128)(2,1)}), bf16[8,8,640]{2,1,0:T(8,128)(2,1)S(1)}, u32[]{:S(2)}, u32[]{:S(2)}) async-start(bf16[8,8,640]{2,1,0:T(8,128)(2,1)} %get-tuple-element.12), calls=%async_computation | async-start | bytes 163840 | tf_op jit(solution)/shard_map/all_to_all | solution.py:264
  23.8 15.8 %copy-start = (bf16[176,640]{1,0:T(8,128)(2,1)S(1)}, bf16[176,640]{1,0:T(8,128)(2,1)}, u32[]{:S(2)}) copy-start(bf16[176,640]{1,0:T(8,128)(2,1)} %get-tuple-element.13.refs_0_) | copy-start | bytes 675844
  50.5 24.8 %copy-start.3 = (s32[256]{0:T(256)S(1)}, s32[256]{0:T(256)}, u32[]{:S(2)}) copy-start(s32[256]{0:T(256)} %param.18) | copy-start | bytes 3076
  71.9 6.2 %collective-permute-start.3 = (bf16[128,5120]{1,0:T(8,128)(2,1)S(1)}, bf16[128,5120]{1,0:T(8,128)(2,1)S(1)}, u32[]{:S(2)}, u32[]{:S(2)}) collective-permute-start(bf16[128,5120]{1,0:T(8,128)(2,1)S(1)} %bitcast.23), channel_id=1, source_target_pairs={{0,1},{1,0},{2,3},{3,2},{4,5},{5,4},{6,7},{7,6},{8,9},{9,8},{10,11... | collective-permute-start | bytes 3932168 | tf_op jit(solution)/shard_map/ppermute | solution.py:292
  78.4 21.8 %copy-start.1 = (f32[256]{0:T(256)S(1)}, f32[256]{0:T(256)}, u32[]{:S(2)}) copy-start(f32[256]{0:T(256)} %param.19) | copy-start | bytes 3076

commit v12 on v11

--- a/solution.py
+++ b/solution.py
@@ -93,10 +93,8 @@
     ]
     for load in small + sum(loads, []):
         load.start()
-    for load in small:
+    for load in small[:2]:
         load.wait()
-    pack_tail(sizes, hidden_ref, gain_ref, pack_ref)
-    leave.start()
 
     query = query_ref[...].astype(f32)
     fresh = new_ref[...].astype(f32)
@@ -129,6 +127,11 @@
         mass = jnp.sum(weights, axis=1, keepdims=True) + own_weight
         coarse = weights.astype(bf16)
         fine = (weights - coarse.astype(f32)).astype(bf16)
+        if portion is portions[0]:
+            for load in small[2:]:
+                load.wait()
+            pack_tail(sizes, hidden_ref, gain_ref, pack_ref)
+            leave.start()
         for load in value_loads:
             load.wait()
         for k, r in enumerate(portion):

time: 102 us -> 101 us (level)
  no operation moved by 1% of the time
where the time goes in v12:
time: 101 us
  blocking collectives  63.9 us (63%)
  starting transfers between devices  16.1 us (16%)
  Pallas kernels  11.5 us (11%)
  waiting for transfers between devices  7.42 us (7%)
    all_to_all x1, blocking collectives, shards(): lax.all_to_all(half, ('y', 'x'), split_axis=0, concat_axis=0, tiled=False)  21.4 us
    all_to_all x2, blocking collectives, spread(): return lax.all_to_all(many, axes, split_axis=0, concat_axis=0, tiled=False)  19.6 us
    all_to_all x1, blocking collectives, shards(): lax.all_to_all(partial, ('c', 'y'), split_axis=0, concat_axis=0, tiled=Fa...  12.6 us
    all_to_all x1, blocking collectives, shards(): rows = lax.all_to_all(rows, 'z', split_axis=0, concat_axis=0, tiled=False)  10.3 us
    all_to_all x1, starting transfers between devices, shards(): lax.all_to_all(many, 'z', split_axis=0, concat_axis=0, tiled=False)  8.19 us
    pallas_call x1, Pallas kernels, shards(): pl.pallas_call(functools.partial(attend_kernel, HEADS // KV_HEADS, sizes)...  5.31 us
    ppermute x3, waiting for transfers between devices, from_along_x(): return lax.ppermute(block, 'x', [(i, (i + step) % nx) for i in range(nx)])  4.61 us
    ppermute x3, starting transfers between devices, from_along_x(): return lax.ppermute(block, 'x', [(i, (i + step) % nx) for i in range(nx)])  4.51 us
  transfers between devices with their start and end apart: 5, of which 2 were waited for; matrix products, arithmetic and copies ran while one was open for 0% of the time, Pallas kernels for 3%

profile of v12, /device:TPU:1, one launch (start us, length us, event | category | flops | bytes accessed | tf_op | source)
XLA Modules:
  0.0 100.7 jit_solution(10817030122257876862)
XLA Ops:
  0.6 0.0 copy-start.2
  0.6 5.3 %attend.1 = (bf16[8,8,640]{2,1,0:T(8,128)(2,1)}, bf16[176,640]{1,0:T(8,128)(2,1)}) custom-call(s32[256]{0:T(256)} %lengths_ref.1, bf16[8,640]{1,0:T(8,128)(2,1)} %query_hbm.1, bf16[8,2,128]{2,1,0:T(2,128)(2,1)} %new_hbm.1, bf16[8,2,1024,128]{3,2,1,0:T(8,128)(2,1)} %cache_ref.1, bf16[160,640]{1,0:T(8,128)(2,1)} %bitcast.27, bf16[160,256]{1,0:T(8,128)(2,1)} %bitcast.29, ...), custom_call_target="tpu_custom_call" | custom-call | tf_op jit(solution)/shard_map/attend/pallas_call | solution.py:242
  6.0 3.4 %collective-permute-start.2 = (bf16[176,640]{1,0:T(8,128)(2,1)}, bf16[176,640]{1,0:T(8,128)(2,1)S(1)}, u32[]{:S(2)}, u32[]{:S(2)}) collective-permute-start(bf16[176,640]{1,0:T(8,128)(2,1)} %get-tuple-element.13.refs_0_), channel_id=1, source_target_pairs={{0,24},{8,0},{16,8},{24,16},{1,25},{9,1},{17,9},{25,17},{2,26},{10... | collective-permute-start | bytes 675848 | tf_op jit(solution)/shard_map/ppermute | solution.py:240
  9.3 0.5 collective-permute-start.1
  9.9 0.6 collective-permute-start
  10.5 8.2 %all-to-all-start = ((bf16[8,8,640]{2,1,0:T(8,128)(2,1)}), bf16[8,8,640]{2,1,0:T(8,128)(2,1)S(1)}, u32[]{:S(2)}, u32[]{:S(2)}) async-start(bf16[8,8,640]{2,1,0:T(8,128)(2,1)} %get-tuple-element.12), calls=%async_computation | async-start | bytes 163840 | tf_op jit(solution)/shard_map/all_to_all | solution.py:267
  18.7 0.0 collective-permute-done.2.refs_3_
  18.7 0.0 collective-permute-done.1.refs_2_
  18.8 4.6 %collective-permute-done.refs_1_ = bf16[176,640]{1,0:T(8,128)(2,1)S(1)} collective-permute-done((bf16[176,640]{1,0:T(8,128)(2,1)}, bf16[176,640]{1,0:T(8,128)(2,1)S(1)}, u32[]{:S(2)}, u32[]{:S(2)}) %collective-permute-start) | collective-permute-done | bytes 225312 | tf_op jit(solution)/shard_map/ppermute | solution.py:240
  23.3 0.0 copy-start
  23.4 2.8 %all-to-all-done = bf16[8,8,640]{2,1,0:T(8,128)(2,1)S(1)} async-done(((bf16[8,8,640]{2,1,0:T(8,128)(2,1)}), bf16[8,8,640]{2,1,0:T(8,128)(2,1)S(1)}, u32[]{:S(2)}, u32[]{:S(2)}) %all-to-all-start) | async-done | bytes 81952 | tf_op jit(solution)/shard_map/all_to_all | solution.py:267
  26.2 0.0 copy-done.2
  26.2 0.4 fusion
  26.5 12.6 %all_to_all.30.partial_ref = f32[8,8,640]{2,1,0:T(8,128)S(1)} all-to-all(f32[8,8,640]{2,1,0:T(8,128)S(1)} %fusion), channel_id=1, replica_groups=mesh['z'=8,'x'=4,'y'=4,'c'=2] {'c','y'}, dimensions={0} | all-to-all | bytes 327680 | tf_op jit(solution)/shard_map/all_to_all | solution.py:273
  39.2 0.0 copy-done
  39.2 0.3 resid.1
  39.5 10.3 %all_to_all.31.rows_ref = bf16[8,8,768]{2,1,0:T(8,128)(2,1)S(1)} all-to-all(bf16[8,8,768]{2,1,0:T(8,128)(2,1)S(1)} %resid.1), channel_id=1, replica_groups=mesh['z'=8,'x'=4,'y'=4,'c'=2] {'z'}, dimensions={0} | all-to-all | bytes 196608 | tf_op jit(solution)/shard_map/all_to_all | solution.py:284
  49.8 0.2 norm.1
  50.1 0.0 copy-start.3
  50.1 21.4 %all_to_all.32 = bf16[16,8,5120]{2,1,0:T(8,128)(2,1)S(1)} all-to-all(bf16[16,8,5120]{2,1,0:T(8,128)(2,1)S(1)} %norm.1), channel_id=1, replica_groups=mesh['z'=8,'x'=4,'y'=4,'c'=2] {'y','x'}, dimensions={0} | all-to-all | bytes 2621440 | tf_op jit(solution)/shard_map/all_to_all | solution.py:293
  71.4 3.4 %collective-permute-start.3 = (bf16[128,5120]{1,0:T(8,128)(2,1)S(1)}, bf16[128,5120]{1,0:T(8,128)(2,1)S(1)}, u32[]{:S(2)}, u32[]{:S(2)}) collective-permute-start(bf16[128,5120]{1,0:T(8,128)(2,1)S(1)} %bitcast.23), channel_id=1, source_target_pairs={{0,1},{1,0},{2,3},{3,2},{4,5},{5,4},{6,7},{7,6},{8,9},{9,8},{10,11... | collective-permute-start | bytes 3932168 | tf_op jit(solution)/shard_map/ppermute | solution.py:295
  74.8 0.0 copy-done.3
  74.8 2.8 %fetch.1.head_ref = bf16[594,5120]{1,0:T(8,128)(2,1)S(1)} custom-call(bf16[594,5120]{1,0:T(8,128)(2,1)} %head_hbm.1, bf16[128,5120]{1,0:T(8,128)(2,1)S(1)} %bitcast.24), custom_call_target="tpu_custom_call" | custom-call | tf_op jit(solution)/shard_map/fetch/pallas_call | solution.py:296
  77.6 0.0 collective-permute-done.3
  77.6 0.2 broadcast_select_fusion.1
  77.8 0.2 pad_maximum_fusion.rows_ref
  78.0 0.0 copy-start.1
  78.0 2.0 %logits.1 = (f32[594,256]{1,0:T(8,128)S(1)}, f32[2,256]{1,0:T(2,128)S(1)}) custom-call(bf16[594,5120]{1,0:T(8,128)(2,1)S(1)} %fetch.1.head_ref, bf16[256,5120]{1,0:T(8,128)(2,1)S(1)} %pad_maximum_fusion.rows_ref, s32[1,256]{1,0:T(1,128)S(1)} %bitcast.25), custom_call_target="tpu_custom_call" | custom-call | tf_op jit(solution)/shard_map/logits/pallas_call | solution.py:313
  80.0 10.6 %all_to_all.33 = f32[32,2,256]{2,1,0:T(2,128)S(1)} all-to-all(f32[32,2,256]{2,1,0:T(2,128)S(1)} %broadcast_in_dim.24), channel_id=1, replica_groups=mesh['z'=8,'x'=4,'y'=4,'c'=2] {'x','y','c'}, dimensions={0} | all-to-all | bytes 131072 | tf_op jit(solution)/shard_map/all_to_all | solution.py:229
  90.6 0.1 slice_reduce_fusion.1
  90.8 9.0 %all_to_all.34.stats_ref = f32[8,2,256]{2,1,0:T(2,128)S(1)} all-to-all(f32[8,2,256]{2,1,0:T(2,128)S(1)} %broadcast_in_dim.25), channel_id=1, replica_groups=mesh['z'=8,'x'=4,'y'=4,'c'=2] {'z'}, dimensions={0} | all-to-all | bytes 32768 | tf_op jit(solution)/shard_map/all_to_all | solution.py:229
  99.8 0.0 copy-done.1
  99.8 0.9 final.1
  (9 shorter events, 0.1 us)
Async XLA Ops:
  0.6 25.5 %copy-start.2 = (bf16[640,160]{0,1:T(8,128)(2,1)S(1)}, bf16[640,160]{0,1:T(8,128)(2,1)}, u32[]{:S(2)}) copy-start(bf16[640,160]{0,1:T(8,128)(2,1)} %param.15) | copy-start | bytes 614404
  6.0 12.7 %collective-permute-start.2 = (bf16[176,640]{1,0:T(8,128)(2,1)}, bf16[176,640]{1,0:T(8,128)(2,1)S(1)}, u32[]{:S(2)}, u32[]{:S(2)}) collective-permute-start(bf16[176,640]{1,0:T(8,128)(2,1)} %get-tuple-element.13.refs_0_), channel_id=1, source_target_pairs={{0,24},{8,0},{16,8},{24,16},{1,25},{9,1},{17,9},{25,17},{2,26},{10... | collective-permute-start | bytes 675848 | tf_op jit(solution)/shard_map/ppermute | solution.py:240
  9.3 9.4 %collective-permute-start.1 = (bf16[176,640]{1,0:T(8,128)(2,1)}, bf16[176,640]{1,0:T(8,128)(2,1)S(1)}, u32[]{:S(2)}, u32[]{:S(2)}) collective-permute-start(bf16[176,640]{1,0:T(8,128)(2,1)} %get-tuple-element.13.refs_0_), channel_id=1, source_target_pairs={{0,16},{8,24},{16,0},{24,8},{1,17},{9,25},{17,1},{25,9},{2,18},{10... | collective-permute-start | bytes 675848 | tf_op jit(solution)/shard_map/ppermute | solution.py:240
  9.9 13.5 %collective-permute-start = (bf16[176,640]{1,0:T(8,128)(2,1)}, bf16[176,640]{1,0:T(8,128)(2,1)S(1)}, u32[]{:S(2)}, u32[]{:S(2)}) collective-permute-start(bf16[176,640]{1,0:T(8,128)(2,1)} %get-tuple-element.13.refs_0_), channel_id=1, source_target_pairs={{0,8},{8,16},{16,24},{24,0},{1,9},{9,17},{17,25},{25,1},{2,10},{10... | collective-permute-start | bytes 675848 | tf_op jit(solution)/shard_map/ppermute | solution.py:240
  10.5 15.7 %all-to-all-start = ((bf16[8,8,640]{2,1,0:T(8,128)(2,1)}), bf16[8,8,640]{2,1,0:T(8,128)(2,1)S(1)}, u32[]{:S(2)}, u32[]{:S(2)}) async-start(bf16[8,8,640]{2,1,0:T(8,128)(2,1)} %get-tuple-element.12), calls=%async_computation | async-start | bytes 163840 | tf_op jit(solution)/shard_map/all_to_all | solution.py:267
  23.3 15.8 %copy-start = (bf16[176,640]{1,0:T(8,128)(2,1)S(1)}, bf16[176,640]{1,0:T(8,128)(2,1)}, u32[]{:S(2)}) copy-start(bf16[176,640]{1,0:T(8,128)(2,1)} %get-tuple-element.13.refs_0_) | copy-start | bytes 675844
  50.1 24.8 %copy-start.3 = (s32[256]{0:T(256)S(1)}, s32[256]{0:T(256)}, u32[]{:S(2)}) copy-start(s32[256]{0:T(256)} %param.18) | copy-start | bytes 3076
  71.4 6.2 %collective-permute-start.3 = (bf16[128,5120]{1,0:T(8,128)(2,1)S(1)}, bf16[128,5120]{1,0:T(8,128)(2,1)S(1)}, u32[]{:S(2)}, u32[]{:S(2)}) collective-permute-start(bf16[128,5120]{1,0:T(8,128)(2,1)S(1)} %bitcast.23), channel_id=1, source_target_pairs={{0,1},{1,0},{2,3},{3,2},{4,5},{5,4},{6,7},{7,6},{8,9},{9,8},{10,11... | collective-permute-start | bytes 3932168 | tf_op jit(solution)/shard_map/ppermute | solution.py:295
  78.0 21.8 %copy-start.1 = (f32[256]{0:T(256)S(1)}, f32[256]{0:T(256)}, u32[]{:S(2)}) copy-start(f32[256]{0:T(256)} %param.19) | copy-start | bytes 3076
